TPU v7x, 256 devices: a whole 4x4x8 slice. The times are simulated.
256 devices in a mesh: dp: 16 (over z_hi, x), fsdp: 16 (over y, z_lo, core).
Axes of the slice: x: 4, y: 4, z: 8 (z_hi: 4, z_lo: 2; z = z_hi * 2 + z_lo), core: 2. Of those that a mesh axis runs over, the one named last changes fastest.
Arguments:
- hidden: bfloat16 [12288, 14336], P('fsdp', 'dp'), may hold values from -6 to 6
- cotangent: bfloat16 [12288, 4096], P('fsdp'), may hold values from -6 to 6
- weight: bfloat16 [14336, 4096], P('dp', 'fsdp'), may hold values from -0.0625 to 0.0625
- basis: bfloat16 [14336, 512], P('dp'), may hold values from -0.0625 to 0.0625
- first_moment: float32 [512, 4096], P('dp', 'fsdp'), may hold values from -665.1075 to 665.1075
- second_moment: float32 [512, 4096], P('dp', 'fsdp'), may hold values from 13 to 3076
Outputs:
- output: bfloat16 [12288, 4096], P('fsdp', 'dp')
- act_grad: bfloat16 [12288, 14336], P('fsdp', 'dp')
- new_first: float32 [512, 4096], P('dp', 'fsdp')
- new_second: float32 [512, 4096], P('dp', 'fsdp')
- update: bfloat16 [14336, 4096], P('dp', 'fsdp')
All inputs are finite; a program needn't handle non-finite values.
Results may differ from a plain program's by a relative error of at most 0.0051.
Values may be sent and summed in bfloat16 or wider, within the bound.
No kernel may reach another device: no remote copies, remote signals or barrier semaphores. Data moves between devices by JAX's collectives and lax.ppermute only.
A program may use at most 128 MiB of HBM per device.

v0:
```python
import functools

import jax
import jax.numpy as jnp
from jax import lax
from jax.experimental import pallas as pl
from jax.experimental.pallas import tpu as pltpu
from jax.sharding import Mesh
from jax.sharding import PartitionSpec as P

STEP = 20
BF = jnp.bfloat16
F32 = jnp.float32
AXES = ("zh", "x", "y", "zl", "c")
SIZE = dict(zh=4, x=4, y=4, zl=2, c=2)
FSDP = ("y", "zl", "c")
DP = ("zh", "x")
W = 256
MIB = 1024 * 1024
LIGHT = pl.CostEstimate(flops=1 << 20, bytes_accessed=1 << 16, transcendentals=0)
COST = pl.CostEstimate(flops=1 << 33, bytes_accessed=1 << 25, transcendentals=0)


def shift(array, axis, by):
    n = SIZE[axis]
    return lax.ppermute(array, axis, [(i, (i + by) % n) for i in range(n)])


def swap(array, axes):
    return lax.all_to_all(array, axes, 0, 0, tiled=True)


def after(value, *others):
    return lax.optimization_barrier((value, *others))[0]


def in_hbm(value):
    return pltpu.with_memory_space_constraint(value, pltpu.HBM)


def params(limit):
    return pltpu.CompilerParams(vmem_limit_bytes=limit * MIB)


def partial_kernel(m, start, slot_of, h_ref, *refs):
    w_refs, outs = refs[: 4 * m], refs[4 * m : 4 * m + 4]
    mine, wide, held, h_sem, w_sems, out_sems = refs[4 * m + 4 :]

    def load(k, block, slot):
        return pltpu.make_async_copy(
            w_refs[4 * block + slot], wide.at[k, :, pl.ds(block * W, W)], w_sems.at[k, block]
        )

    def store(k):
        return pltpu.make_async_copy(held.at[k], outs[k], out_sems.at[k])

    hidden = pltpu.make_async_copy(h_ref.at[pl.ds(start, mine.shape[0])], mine, h_sem)
    hidden.start()
    for k in range(4):
        for block in range(m):
            for slot in range(4):

                @pl.when(slot_of[k] == slot)
                def _(k=k, block=block, slot=slot):
                    load(k, block, slot).start()

    hidden.wait()
    for k in range(4):
        for block in range(m):
            load(k, block, 0).wait()
        held[k] = jnp.dot(mine[...], wide[k], preferred_element_type=F32).astype(BF)
        store(k).start()
    for k in range(4):
        store(k).wait()


def partials(hidden, blocks, slot_of, start, rows):
    full = hidden.shape[1]
    m = len(blocks)
    flat = [w for four in blocks for w in four]
    anywhere = pl.BlockSpec(memory_space=pl.ANY)
    return pl.pallas_call(
        functools.partial(partial_kernel, m, start),
        out_shape=[pltpu.HBM((rows, m * W), BF)] * 4,
        grid_spec=pltpu.PrefetchScalarGridSpec(
            num_scalar_prefetch=1,
            grid=(1,),
            in_specs=[anywhere] * (1 + 4 * m),
            out_specs=[anywhere] * 4,
            scratch_shapes=[
                pltpu.VMEM((rows, full), BF),
                pltpu.VMEM((4, full, m * W), BF),
                pltpu.VMEM((4, rows, m * W), BF),
                pltpu.SemaphoreType.DMA,
                pltpu.SemaphoreType.DMA((4, m)),
                pltpu.SemaphoreType.DMA((4,)),
            ],
        ),
        compiler_params=params(20),
        cost_estimate=COST,
        name="partials",
    )(slot_of, in_hbm(hidden), *flat)


def regroup_kernel(offsets, place, *refs):
    outs = refs[4 * len(offsets) :]
    i = pl.program_id(0)

    def add(group, offs):
        four = refs[4 * group : 4 * group + 4]
        total = four[0][...].astype(F32)
        for ref in four[1:]:
            total += ref[...].astype(F32)
        total = total.astype(BF)
        for block, off in enumerate(offs):
            for which in range(4):

                @pl.when(place[off] == which)
                def _(total=total, block=block, which=which):
                    outs[which][...] = total[:, block * W : (block + 1) * W]

    for group, offs in enumerate(offsets[:-2]):
        add(group, offs)
    pl.when(i < 2)(lambda: add(len(offsets) - 2, offsets[-2]))
    pl.when(i >= 2)(lambda: add(len(offsets) - 1, offsets[-1]))


def regroup(groups, place):
    rows = groups[0][0][0].shape[0]
    tile = rows // 4
    specs, arrays = [], []
    row_of = [lambda i: i] * (len(groups) - 2) + [lambda i: jnp.minimum(i, 1), lambda i: jnp.maximum(i - 2, 0)]
    for (four, offs), row in zip(groups, row_of):
        specs += [pl.BlockSpec((tile, len(offs) * W), lambda i, s, row=row: (row(i), 0))] * 4
        arrays += four
    return pl.pallas_call(
        functools.partial(regroup_kernel, [offs for _, offs in groups]),
        out_shape=[pltpu.HBM((rows, W), BF)] * 4,
        grid_spec=pltpu.PrefetchScalarGridSpec(
            num_scalar_prefetch=1,
            grid=(rows // tile,),
            in_specs=specs,
            out_specs=[pl.BlockSpec((tile, W), lambda i, s: (i, 0))] * 4,
        ),
        compiler_params=params(16),
        cost_estimate=COST,
        name="regroup",
    )(place, *arrays)


def spread(parts, axis):
    got = [parts[3]] + [shift(parts[k - 1], axis, k) for k in (1, 3, 2)]
    return [in_hbm(part) for part in got] if axis == "x" else got


def finish_kernel(a, b, c, d, out):
    total = a[...].astype(F32) + b[...].astype(F32) + c[...].astype(F32) + d[...].astype(F32)
    out[...] = total.astype(BF)


def finish(parts):
    rows = parts[0].shape[0]
    tile = rows // 2
    spec = pl.BlockSpec((tile, W), lambda i: (i, 0))
    return pl.pallas_call(
        finish_kernel,
        out_shape=jax.ShapeDtypeStruct((rows, W), BF),
        grid=(2,),
        in_specs=[spec] * 4,
        out_specs=spec,
        compiler_params=params(12),
        cost_estimate=LIGHT,
        name="finish",
    )(*parts)


def low_kernel(parts, out):
    total = parts[0].astype(F32)
    for s in range(1, 4):
        total += parts[s].astype(F32)
    out[...] = total.astype(BF)


def low_sum(parts):
    return pl.pallas_call(
        low_kernel,
        out_shape=jax.ShapeDtypeStruct(parts.shape[1:], BF),
        in_specs=[pl.BlockSpec(memory_space=pltpu.VMEM)],
        out_specs=pl.BlockSpec(memory_space=pltpu.VMEM),
        compiler_params=params(8),
        cost_estimate=COST,
        name="low_sum",
    )(parts)


def grad_kernel(low_ref, cot_ref, out, low):
    @pl.when(pl.program_id(0) == 0)
    def _():
        low_kernel(low_ref, low)

    for block in range(4):
        out[block] = jnp.dot(
            low[...], cot_ref[:, block * W : (block + 1) * W], preferred_element_type=F32
        )


def grad_partial(low_parts, cotangent):
    tokens, features = cotangent.shape
    ranks = low_parts.shape[1]
    return pl.pallas_call(
        grad_kernel,
        out_shape=pltpu.HBM((features // W, ranks, W), F32),
        grid=(features // (4 * W),),
        in_specs=[
            pl.BlockSpec(low_parts.shape, lambda i: (0, 0, 0)),
            pl.BlockSpec((tokens, 4 * W), lambda i: (0, i)),
        ],
        out_specs=pl.BlockSpec((4, ranks, W), lambda i: (i, 0, 0)),
        scratch_shapes=[pltpu.VMEM((ranks, tokens), BF)],
        compiler_params=params(8),
        cost_estimate=COST,
        name="grad_partial",
    )(low_parts, in_hbm(cotangent))


def moments_kernel(grads, first, second, new_first, new_second, normed):
    grad = grads[0]
    for s in range(1, 16):
        grad = grad + grads[s]
    one = 0.9 * first[...] + 0.1 * grad
    two = 0.999 * second[...] + 0.001 * grad * grad
    new_first[...] = one
    new_second[...] = two
    first_fix = 1.0 - 0.9**STEP
    second_fix = 1.0 - 0.999**STEP
    step = (one / first_fix / (jnp.sqrt(two / second_fix) + 1e-08)).astype(BF)
    for s in range(16):
        normed[s] = step


def moments(grads, first, second):
    full = pl.BlockSpec(memory_space=pltpu.VMEM)
    return pl.pallas_call(
        moments_kernel,
        out_shape=[jax.ShapeDtypeStruct(first.shape, F32)] * 2
        + [jax.ShapeDtypeStruct((16, *first.shape), BF)],
        in_specs=[full] * 3,
        out_specs=[full] * 3,
        compiler_params=params(8),
        cost_estimate=LIGHT,
        name="moments",
    )(grads, first, second)


def act_kernel(order, cot_ref, *refs):
    w_refs, out_ref = refs[:16], refs[16]
    cots, wide, total, cot_sems, w_sems = refs[17:]
    span = 4 * W

    def cot_part(i):
        at = pl.multiple_of(order[i] * span, span)
        return pltpu.make_async_copy(cot_ref.at[:, pl.ds(at, span)], cots.at[i], cot_sems.at[i])

    def shard(i, slot):
        at = pl.multiple_of(order[4 + slot] * W, W)
        return pltpu.make_async_copy(
            w_refs[4 * i + slot], wide.at[i, :, pl.ds(at, W)], w_sems.at[i, slot]
        )

    for i in range(4):
        for slot in range(4):
            shard(i, slot).start()
        cot_part(i).start()
    for i in range(4):
        for slot in range(4):
            shard(i, slot).wait()
        cot_part(i).wait()
        product = lax.dot_general(
            cots[i], wide[i], (((1,), (1,)), ((), ())), preferred_element_type=F32
        )
        if i == 0:
            total[...] = product
        elif i < 3:
            total[...] += product
        else:
            out_ref[...] = (total[...] + product).astype(BF)


def act(cotangent, blocks, order):
    tokens, features = cotangent.shape
    flat = [w for four in blocks for w in four]
    full = flat[0].shape[0]
    anywhere = pl.BlockSpec(memory_space=pl.ANY)
    return pl.pallas_call(
        act_kernel,
        out_shape=jax.ShapeDtypeStruct((tokens, full), BF),
        grid_spec=pltpu.PrefetchScalarGridSpec(
            num_scalar_prefetch=1,
            grid=(1,),
            in_specs=[anywhere] * 17,
            out_specs=pl.BlockSpec((tokens, full), lambda i, s: (0, 0)),
            scratch_shapes=[
                pltpu.VMEM((4, tokens, 4 * W), BF),
                pltpu.VMEM((4, full, 4 * W), BF),
                pltpu.VMEM((tokens, full), F32),
                pltpu.SemaphoreType.DMA((4,)),
                pltpu.SemaphoreType.DMA((4, 4)),
            ],
        ),
        compiler_params=params(30),
        cost_estimate=COST,
        name="act_grad",
    )(order, in_hbm(cotangent), *flat)


def on_device(hidden, cotangent, weight, basis, first_moment, second_moment):
    zh, x, y, zl, c = (lax.axis_index(a) for a in AXES)
    tokens = hidden.shape[0]
    half = tokens // 2

    low_part = lax.dot_general(
        basis, hidden, (((0,), (1,)), ((), ())), preferred_element_type=F32
    ).astype(BF)
    low_part = low_part.reshape(4, 4, 32, tokens).transpose(1, 0, 2, 3)

    side = shift(weight, "zl", 1)
    next0, prev0 = shift(weight, "y", -1), shift(weight, "y", 1)
    low_x = swap(after(low_part, weight), "x")
    side = after(side, low_part, next0, prev0)
    next1, prev1 = shift(side, "y", -1), shift(side, "y", 1)

    def both_cores(own, other):
        return own, shift(own, "c", 1), other, shift(other, "c", 1)

    dest = [2 * (zl ^ (s // 2)) + (c ^ (s % 2)) for s in range(4)]
    goals = [(x + k) % 4 for k in (1, 2, 3, 0)]
    slot_of = jnp.stack([2 * ((g // 2) ^ zl) + ((g % 2) ^ c) for g in goals]).astype(jnp.int32)
    place = jnp.stack([(y + k - zh + 3) % 4 for k in range(4)]).astype(jnp.int32)

    slots = {0: both_cores(weight, side)}
    next0c, prev0c = shift(after(next0, low_part), "c", 1), shift(after(prev0, low_part), "c", 1)
    part0 = partials(after(hidden, next0c, prev0c, low_x), [slots[0]], slot_of, 0, tokens)
    sum0 = spread(part0, "x")
    next1c, prev1c = shift(after(next1, *part0), "c", 1), shift(after(prev1, *part0), "c", 1)
    slots[1] = next0, next0c, next1, next1c
    slots[3] = prev0, prev0c, prev1, prev1c
    far0 = shift(after(next0, next1c, prev1c, *part0), "y", -1)
    far1 = shift(after(prev1, next1c, prev1c, *part0), "y", 1)
    near = [slots[1], slots[3]]
    part1 = partials(after(hidden, *part0), near, slot_of, 0, tokens)
    sum1 = spread(part1, "x")
    slots[2] = both_cores(after(far0, *sum0[1:]), after(far1, *sum0[1:]))
    low_z = swap(low_sum(after(low_x, *part1)), "zh")
    part2 = partials(after(hidden, *part1), [slots[2]], slot_of, 0, half)
    sum2 = spread(part2, "x")
    part3 = partials(after(hidden, *sum1[1:], *part2), [slots[2]], slot_of, half, half)
    sum3 = spread(part3, "x")

    grad_all = swap(grad_partial(after(low_z, *part2), cotangent), FSDP)
    new_first, new_second, normed = moments(grad_all, first_moment, second_moment)
    normed_all = swap(normed, DP)

    order = jnp.stack([(y + off) % 4 for off in slots] + dest).astype(jnp.int32)
    zparts = regroup([(sum0, (0,)), (sum1, (1, 3)), (sum2, (2,)), (sum3, (2,))], place)
    act_grad = act(after(cotangent, *zparts), [[in_hbm(w) for w in four] for four in slots.values()], order)
    normed_all = after(normed_all, *zparts).reshape(-1, W)
    update = jnp.dot(basis, normed_all, preferred_element_type=F32).astype(BF)
    output = finish(spread(zparts, "zh"))
    return output, act_grad, new_first, new_second, update


def solution(mesh):
    fine = Mesh(mesh.devices.reshape(tuple(SIZE[a] for a in AXES)), AXES)
    in_specs = (
        P(FSDP, DP),
        P(FSDP, None),
        P(DP, FSDP),
        P(DP, None),
        P(DP, FSDP),
        P(DP, FSDP),
    )
    out_specs = (P(FSDP, DP), P(FSDP, DP), P(DP, FSDP), P(DP, FSDP), P(DP, FSDP))
    return jax.shard_map(
        on_device, mesh=fine, in_specs=in_specs, out_specs=out_specs, check_vma=False
    )
```

profile of v0, /device:TPU:32, one launch (start us, length us, event | category | flops | bytes accessed | tf_op | source)
XLA Modules:
  0.0 167.2 jit_solution(243408262367261770)
XLA Ops:
  0.6 1.7 collective-permute-start.2
  2.3 1.7 collective-permute-start
  4.0 1.8 %collective-permute-start.5 = (bf16[896,256]{1,0:T(8,128)(2,1)}, bf16[896,256]{1,0:T(8,128)(2,1)}, u32[]{:S(2)}, u32[]{:S(2)}) collective-permute-start(bf16[896,256]{1,0:T(8,128)(2,1)} %refs_0_.3), channel_id=1, source_target_pairs={{0,2},{2,0},{1,3},{3,1},{4,6},{6,4},{5,7},{7,5},{8,10},{10,8},{9,1... | collective-permute-start | bytes 1376264 | tf_op jit(solution)/shard_map/ppermute | solution.py:26
  5.8 2.4 %convolution_convert_fusion = bf16[512,768]{1,0:T(8,128)(2,1)S(1)} fusion(bf16[896,512]{1,0:T(8,128)(2,1)S(1)} %copy-done, bf16[768,896]{1,0:T(8,128)(2,1)} %h_ref.3), kind=kOutput, calls=%fused_computation | convolution fusion | flops 705036288 | bytes 3080192 | tf_op jit(solution)/shard_map/dot_general | solution.py:321
  8.2 0.9 copy.15
  9.1 3.5 %all-to-all-start = ((bf16[4,4,32,768]{3,2,1,0:T(8,128)(2,1)}), bf16[4,4,32,768]{3,2,1,0:T(8,128)(2,1)S(1)}, u32[]{:S(2)}, u32[]{:S(2)}) async-start(bf16[4,4,32,768]{3,2,1,0:T(8,128)(2,1)} %bitcast.27), calls=%async_computation | async-start | bytes 1572864 | tf_op jit(solution)/shard_map/all_to_all | solution.py:30
  12.7 1.7 %collective-permute-done.2.refs_4_.refs_8_ = bf16[896,256]{1,0:T(8,128)(2,1)S(1)} collective-permute-done((bf16[896,256]{1,0:T(8,128)(2,1)}, bf16[896,256]{1,0:T(8,128)(2,1)S(1)}, u32[]{:S(2)}, u32[]{:S(2)}) %collective-permute-start.2) | collective-permute-done | bytes 458784 | tf_op jit(solution)/shard_map/ppermute | solution.py:26
  14.6 0.5 collective-permute-start.3
  15.1 1.1 collective-permute-done.5.refs_2_
  16.7 2.8 %collective-permute-start.10 = (bf16[896,256]{1,0:T(8,128)(2,1)}, bf16[896,256]{1,0:T(8,128)(2,1)}, u32[]{:S(2)}, u32[]{:S(2)}) collective-permute-start(bf16[896,256]{1,0:T(8,128)(2,1)} %collective-permute-done.5.refs_2_), channel_id=1, source_target_pairs={{0,12},{4,0},{8,4},{12,8},{1,13},{5,1},{9,5},{13,9},{2,14},{6,2},{... | collective-permute-start | bytes 1376264 | tf_op jit(solution)/shard_map/ppermute | solution.py:26
  19.5 4.0 %all-to-all-done.parts = bf16[4,4,32,768]{3,2,1,0:T(8,128)(2,1)S(1)} async-done(((bf16[4,4,32,768]{3,2,1,0:T(8,128)(2,1)}), bf16[4,4,32,768]{3,2,1,0:T(8,128)(2,1)S(1)}, u32[]{:S(2)}, u32[]{:S(2)}) %all-to-all-start) | async-done | bytes 786464 | tf_op jit(solution)/shard_map/all_to_all | solution.py:30
  23.5 6.7 %partials.4 = (bf16[768,256]{1,0:T(8,128)(2,1)}, bf16[768,256]{1,0:T(8,128)(2,1)}, bf16[768,256]{1,0:T(8,128)(2,1)}, bf16[768,256]{1,0:T(8,128)(2,1)}) custom-call(s32[4]{0:T(128)S(1)} %pad_add_fusion.1.slot_of, bf16[768,896]{1,0:T(8,128)(2,1)} %h_ref.3, bf16[896,256]{1,0:T(8,128)(2,1)S(1)} %copy-done.4, bf16[896,256]{1,0:T(8,128)(2,1)} %collective-permute-done.4.refs_1_, ...), custom_call_target="tpu_custom_call" | custom-call | flops 8589934592 | bytes 33554432 | tf_op jit(solution)/shard_map/partials/pallas_call | solution.py:82
  30.1 0.5 collective-permute-done.12.refs_6_.refs_10_
  30.7 0.5 collective-permute-start.13
  31.2 1.5 collective-permute-start.7
  32.7 1.7 %collective-permute-start.8 = (bf16[768,256]{1,0:T(8,128)(2,1)}, bf16[768,256]{1,0:T(8,128)(2,1)S(1)}, u32[]{:S(2)}, u32[]{:S(2)}) collective-permute-start(bf16[768,256]{1,0:T(8,128)(2,1)} %get-tuple-element.53), channel_id=1, source_target_pairs={{0,48},{16,0},{32,16},{48,32},{1,49},{17,1},{33,17},{49,33},{2,50}... | collective-permute-start | bytes 1179656 | tf_op jit(solution)/shard_map/ppermute | solution.py:26
  34.4 1.8 %collective-permute-start.9 = (bf16[768,256]{1,0:T(8,128)(2,1)}, bf16[768,256]{1,0:T(8,128)(2,1)S(1)}, u32[]{:S(2)}, u32[]{:S(2)}) collective-permute-start(bf16[768,256]{1,0:T(8,128)(2,1)} %get-tuple-element.54), channel_id=1, source_target_pairs={{0,32},{16,48},{32,0},{48,16},{1,33},{17,49},{33,1},{49,17},{2,34}... | collective-permute-start | bytes 1179656 | tf_op jit(solution)/shard_map/ppermute | solution.py:26
  36.3 3.0 %collective-permute-start.17 = (bf16[896,256]{1,0:T(8,128)(2,1)S(1)}, bf16[896,256]{1,0:T(8,128)(2,1)}, u32[]{:S(2)}, u32[]{:S(2)}) collective-permute-start(bf16[896,256]{1,0:T(8,128)(2,1)S(1)} %collective-permute-done.refs_0_.refs_4_), channel_id=1, source_target_pairs={{0,12},{4,0},{8,4},{12,8},{1,13},{5,1},{9,5},{13,9},{2,14},{6,2},{... | collective-permute-start | bytes 1376264 | tf_op jit(solution)/shard_map/ppermute | solution.py:26
  39.3 6.8 %partials.5 = (bf16[768,512]{1,0:T(8,128)(2,1)}, bf16[768,512]{1,0:T(8,128)(2,1)}, bf16[768,512]{1,0:T(8,128)(2,1)}, bf16[768,512]{1,0:T(8,128)(2,1)}) custom-call(s32[4]{0:T(128)S(1)} %pad_add_fusion.1.slot_of, bf16[768,896]{1,0:T(8,128)(2,1)} %h_ref.3, bf16[896,256]{1,0:T(8,128)(2,1)S(1)} %collective-permute-done.refs_0_.refs_4_, ...), custom_call_target="tpu_custom_call" | custom-call | flops 8589934592 | bytes 33554432 | tf_op jit(solution)/shard_map/partials/pallas_call | solution.py:82
  46.2 0.7 collective-permute-start.14
  46.9 3.3 %collective-permute-done.8.refs_2_ = bf16[768,256]{1,0:T(8,128)(2,1)S(1)} collective-permute-done((bf16[768,256]{1,0:T(8,128)(2,1)}, bf16[768,256]{1,0:T(8,128)(2,1)S(1)}, u32[]{:S(2)}, u32[]{:S(2)}) %collective-permute-start.8) | collective-permute-done | bytes 393248 | tf_op jit(solution)/shard_map/ppermute | solution.py:26
  50.2 4.0 %collective-permute-start.15 = (bf16[768,512]{1,0:T(8,128)(2,1)}, bf16[768,512]{1,0:T(8,128)(2,1)}, u32[]{:S(2)}, u32[]{:S(2)}) collective-permute-start(bf16[768,512]{1,0:T(8,128)(2,1)} %get-tuple-element.60), channel_id=1, source_target_pairs={{0,48},{16,0},{32,16},{48,32},{1,49},{17,1},{33,17},{49,33},{2,50}... | collective-permute-start | bytes 2359304 | tf_op jit(solution)/shard_map/ppermute | solution.py:26
  54.2 0.6 collective-permute-start.16
  55.5 0.8 low_sum.1
  56.2 8.6 %all-to-all-start.1 = ((bf16[4,32,768]{2,1,0:T(8,128)(2,1)}), bf16[4,32,768]{2,1,0:T(8,128)(2,1)S(1)}, u32[]{:S(2)}, u32[]{:S(2)}) async-start(bf16[4,32,768]{2,1,0:T(8,128)(2,1)} %low_sum.1), calls=%async_computation.1 | async-start | bytes 393216 | tf_op jit(solution)/shard_map/all_to_all | solution.py:30
  64.9 4.6 %partials.6 = (bf16[384,256]{1,0:T(8,128)(2,1)}, bf16[384,256]{1,0:T(8,128)(2,1)}, bf16[384,256]{1,0:T(8,128)(2,1)}, bf16[384,256]{1,0:T(8,128)(2,1)}) custom-call(s32[4]{0:T(128)S(1)} %pad_add_fusion.1.slot_of, bf16[768,896]{1,0:T(8,128)(2,1)} %h_ref.3, bf16[896,256]{1,0:T(8,128)(2,1)} %collective-permute-done.17.refs_0_.refs_12_, ...), custom_call_target="tpu_custom_call" | custom-call | flops 8589934592 | bytes 33554432 | tf_op jit(solution)/shard_map/partials/pallas_call | solution.py:82
  69.5 1.2 collective-permute-start.21
  70.7 2.1 %collective-permute-start.22 = (bf16[384,256]{1,0:T(8,128)(2,1)}, bf16[384,256]{1,0:T(8,128)(2,1)S(1)}, u32[]{:S(2)}, u32[]{:S(2)}) collective-permute-start(bf16[384,256]{1,0:T(8,128)(2,1)} %get-tuple-element.69), channel_id=1, source_target_pairs={{0,48},{16,0},{32,16},{48,32},{1,49},{17,1},{33,17},{49,33},{2,50}... | collective-permute-start | bytes 589832 | tf_op jit(solution)/shard_map/ppermute | solution.py:26
  72.9 2.2 %collective-permute-start.23 = (bf16[384,256]{1,0:T(8,128)(2,1)}, bf16[384,256]{1,0:T(8,128)(2,1)}, u32[]{:S(2)}, u32[]{:S(2)}) collective-permute-start(bf16[384,256]{1,0:T(8,128)(2,1)} %get-tuple-element.70), channel_id=1, source_target_pairs={{0,32},{16,48},{32,0},{48,16},{1,33},{17,49},{33,1},{49,17},{2,34}... | collective-permute-start | bytes 589832 | tf_op jit(solution)/shard_map/ppermute | solution.py:26
  75.0 12.9 %collective-permute-done.16.refs_7_ = bf16[768,512]{1,0:T(8,128)(2,1)} collective-permute-done((bf16[768,512]{1,0:T(8,128)(2,1)}, bf16[768,512]{1,0:T(8,128)(2,1)}, u32[]{:S(2)}, u32[]{:S(2)}) %collective-permute-start.16) | collective-permute-done | bytes 786464 | tf_op jit(solution)/shard_map/ppermute | solution.py:26
  87.9 4.6 %partials.7 = (bf16[384,256]{1,0:T(8,128)(2,1)}, bf16[384,256]{1,0:T(8,128)(2,1)}, bf16[384,256]{1,0:T(8,128)(2,1)}, bf16[384,256]{1,0:T(8,128)(2,1)}) custom-call(s32[4]{0:T(128)S(1)} %pad_add_fusion.1.slot_of, bf16[768,896]{1,0:T(8,128)(2,1)} %h_ref.3, bf16[896,256]{1,0:T(8,128)(2,1)} %collective-permute-done.17.refs_0_.refs_12_, ...), custom_call_target="tpu_custom_call" | custom-call | flops 8589934592 | bytes 33554432 | tf_op jit(solution)/shard_map/partials/pallas_call | solution.py:82
  92.6 3.3 %collective-permute-start.24 = (bf16[384,256]{1,0:T(8,128)(2,1)}, bf16[384,256]{1,0:T(8,128)(2,1)S(1)}, u32[]{:S(2)}, u32[]{:S(2)}) collective-permute-start(bf16[384,256]{1,0:T(8,128)(2,1)} %get-tuple-element.73), channel_id=1, source_target_pairs={{0,16},{16,32},{32,48},{48,0},{1,17},{17,33},{33,49},{49,1},{2,18}... | collective-permute-start | bytes 589832 | tf_op jit(solution)/shard_map/ppermute | solution.py:26
  96.1 1.9 %collective-permute-start.26 = (bf16[384,256]{1,0:T(8,128)(2,1)}, bf16[384,256]{1,0:T(8,128)(2,1)S(1)}, u32[]{:S(2)}, u32[]{:S(2)}) collective-permute-start(bf16[384,256]{1,0:T(8,128)(2,1)} %get-tuple-element.75), channel_id=1, source_target_pairs={{0,32},{16,48},{32,0},{48,16},{1,33},{17,49},{33,1},{49,17},{2,34}... | collective-permute-start | bytes 589832 | tf_op jit(solution)/shard_map/ppermute | solution.py:26
  98.0 5.0 %grad_partial.1 = f32[16,32,256]{2,1,0:T(8,128)} custom-call(bf16[4,32,768]{2,1,0:T(8,128)(2,1)S(1)} %all-to-all-done.1.low_ref, bf16[768,4096]{1,0:T(8,128)(2,1)} %cot_ref.2), custom_call_target="tpu_custom_call" | custom-call | flops 8589934592 | bytes 33554432 | tf_op jit(solution)/shard_map/grad_partial/pallas_call | solution.py:210
  103.0 5.7 %all-to-all-start.2 = ((f32[16,32,256]{2,1,0:T(8,128)}), f32[16,32,256]{2,1,0:T(8,128)S(1)}, u32[]{:S(2)}, u32[]{:S(2)}) async-start(f32[16,32,256]{2,1,0:T(8,128)} %grad_partial.1), calls=%async_computation.2 | async-start | bytes 1048576 | tf_op jit(solution)/shard_map/all_to_all | solution.py:30
  109.0 0.6 copy-done.15
  109.8 5.9 %regroup.1 = (bf16[768,256]{1,0:T(8,128)(2,1)}, bf16[768,256]{1,0:T(8,128)(2,1)}, bf16[768,256]{1,0:T(8,128)(2,1)}, bf16[768,256]{1,0:T(8,128)(2,1)}) custom-call(s32[4]{0:T(128)S(1)} %pad_add_fusion.place, bf16[768,256]{1,0:T(8,128)(2,1)} %get-tuple-element.51.refs_0_, bf16[768,256]{1,0:T(8,128)(2,1)} %copy-done.11, bf16[768,256]{1,0:T(8,128)(2,1)} %copy-done.12, ...), custom_call_target="tpu_custom_call" | custom-call | flops 8589934592 | bytes 33554432 | tf_op jit(solution)/shard_map/regroup/pallas_call | solution.py:136
  115.7 3.3 %collective-permute-start.27 = (bf16[768,256]{1,0:T(8,128)(2,1)}, bf16[768,256]{1,0:T(8,128)(2,1)S(1)}, u32[]{:S(2)}, u32[]{:S(2)}) collective-permute-start(bf16[768,256]{1,0:T(8,128)(2,1)} %get-tuple-element.77), channel_id=1, source_target_pairs={{0,64},{64,128},{128,192},{192,0},{1,65},{65,129},{129,193},{193,1... | collective-permute-start | bytes 1179656 | tf_op jit(solution)/shard_map/ppermute | solution.py:26
  119.0 2.5 %collective-permute-start.28 = (bf16[768,256]{1,0:T(8,128)(2,1)}, bf16[768,256]{1,0:T(8,128)(2,1)S(1)}, u32[]{:S(2)}, u32[]{:S(2)}) collective-permute-start(bf16[768,256]{1,0:T(8,128)(2,1)} %get-tuple-element.78), channel_id=1, source_target_pairs={{0,192},{64,0},{128,64},{192,128},{1,193},{65,1},{129,65},{193,129... | collective-permute-start | bytes 1179656 | tf_op jit(solution)/shard_map/ppermute | solution.py:26
  121.6 5.0 %collective-permute-start.29 = (bf16[768,256]{1,0:T(8,128)(2,1)}, bf16[768,256]{1,0:T(8,128)(2,1)S(1)}, u32[]{:S(2)}, u32[]{:S(2)}) collective-permute-start(bf16[768,256]{1,0:T(8,128)(2,1)} %get-tuple-element.79), channel_id=1, source_target_pairs={{0,128},{64,192},{128,0},{192,64},{1,129},{65,193},{129,1},{193,65... | collective-permute-start | bytes 1179656 | tf_op jit(solution)/shard_map/ppermute | solution.py:26
  126.5 0.8 moments.1
  127.3 4.3 %all-to-all-start.3 = ((bf16[16,32,256]{2,1,0:T(8,128)(2,1)}), bf16[16,32,256]{2,1,0:T(8,128)(2,1)S(1)}, u32[]{:S(2)}, u32[]{:S(2)}) async-start(bf16[16,32,256]{2,1,0:T(8,128)(2,1)} %get-tuple-element.85), calls=%async_computation.3 | async-start | bytes 524288 | tf_op jit(solution)/shard_map/all_to_all | solution.py:30
  131.7 12.2 %act_grad.1 = bf16[768,896]{1,0:T(8,128)(2,1)} custom-call(s32[8]{0:T(128)S(1)} %stack.75.order, bf16[768,4096]{1,0:T(8,128)(2,1)} %cot_ref.2, bf16[896,256]{1,0:T(8,128)(2,1)} %refs_0_.3, bf16[896,256]{1,0:T(8,128)(2,1)} %collective-permute-done.4.refs_1_, bf16[896,256]{1,0:T(8,128)(2,1)} %collective-permute-done.5.refs_2_, ...), custom_call_target="tpu_custom_call" | custom-call | flops 8589934592 | bytes 33554432 | tf_op jit(solution)/shard_map/act_grad/pallas_call | solution.py:294
  143.9 16.5 %collective-permute-done.27.b = bf16[768,256]{1,0:T(8,128)(2,1)S(1)} collective-permute-done((bf16[768,256]{1,0:T(8,128)(2,1)}, bf16[768,256]{1,0:T(8,128)(2,1)S(1)}, u32[]{:S(2)}, u32[]{:S(2)}) %collective-permute-start.27) | collective-permute-done | bytes 393248 | tf_op jit(solution)/shard_map/ppermute | solution.py:26
  160.4 1.4 collective-permute-done.29.d
  161.8 0.9 finish.1
  162.7 3.0 %all-to-all-done.3 = bf16[16,32,256]{2,1,0:T(8,128)(2,1)S(1)} async-done(((bf16[16,32,256]{2,1,0:T(8,128)(2,1)}), bf16[16,32,256]{2,1,0:T(8,128)(2,1)S(1)}, u32[]{:S(2)}, u32[]{:S(2)}) %all-to-all-start.3) | async-done | bytes 262176 | tf_op jit(solution)/shard_map/all_to_all | solution.py:30
  166.2 1.0 copy.13
  (75 shorter events, 2.5 us)
Async XLA Ops:
  0.6 5.2 %copy-start = (bf16[896,512]{1,0:T(8,128)(2,1)S(1)}, bf16[896,512]{1,0:T(8,128)(2,1)}, u32[]{:S(2)}) copy-start(bf16[896,512]{1,0:T(8,128)(2,1)} %param.9) | copy-start | bytes 2752516
  0.6 13.8 %collective-permute-start.2 = (bf16[896,256]{1,0:T(8,128)(2,1)}, bf16[896,256]{1,0:T(8,128)(2,1)S(1)}, u32[]{:S(2)}, u32[]{:S(2)}) collective-permute-start(bf16[896,256]{1,0:T(8,128)(2,1)} %refs_0_.3), channel_id=1, source_target_pairs={{0,4},{4,8},{8,12},{12,0},{1,5},{5,9},{9,13},{13,1},{2,6},{6,10},{... | collective-permute-start | bytes 1376264 | tf_op jit(solution)/shard_map/ppermute | solution.py:26
  2.3 12.2 %collective-permute-start = (bf16[896,256]{1,0:T(8,128)(2,1)}, bf16[896,256]{1,0:T(8,128)(2,1)S(1)}, u32[]{:S(2)}, u32[]{:S(2)}) collective-permute-start(bf16[896,256]{1,0:T(8,128)(2,1)} %refs_0_.3), channel_id=1, source_target_pairs={{0,12},{4,0},{8,4},{12,8},{1,13},{5,1},{9,5},{13,9},{2,14},{6,2},{... | collective-permute-start | bytes 1376264 | tf_op jit(solution)/shard_map/ppermute | solution.py:26
  4.0 12.2 %collective-permute-start.5 = (bf16[896,256]{1,0:T(8,128)(2,1)}, bf16[896,256]{1,0:T(8,128)(2,1)}, u32[]{:S(2)}, u32[]{:S(2)}) collective-permute-start(bf16[896,256]{1,0:T(8,128)(2,1)} %refs_0_.3), channel_id=1, source_target_pairs={{0,2},{2,0},{1,3},{3,1},{4,6},{6,4},{5,7},{7,5},{8,10},{10,8},{9,1... | collective-permute-start | bytes 1376264 | tf_op jit(solution)/shard_map/ppermute | solution.py:26
  8.2 4.5 %copy-start.4 = (bf16[896,256]{1,0:T(8,128)(2,1)S(1)}, bf16[896,256]{1,0:T(8,128)(2,1)}, u32[]{:S(2)}) copy-start(bf16[896,256]{1,0:T(8,128)(2,1)} %refs_0_.3) | copy-start | bytes 1376260
  9.1 14.3 %all-to-all-start = ((bf16[4,4,32,768]{3,2,1,0:T(8,128)(2,1)}), bf16[4,4,32,768]{3,2,1,0:T(8,128)(2,1)S(1)}, u32[]{:S(2)}, u32[]{:S(2)}) async-start(bf16[4,4,32,768]{3,2,1,0:T(8,128)(2,1)} %bitcast.27), calls=%async_computation | async-start | bytes 1572864 | tf_op jit(solution)/shard_map/all_to_all | solution.py:30
  12.6 10.8 %collective-permute-start.4 = (bf16[896,256]{1,0:T(8,128)(2,1)S(1)}, bf16[896,256]{1,0:T(8,128)(2,1)}, u32[]{:S(2)}, u32[]{:S(2)}) collective-permute-start(bf16[896,256]{1,0:T(8,128)(2,1)S(1)} %copy-done.4), channel_id=1, source_target_pairs={{0,1},{1,0},{2,3},{3,2},{4,5},{5,4},{6,7},{7,6},{8,9},{9,8},{10,11... | collective-permute-start | bytes 1376264 | tf_op jit(solution)/shard_map/ppermute | solution.py:26
  14.5 24.8 %copy-start.5 = (bf16[896,256]{1,0:T(8,128)(2,1)}, bf16[896,256]{1,0:T(8,128)(2,1)S(1)}, u32[]{:S(2)}) copy-start(bf16[896,256]{1,0:T(8,128)(2,1)S(1)} %collective-permute-done.2.refs_4_.refs_8_) | copy-start | bytes 1376260
  14.5 24.8 %copy-start.6 = (bf16[896,256]{1,0:T(8,128)(2,1)}, bf16[896,256]{1,0:T(8,128)(2,1)S(1)}, u32[]{:S(2)}) copy-start(bf16[896,256]{1,0:T(8,128)(2,1)S(1)} %collective-permute-done.refs_0_.refs_4_) | copy-start | bytes 1376260
  14.5 2.2 %collective-permute-start.1 = (bf16[896,256]{1,0:T(8,128)(2,1)S(1)}, bf16[896,256]{1,0:T(8,128)(2,1)}, u32[]{:S(2)}, u32[]{:S(2)}) collective-permute-start(bf16[896,256]{1,0:T(8,128)(2,1)S(1)} %collective-permute-done.refs_0_.refs_4_), channel_id=1, source_target_pairs={{0,1},{1,0},{2,3},{3,2},{4,5},{5,4},{6,7},{7,6},{8,9},{9,8},{10,11... | collective-permute-start | bytes 1376264 | tf_op jit(solution)/shard_map/ppermute | solution.py:26
  14.6 8.9 %collective-permute-start.3 = (bf16[896,256]{1,0:T(8,128)(2,1)S(1)}, bf16[896,256]{1,0:T(8,128)(2,1)}, u32[]{:S(2)}, u32[]{:S(2)}) collective-permute-start(bf16[896,256]{1,0:T(8,128)(2,1)S(1)} %collective-permute-done.2.refs_4_.refs_8_), channel_id=1, source_target_pairs={{0,1},{1,0},{2,3},{3,2},{4,5},{5,4},{6,7},{7,6},{8,9},{9,8},{10,11... | collective-permute-start | bytes 1376264 | tf_op jit(solution)/shard_map/ppermute | solution.py:26
  16.1 7.3 %collective-permute-start.6 = (bf16[896,256]{1,0:T(8,128)(2,1)}, bf16[896,256]{1,0:T(8,128)(2,1)}, u32[]{:S(2)}, u32[]{:S(2)}) collective-permute-start(bf16[896,256]{1,0:T(8,128)(2,1)} %collective-permute-done.5.refs_2_), channel_id=1, source_target_pairs={{0,1},{1,0},{2,3},{3,2},{4,5},{5,4},{6,7},{7,6},{8,9},{9,8},{10,11... | collective-permute-start | bytes 1376264 | tf_op jit(solution)/shard_map/ppermute | solution.py:26
  16.2 14.5 %collective-permute-start.12 = (bf16[896,256]{1,0:T(8,128)(2,1)}, bf16[896,256]{1,0:T(8,128)(2,1)}, u32[]{:S(2)}, u32[]{:S(2)}) collective-permute-start(bf16[896,256]{1,0:T(8,128)(2,1)} %collective-permute-done.5.refs_2_), channel_id=1, source_target_pairs={{0,4},{4,8},{8,12},{12,0},{1,5},{5,9},{9,13},{13,1},{2,6},{6,10},{... | collective-permute-start | bytes 1376264 | tf_op jit(solution)/shard_map/ppermute | solution.py:26
  16.7 14.0 %collective-permute-start.10 = (bf16[896,256]{1,0:T(8,128)(2,1)}, bf16[896,256]{1,0:T(8,128)(2,1)}, u32[]{:S(2)}, u32[]{:S(2)}) collective-permute-start(bf16[896,256]{1,0:T(8,128)(2,1)} %collective-permute-done.5.refs_2_), channel_id=1, source_target_pairs={{0,12},{4,0},{8,4},{12,8},{1,13},{5,1},{9,5},{13,9},{2,14},{6,2},{... | collective-permute-start | bytes 1376264 | tf_op jit(solution)/shard_map/ppermute | solution.py:26
  30.7 5.6 %collective-permute-start.11 = (bf16[896,256]{1,0:T(8,128)(2,1)}, bf16[896,256]{1,0:T(8,128)(2,1)S(1)}, u32[]{:S(2)}, u32[]{:S(2)}) collective-permute-start(bf16[896,256]{1,0:T(8,128)(2,1)} %collective-permute-done.10.refs_2_.refs_6_), channel_id=1, source_target_pairs={{0,1},{1,0},{2,3},{3,2},{4,5},{5,4},{6,7},{7,6},{8,9},{9,8},{10,11... | collective-permute-start | bytes 1376264 | tf_op jit(solution)/shard_map/ppermute | solution.py:26
  30.7 5.6 %collective-permute-start.13 = (bf16[896,256]{1,0:T(8,128)(2,1)}, bf16[896,256]{1,0:T(8,128)(2,1)S(1)}, u32[]{:S(2)}, u32[]{:S(2)}) collective-permute-start(bf16[896,256]{1,0:T(8,128)(2,1)} %collective-permute-done.12.refs_6_.refs_10_), channel_id=1, source_target_pairs={{0,1},{1,0},{2,3},{3,2},{4,5},{5,4},{6,7},{7,6},{8,9},{9,8},{10,11... | collective-permute-start | bytes 1376264 | tf_op jit(solution)/shard_map/ppermute | solution.py:26
  31.2 15.0 %collective-permute-start.7 = (bf16[768,256]{1,0:T(8,128)(2,1)}, bf16[768,256]{1,0:T(8,128)(2,1)S(1)}, u32[]{:S(2)}, u32[]{:S(2)}) collective-permute-start(bf16[768,256]{1,0:T(8,128)(2,1)} %get-tuple-element.52), channel_id=1, source_target_pairs={{0,16},{16,32},{32,48},{48,0},{1,17},{17,33},{33,49},{49,1},{2,18}... | collective-permute-start | bytes 1179656 | tf_op jit(solution)/shard_map/ppermute | solution.py:26
  32.7 17.5 %collective-permute-start.8 = (bf16[768,256]{1,0:T(8,128)(2,1)}, bf16[768,256]{1,0:T(8,128)(2,1)S(1)}, u32[]{:S(2)}, u32[]{:S(2)}) collective-permute-start(bf16[768,256]{1,0:T(8,128)(2,1)} %get-tuple-element.53), channel_id=1, source_target_pairs={{0,48},{16,0},{32,16},{48,32},{1,49},{17,1},{33,17},{49,33},{2,50}... | collective-permute-start | bytes 1179656 | tf_op jit(solution)/shard_map/ppermute | solution.py:26
  34.4 19.8 %collective-permute-start.9 = (bf16[768,256]{1,0:T(8,128)(2,1)}, bf16[768,256]{1,0:T(8,128)(2,1)S(1)}, u32[]{:S(2)}, u32[]{:S(2)}) collective-permute-start(bf16[768,256]{1,0:T(8,128)(2,1)} %get-tuple-element.54), channel_id=1, source_target_pairs={{0,32},{16,48},{32,0},{48,16},{1,33},{17,49},{33,1},{49,17},{2,34}... | collective-permute-start | bytes 1179656 | tf_op jit(solution)/shard_map/ppermute | solution.py:26
  36.2 9.9 %copy-start.7 = (bf16[896,256]{1,0:T(8,128)(2,1)}, bf16[896,256]{1,0:T(8,128)(2,1)S(1)}, u32[]{:S(2)}) copy-start(bf16[896,256]{1,0:T(8,128)(2,1)S(1)} %collective-permute-done.11.refs_3_.refs_7_) | copy-start | bytes 1376260
  36.3 9.9 %copy-start.8 = (bf16[896,256]{1,0:T(8,128)(2,1)}, bf16[896,256]{1,0:T(8,128)(2,1)S(1)}, u32[]{:S(2)}) copy-start(bf16[896,256]{1,0:T(8,128)(2,1)S(1)} %collective-permute-done.13.refs_7_.refs_11_) | copy-start | bytes 1376260
  36.3 18.6 %collective-permute-start.17 = (bf16[896,256]{1,0:T(8,128)(2,1)S(1)}, bf16[896,256]{1,0:T(8,128)(2,1)}, u32[]{:S(2)}, u32[]{:S(2)}) collective-permute-start(bf16[896,256]{1,0:T(8,128)(2,1)S(1)} %collective-permute-done.refs_0_.refs_4_), channel_id=1, source_target_pairs={{0,12},{4,0},{8,4},{12,8},{1,13},{5,1},{9,5},{13,9},{2,14},{6,2},{... | collective-permute-start | bytes 1376264 | tf_op jit(solution)/shard_map/ppermute | solution.py:26
  39.3 15.6 %collective-permute-start.19 = (bf16[896,256]{1,0:T(8,128)(2,1)}, bf16[896,256]{1,0:T(8,128)(2,1)}, u32[]{:S(2)}, u32[]{:S(2)}) collective-permute-start(bf16[896,256]{1,0:T(8,128)(2,1)} %collective-permute-done.12.refs_6_.refs_10_), channel_id=1, source_target_pairs={{0,4},{4,8},{8,12},{12,0},{1,5},{5,9},{9,13},{13,1},{2,6},{6,10},{... | collective-permute-start | bytes 1376264 | tf_op jit(solution)/shard_map/ppermute | solution.py:26
  46.2 10.1 %copy-start.11 = (bf16[768,256]{1,0:T(8,128)(2,1)}, bf16[768,256]{1,0:T(8,128)(2,1)S(1)}, u32[]{:S(2)}) copy-start(bf16[768,256]{1,0:T(8,128)(2,1)S(1)} %collective-permute-done.7.refs_1_) | copy-start | bytes 1179652
  46.2 26.7 %collective-permute-start.14 = (bf16[768,512]{1,0:T(8,128)(2,1)}, bf16[768,512]{1,0:T(8,128)(2,1)}, u32[]{:S(2)}, u32[]{:S(2)}) collective-permute-start(bf16[768,512]{1,0:T(8,128)(2,1)} %get-tuple-element.59), channel_id=1, source_target_pairs={{0,16},{16,32},{32,48},{48,0},{1,17},{17,33},{33,49},{49,1},{2,18}... | collective-permute-start | bytes 2359304 | tf_op jit(solution)/shard_map/ppermute | solution.py:26
  50.2 4.7 %copy-start.12 = (bf16[768,256]{1,0:T(8,128)(2,1)}, bf16[768,256]{1,0:T(8,128)(2,1)S(1)}, u32[]{:S(2)}) copy-start(bf16[768,256]{1,0:T(8,128)(2,1)S(1)} %collective-permute-done.8.refs_2_) | copy-start | bytes 1179652
  50.2 24.8 %collective-permute-start.15 = (bf16[768,512]{1,0:T(8,128)(2,1)}, bf16[768,512]{1,0:T(8,128)(2,1)}, u32[]{:S(2)}, u32[]{:S(2)}) collective-permute-start(bf16[768,512]{1,0:T(8,128)(2,1)} %get-tuple-element.60), channel_id=1, source_target_pairs={{0,48},{16,0},{32,16},{48,32},{1,49},{17,1},{33,17},{49,33},{2,50}... | collective-permute-start | bytes 2359304 | tf_op jit(solution)/shard_map/ppermute | solution.py:26
  54.2 33.7 %collective-permute-start.16 = (bf16[768,512]{1,0:T(8,128)(2,1)}, bf16[768,512]{1,0:T(8,128)(2,1)}, u32[]{:S(2)}, u32[]{:S(2)}) collective-permute-start(bf16[768,512]{1,0:T(8,128)(2,1)} %get-tuple-element.61), channel_id=1, source_target_pairs={{0,32},{16,48},{32,0},{48,16},{1,33},{17,49},{33,1},{49,17},{2,34}... | collective-permute-start | bytes 2359304 | tf_op jit(solution)/shard_map/ppermute | solution.py:26
  54.9 10.0 %collective-permute-start.18 = (bf16[896,256]{1,0:T(8,128)(2,1)}, bf16[896,256]{1,0:T(8,128)(2,1)S(1)}, u32[]{:S(2)}, u32[]{:S(2)}) collective-permute-start(bf16[896,256]{1,0:T(8,128)(2,1)} %collective-permute-done.17.refs_0_.refs_12_), channel_id=1, source_target_pairs={{0,1},{1,0},{2,3},{3,2},{4,5},{5,4},{6,7},{7,6},{8,9},{9,8},{10,11... | collective-permute-start | bytes 1376264 | tf_op jit(solution)/shard_map/ppermute | solution.py:26
  55.0 9.9 %collective-permute-start.20 = (bf16[896,256]{1,0:T(8,128)(2,1)}, bf16[896,256]{1,0:T(8,128)(2,1)S(1)}, u32[]{:S(2)}, u32[]{:S(2)}) collective-permute-start(bf16[896,256]{1,0:T(8,128)(2,1)} %collective-permute-done.19.refs_2_.refs_14_), channel_id=1, source_target_pairs={{0,1},{1,0},{2,3},{3,2},{4,5},{5,4},{6,7},{7,6},{8,9},{9,8},{10,11... | collective-permute-start | bytes 1376264 | tf_op jit(solution)/shard_map/ppermute | solution.py:26
  56.2 36.3 %all-to-all-start.1 = ((bf16[4,32,768]{2,1,0:T(8,128)(2,1)}), bf16[4,32,768]{2,1,0:T(8,128)(2,1)S(1)}, u32[]{:S(2)}, u32[]{:S(2)}) async-start(bf16[4,32,768]{2,1,0:T(8,128)(2,1)} %low_sum.1), calls=%async_computation.1 | async-start | bytes 393216 | tf_op jit(solution)/shard_map/all_to_all | solution.py:30
  64.9 23.0 %copy-start.9 = (bf16[896,256]{1,0:T(8,128)(2,1)}, bf16[896,256]{1,0:T(8,128)(2,1)S(1)}, u32[]{:S(2)}) copy-start(bf16[896,256]{1,0:T(8,128)(2,1)S(1)} %collective-permute-done.18.refs_1_.refs_13_) | copy-start | bytes 1376260
  64.9 23.0 %copy-start.10 = (bf16[896,256]{1,0:T(8,128)(2,1)}, bf16[896,256]{1,0:T(8,128)(2,1)S(1)}, u32[]{:S(2)}) copy-start(bf16[896,256]{1,0:T(8,128)(2,1)S(1)} %collective-permute-done.20.refs_3_.refs_15_) | copy-start | bytes 1376260
  69.5 26.6 %collective-permute-start.21 = (bf16[384,256]{1,0:T(8,128)(2,1)}, bf16[384,256]{1,0:T(8,128)(2,1)S(1)}, u32[]{:S(2)}, u32[]{:S(2)}) collective-permute-start(bf16[384,256]{1,0:T(8,128)(2,1)} %get-tuple-element.68), channel_id=1, source_target_pairs={{0,16},{16,32},{32,48},{48,0},{1,17},{17,33},{33,49},{49,1},{2,18}... | collective-permute-start | bytes 589832 | tf_op jit(solution)/shard_map/ppermute | solution.py:26
  70.7 38.2 %collective-permute-start.22 = (bf16[384,256]{1,0:T(8,128)(2,1)}, bf16[384,256]{1,0:T(8,128)(2,1)S(1)}, u32[]{:S(2)}, u32[]{:S(2)}) collective-permute-start(bf16[384,256]{1,0:T(8,128)(2,1)} %get-tuple-element.69), channel_id=1, source_target_pairs={{0,48},{16,0},{32,16},{48,32},{1,49},{17,1},{33,17},{49,33},{2,50}... | collective-permute-start | bytes 589832 | tf_op jit(solution)/shard_map/ppermute | solution.py:26
  72.9 36.1 %collective-permute-start.23 = (bf16[384,256]{1,0:T(8,128)(2,1)}, bf16[384,256]{1,0:T(8,128)(2,1)}, u32[]{:S(2)}, u32[]{:S(2)}) collective-permute-start(bf16[384,256]{1,0:T(8,128)(2,1)} %get-tuple-element.70), channel_id=1, source_target_pairs={{0,32},{16,48},{32,0},{48,16},{1,33},{17,49},{33,1},{49,17},{2,34}... | collective-permute-start | bytes 589832 | tf_op jit(solution)/shard_map/ppermute | solution.py:26
  92.6 16.4 %collective-permute-start.24 = (bf16[384,256]{1,0:T(8,128)(2,1)}, bf16[384,256]{1,0:T(8,128)(2,1)S(1)}, u32[]{:S(2)}, u32[]{:S(2)}) collective-permute-start(bf16[384,256]{1,0:T(8,128)(2,1)} %get-tuple-element.73), channel_id=1, source_target_pairs={{0,16},{16,32},{32,48},{48,0},{1,17},{17,33},{33,49},{49,1},{2,18}... | collective-permute-start | bytes 589832 | tf_op jit(solution)/shard_map/ppermute | solution.py:26
  95.9 13.1 %collective-permute-start.25 = (bf16[384,256]{1,0:T(8,128)(2,1)}, bf16[384,256]{1,0:T(8,128)(2,1)S(1)}, u32[]{:S(2)}, u32[]{:S(2)}) collective-permute-start(bf16[384,256]{1,0:T(8,128)(2,1)} %get-tuple-element.74), channel_id=1, source_target_pairs={{0,48},{16,0},{32,16},{48,32},{1,49},{17,1},{33,17},{49,33},{2,50}... | collective-permute-start | bytes 589832 | tf_op jit(solution)/shard_map/ppermute | solution.py:26
  96.1 7.0 %copy-start.14 = (bf16[384,256]{1,0:T(8,128)(2,1)}, bf16[384,256]{1,0:T(8,128)(2,1)S(1)}, u32[]{:S(2)}) copy-start(bf16[384,256]{1,0:T(8,128)(2,1)S(1)} %collective-permute-done.21.refs_9_) | copy-start | bytes 589828
  96.1 12.9 %collective-permute-start.26 = (bf16[384,256]{1,0:T(8,128)(2,1)}, bf16[384,256]{1,0:T(8,128)(2,1)S(1)}, u32[]{:S(2)}, u32[]{:S(2)}) collective-permute-start(bf16[384,256]{1,0:T(8,128)(2,1)} %get-tuple-element.75), channel_id=1, source_target_pairs={{0,32},{16,48},{32,0},{48,16},{1,33},{17,49},{33,1},{49,17},{2,34}... | collective-permute-start | bytes 589832 | tf_op jit(solution)/shard_map/ppermute | solution.py:26
  103.0 23.5 %all-to-all-start.2 = ((f32[16,32,256]{2,1,0:T(8,128)}), f32[16,32,256]{2,1,0:T(8,128)S(1)}, u32[]{:S(2)}, u32[]{:S(2)}) async-start(f32[16,32,256]{2,1,0:T(8,128)} %grad_partial.1), calls=%async_computation.2 | async-start | bytes 1048576 | tf_op jit(solution)/shard_map/all_to_all | solution.py:30
  109.8 16.7 %copy-start.2 = (f32[32,256]{1,0:T(8,128)S(1)}, f32[32,256]{1,0:T(8,128)}, u32[]{:S(2)}) copy-start(f32[32,256]{1,0:T(8,128)} %first.1) | copy-start | bytes 98308
  109.8 16.7 %copy-start.3 = (f32[32,256]{1,0:T(8,128)S(1)}, f32[32,256]{1,0:T(8,128)}, u32[]{:S(2)}) copy-start(f32[32,256]{1,0:T(8,128)} %second.1) | copy-start | bytes 98308
  115.7 44.7 %collective-permute-start.27 = (bf16[768,256]{1,0:T(8,128)(2,1)}, bf16[768,256]{1,0:T(8,128)(2,1)S(1)}, u32[]{:S(2)}, u32[]{:S(2)}) collective-permute-start(bf16[768,256]{1,0:T(8,128)(2,1)} %get-tuple-element.77), channel_id=1, source_target_pairs={{0,64},{64,128},{128,192},{192,0},{1,65},{65,129},{129,193},{193,1... | collective-permute-start | bytes 1179656 | tf_op jit(solution)/shard_map/ppermute | solution.py:26
  119.0 41.4 %collective-permute-start.28 = (bf16[768,256]{1,0:T(8,128)(2,1)}, bf16[768,256]{1,0:T(8,128)(2,1)S(1)}, u32[]{:S(2)}, u32[]{:S(2)}) collective-permute-start(bf16[768,256]{1,0:T(8,128)(2,1)} %get-tuple-element.78), channel_id=1, source_target_pairs={{0,192},{64,0},{128,64},{192,128},{1,193},{65,1},{129,65},{193,129... | collective-permute-start | bytes 1179656 | tf_op jit(solution)/shard_map/ppermute | solution.py:26
  121.6 40.3 %collective-permute-start.29 = (bf16[768,256]{1,0:T(8,128)(2,1)}, bf16[768,256]{1,0:T(8,128)(2,1)S(1)}, u32[]{:S(2)}, u32[]{:S(2)}) collective-permute-start(bf16[768,256]{1,0:T(8,128)(2,1)} %get-tuple-element.79), channel_id=1, source_target_pairs={{0,128},{64,192},{128,0},{192,64},{1,129},{65,193},{129,1},{193,65... | collective-permute-start | bytes 1179656 | tf_op jit(solution)/shard_map/ppermute | solution.py:26
  127.3 38.4 %all-to-all-start.3 = ((bf16[16,32,256]{2,1,0:T(8,128)(2,1)}), bf16[16,32,256]{2,1,0:T(8,128)(2,1)S(1)}, u32[]{:S(2)}, u32[]{:S(2)}) async-start(bf16[16,32,256]{2,1,0:T(8,128)(2,1)} %get-tuple-element.85), calls=%async_computation.3 | async-start | bytes 524288 | tf_op jit(solution)/shard_map/all_to_all | solution.py:30
  131.7 30.1 %copy-start.1 = (bf16[768,256]{1,0:T(8,128)(2,1)S(1)}, bf16[768,256]{1,0:T(8,128)(2,1)}, u32[]{:S(2)}) copy-start(bf16[768,256]{1,0:T(8,128)(2,1)} %get-tuple-element.76.a) | copy-start | bytes 1179652
  (5 other events, 3.8 us)
where the time goes:
time: 169 us; the launch traced here: 167 us
  starting transfers between devices  67.4 us (40%)
  Pallas kernels  48.4 us (29%)
  waiting for transfers between devices  44.5 us (26%)
  local copies, waits for them, and re-layouts  2.99 us (2%)
  matrix products  2.84 us (2%)
    ppermute x30, starting transfers between devices, shift(): return lax.ppermute(array, axis, [(i, (i + by) % n) for i in range(n)])  45.2 us
    ppermute x30, waiting for transfers between devices, shift(): return lax.ppermute(array, axis, [(i, (i + by) % n) for i in range(n)])  37.5 us
    pallas_call x4, Pallas kernels, partials(): pl.pallas_call(functools.partial(partial_kernel, m, start), out_shape=[pl...  22.8 us
    all_to_all x4, starting transfers between devices, swap(): return lax.all_to_all(array, axes, 0, 0, tiled=True)  22.2 us
    pallas_call x1, Pallas kernels, act(): pl.pallas_call(act_kernel, out_shape=jax.ShapeDtypeStruct((tokens, full),...  12.2 us
    all_to_all x4, waiting for transfers between devices, swap(): return lax.all_to_all(array, axes, 0, 0, tiled=True)  7.04 us
    pallas_call x1, Pallas kernels, regroup(): pl.pallas_call(functools.partial(regroup_kernel, [offs for _, offs in gro...  5.89 us
    pallas_call x1, Pallas kernels, grad_partial(): pl.pallas_call(grad_kernel, out_shape=pltpu.HBM((features // W, ranks, W)...  5.02 us
  transfers between devices with their start and end apart: 34, of which 9 were waited for; matrix products, arithmetic and copies ran while one was open for 2% of the time, Pallas kernels for 29%

commit v1 on v0

--- a/solution.py
+++ b/solution.py
@@ -353,15 +353,16 @@
     low_z = swap(low_sum(after(low_x, *part1)), "zh")
     part2 = partials(after(hidden, *part1), [slots[2]], slot_of, 0, half)
     sum2 = spread(part2, "x")
-    part3 = partials(after(hidden, *sum1[1:], *part2), [slots[2]], slot_of, half, half)
+    grad_part = grad_partial(after(low_z, *part2), cotangent)
+    grad_all = swap(grad_part, FSDP)
+    part3 = partials(after(hidden, grad_part, *sum1[1:], *part2), [slots[2]], slot_of, half, half)
     sum3 = spread(part3, "x")
 
-    grad_all = swap(grad_partial(after(low_z, *part2), cotangent), FSDP)
     new_first, new_second, normed = moments(grad_all, first_moment, second_moment)
     normed_all = swap(normed, DP)
 
     order = jnp.stack([(y + off) % 4 for off in slots] + dest).astype(jnp.int32)
-    zparts = regroup([(sum0, (0,)), (sum1, (1, 3)), (sum2, (2,)), (sum3, (2,))], place)
+    zparts = regroup([(sum0, (0,)), (sum1, (1, 3)), (sum2, (2,)), (sum3, (2,))], after(place, normed))
     act_grad = act(after(cotangent, *zparts), [[in_hbm(w) for w in four] for four in slots.values()], order)
     normed_all = after(normed_all, *zparts).reshape(-1, W)
     update = jnp.dot(basis, normed_all, preferred_element_type=F32).astype(BF)

time: 169 us -> 159 us (0.941)
  waiting for transfers between devices: 44.5 us -> 35.5 us
    ppermute x30, waiting for transfers between devices: 37.5 us -> 29.2 us  [shift(): return lax.ppermute(array, axis, [(i, (i + by) % n) for i in range(n)])]
    all_to_all x4, starting transfers between devices: 22.2 us -> 26.2 us  [swap(): return lax.all_to_all(array, axes, 0, 0, tiled=True)]
    ppermute x30, starting transfers between devices: 45.2 us -> 41.5 us  [shift(): return lax.ppermute(array, axis, [(i, (i + by) % n) for i in range(n)])]
  transfers between devices with their start and end apart: 34 -> 34, of which waited for: 9 -> 9; matrix products, arithmetic and copies ran while one was open for 2% -> 2% of each run, Pallas kernels for 29% -> 31%
where the time goes in v1:
time: 159 us; the launch traced here: 158 us
  starting transfers between devices  67.7 us (43%)
  Pallas kernels  48.3 us (30%)
  waiting for transfers between devices  35.5 us (22%)
  local copies, waits for them, and re-layouts  2.88 us (2%)
  matrix products  2.84 us (2%)
    ppermute x30, starting transfers between devices, shift(): return lax.ppermute(array, axis, [(i, (i + by) % n) for i in range(n)])  41.5 us
    ppermute x30, waiting for transfers between devices, shift(): return lax.ppermute(array, axis, [(i, (i + by) % n) for i in range(n)])  29.2 us
    all_to_all x4, starting transfers between devices, swap(): return lax.all_to_all(array, axes, 0, 0, tiled=True)  26.2 us
    pallas_call x4, Pallas kernels, partials(): pl.pallas_call(functools.partial(partial_kernel, m, start), out_shape=[pl...  22.7 us
    pallas_call x1, Pallas kernels, act(): pl.pallas_call(act_kernel, out_shape=jax.ShapeDtypeStruct((tokens, full),...  12.2 us
    all_to_all x4, waiting for transfers between devices, swap(): return lax.all_to_all(array, axes, 0, 0, tiled=True)  6.3 us
    pallas_call x1, Pallas kernels, regroup(): pl.pallas_call(functools.partial(regroup_kernel, [offs for _, offs in gro...  5.89 us
    pallas_call x1, Pallas kernels, grad_partial(): pl.pallas_call(grad_kernel, out_shape=pltpu.HBM((features // W, ranks, W)...  5.04 us
  transfers between devices with their start and end apart: 34, of which 9 were waited for; matrix products, arithmetic and copies ran while one was open for 2% of the time, Pallas kernels for 31%

profile of v1, /device:TPU:32, one launch (start us, length us, event | category | flops | bytes accessed | tf_op | source)
XLA Modules:
  0.0 158.4 jit_solution(5247368662013448916)
XLA Ops:
  0.6 1.7 %collective-permute-start.2 = (bf16[896,256]{1,0:T(8,128)(2,1)}, bf16[896,256]{1,0:T(8,128)(2,1)S(1)}, u32[]{:S(2)}, u32[]{:S(2)}) collective-permute-start(bf16[896,256]{1,0:T(8,128)(2,1)} %refs_0_.3), channel_id=1, source_target_pairs={{0,4},{4,8},{8,12},{12,0},{1,5},{5,9},{9,13},{13,1},{2,6},{6,10},{... | collective-permute-start | bytes 1376264 | tf_op jit(solution)/shard_map/ppermute | solution.py:26
  2.3 1.7 %collective-permute-start = (bf16[896,256]{1,0:T(8,128)(2,1)}, bf16[896,256]{1,0:T(8,128)(2,1)S(1)}, u32[]{:S(2)}, u32[]{:S(2)}) collective-permute-start(bf16[896,256]{1,0:T(8,128)(2,1)} %refs_0_.3), channel_id=1, source_target_pairs={{0,12},{4,0},{8,4},{12,8},{1,13},{5,1},{9,5},{13,9},{2,14},{6,2},{... | collective-permute-start | bytes 1376264 | tf_op jit(solution)/shard_map/ppermute | solution.py:26
  4.0 1.8 %collective-permute-start.5 = (bf16[896,256]{1,0:T(8,128)(2,1)}, bf16[896,256]{1,0:T(8,128)(2,1)S(1)}, u32[]{:S(2)}, u32[]{:S(2)}) collective-permute-start(bf16[896,256]{1,0:T(8,128)(2,1)} %refs_0_.3), channel_id=1, source_target_pairs={{0,2},{2,0},{1,3},{3,1},{4,6},{6,4},{5,7},{7,5},{8,10},{10,8},{9,1... | collective-permute-start | bytes 1376264 | tf_op jit(solution)/shard_map/ppermute | solution.py:26
  5.8 2.4 %convolution_convert_fusion = bf16[512,768]{1,0:T(8,128)(2,1)S(1)} fusion(bf16[896,512]{1,0:T(8,128)(2,1)S(1)} %copy-done, bf16[768,896]{1,0:T(8,128)(2,1)} %h_ref.3), kind=kOutput, calls=%fused_computation | convolution fusion | flops 705036288 | bytes 3080192 | tf_op jit(solution)/shard_map/dot_general | solution.py:321
  8.2 0.9 copy.15
  9.1 3.5 %all-to-all-start = ((bf16[4,4,32,768]{3,2,1,0:T(8,128)(2,1)}), bf16[4,4,32,768]{3,2,1,0:T(8,128)(2,1)S(1)}, u32[]{:S(2)}, u32[]{:S(2)}) async-start(bf16[4,4,32,768]{3,2,1,0:T(8,128)(2,1)} %bitcast.27), calls=%async_computation | async-start | bytes 1572864 | tf_op jit(solution)/shard_map/all_to_all | solution.py:30
  12.7 1.7 %collective-permute-done.2.refs_4_.refs_8_ = bf16[896,256]{1,0:T(8,128)(2,1)S(1)} collective-permute-done((bf16[896,256]{1,0:T(8,128)(2,1)}, bf16[896,256]{1,0:T(8,128)(2,1)S(1)}, u32[]{:S(2)}, u32[]{:S(2)}) %collective-permute-start.2) | collective-permute-done | bytes 458784 | tf_op jit(solution)/shard_map/ppermute | solution.py:26
  14.6 0.5 collective-permute-start.3
  15.1 0.9 collective-permute-done.5.refs_2_
  16.1 0.7 collective-permute-start.9
  16.9 2.6 %collective-permute-start.7 = (bf16[896,256]{1,0:T(8,128)(2,1)S(1)}, bf16[896,256]{1,0:T(8,128)(2,1)}, u32[]{:S(2)}, u32[]{:S(2)}) collective-permute-start(bf16[896,256]{1,0:T(8,128)(2,1)S(1)} %collective-permute-done.5.refs_2_), channel_id=1, source_target_pairs={{0,12},{4,0},{8,4},{12,8},{1,13},{5,1},{9,5},{13,9},{2,14},{6,2},{... | collective-permute-start | bytes 1376264 | tf_op jit(solution)/shard_map/ppermute | solution.py:26
  19.5 4.0 %all-to-all-done.parts = bf16[4,4,32,768]{3,2,1,0:T(8,128)(2,1)S(1)} async-done(((bf16[4,4,32,768]{3,2,1,0:T(8,128)(2,1)}), bf16[4,4,32,768]{3,2,1,0:T(8,128)(2,1)S(1)}, u32[]{:S(2)}, u32[]{:S(2)}) %all-to-all-start) | async-done | bytes 786464 | tf_op jit(solution)/shard_map/all_to_all | solution.py:30
  23.5 6.7 %partials.4 = (bf16[768,256]{1,0:T(8,128)(2,1)}, bf16[768,256]{1,0:T(8,128)(2,1)}, bf16[768,256]{1,0:T(8,128)(2,1)}, bf16[768,256]{1,0:T(8,128)(2,1)}) custom-call(s32[4]{0:T(128)S(1)} %pad_add_fusion.1.slot_of, bf16[768,896]{1,0:T(8,128)(2,1)} %h_ref.3, bf16[896,256]{1,0:T(8,128)(2,1)S(1)} %copy-done.4, bf16[896,256]{1,0:T(8,128)(2,1)} %collective-permute-done.4.refs_1_, ...), custom_call_target="tpu_custom_call" | custom-call | flops 8589934592 | bytes 33554432 | tf_op jit(solution)/shard_map/partials/pallas_call | solution.py:82
  30.4 0.5 collective-permute-start.10
  30.9 1.5 collective-permute-start.12
  32.4 2.7 %collective-permute-start.14 = (bf16[768,256]{1,0:T(8,128)(2,1)}, bf16[768,256]{1,0:T(8,128)(2,1)S(1)}, u32[]{:S(2)}, u32[]{:S(2)}) collective-permute-start(bf16[768,256]{1,0:T(8,128)(2,1)} %get-tuple-element.53), channel_id=1, source_target_pairs={{0,32},{16,48},{32,0},{48,16},{1,33},{17,49},{33,1},{49,17},{2,34}... | collective-permute-start | bytes 1179656 | tf_op jit(solution)/shard_map/ppermute | solution.py:26
  35.1 1.4 collective-permute-start.13
  36.6 3.0 %collective-permute-start.11 = (bf16[896,256]{1,0:T(8,128)(2,1)S(1)}, bf16[896,256]{1,0:T(8,128)(2,1)}, u32[]{:S(2)}, u32[]{:S(2)}) collective-permute-start(bf16[896,256]{1,0:T(8,128)(2,1)S(1)} %collective-permute-done.refs_0_.refs_4_), channel_id=1, source_target_pairs={{0,12},{4,0},{8,4},{12,8},{1,13},{5,1},{9,5},{13,9},{2,14},{6,2},{... | collective-permute-start | bytes 1376264 | tf_op jit(solution)/shard_map/ppermute | solution.py:26
  39.6 6.8 %partials.5 = (bf16[768,512]{1,0:T(8,128)(2,1)}, bf16[768,512]{1,0:T(8,128)(2,1)}, bf16[768,512]{1,0:T(8,128)(2,1)}, bf16[768,512]{1,0:T(8,128)(2,1)}) custom-call(s32[4]{0:T(128)S(1)} %pad_add_fusion.1.slot_of, bf16[768,896]{1,0:T(8,128)(2,1)} %h_ref.3, bf16[896,256]{1,0:T(8,128)(2,1)S(1)} %collective-permute-done.refs_0_.refs_4_, ...), custom_call_target="tpu_custom_call" | custom-call | flops 8589934592 | bytes 33554432 | tf_op jit(solution)/shard_map/partials/pallas_call | solution.py:82
  46.5 0.7 collective-permute-start.18
  47.2 6.6 %collective-permute-done.14.refs_3_ = bf16[768,256]{1,0:T(8,128)(2,1)S(1)} collective-permute-done((bf16[768,256]{1,0:T(8,128)(2,1)}, bf16[768,256]{1,0:T(8,128)(2,1)S(1)}, u32[]{:S(2)}, u32[]{:S(2)}) %collective-permute-start.14) | collective-permute-done | bytes 393248 | tf_op jit(solution)/shard_map/ppermute | solution.py:26
  53.7 0.8 collective-permute-start.20
  54.5 1.7 %collective-permute-start.19 = (bf16[768,512]{1,0:T(8,128)(2,1)}, bf16[768,512]{1,0:T(8,128)(2,1)}, u32[]{:S(2)}, u32[]{:S(2)}) collective-permute-start(bf16[768,512]{1,0:T(8,128)(2,1)} %get-tuple-element.61), channel_id=1, source_target_pairs={{0,48},{16,0},{32,16},{48,32},{1,49},{17,1},{33,17},{49,33},{2,50}... | collective-permute-start | bytes 2359304 | tf_op jit(solution)/shard_map/ppermute | solution.py:26
  56.3 0.6 collective-permute-start.17
  56.8 0.8 low_sum.1
  57.6 8.2 %all-to-all-start.1 = ((bf16[4,32,768]{2,1,0:T(8,128)(2,1)}), bf16[4,32,768]{2,1,0:T(8,128)(2,1)S(1)}, u32[]{:S(2)}, u32[]{:S(2)}) async-start(bf16[4,32,768]{2,1,0:T(8,128)(2,1)} %low_sum.1), calls=%async_computation.1 | async-start | bytes 393216 | tf_op jit(solution)/shard_map/all_to_all | solution.py:30
  65.8 4.6 %partials.6 = (bf16[384,256]{1,0:T(8,128)(2,1)}, bf16[384,256]{1,0:T(8,128)(2,1)}, bf16[384,256]{1,0:T(8,128)(2,1)}, bf16[384,256]{1,0:T(8,128)(2,1)}) custom-call(s32[4]{0:T(128)S(1)} %pad_add_fusion.1.slot_of, bf16[768,896]{1,0:T(8,128)(2,1)} %h_ref.3, bf16[896,256]{1,0:T(8,128)(2,1)} %collective-permute-done.11.refs_0_.refs_12_, ...), custom_call_target="tpu_custom_call" | custom-call | flops 8589934592 | bytes 33554432 | tf_op jit(solution)/shard_map/partials/pallas_call | solution.py:82
  70.5 2.6 %collective-permute-start.23 = (bf16[384,256]{1,0:T(8,128)(2,1)}, bf16[384,256]{1,0:T(8,128)(2,1)}, u32[]{:S(2)}, u32[]{:S(2)}) collective-permute-start(bf16[384,256]{1,0:T(8,128)(2,1)} %get-tuple-element.70), channel_id=1, source_target_pairs={{0,32},{16,48},{32,0},{48,16},{1,33},{17,49},{33,1},{49,17},{2,34}... | collective-permute-start | bytes 589832 | tf_op jit(solution)/shard_map/ppermute | solution.py:26
  73.1 2.3 %all-to-all-done.1.low_ref = bf16[4,32,768]{2,1,0:T(8,128)(2,1)S(1)} async-done(((bf16[4,32,768]{2,1,0:T(8,128)(2,1)}), bf16[4,32,768]{2,1,0:T(8,128)(2,1)S(1)}, u32[]{:S(2)}, u32[]{:S(2)}) %all-to-all-start.1) | async-done | bytes 196640 | tf_op jit(solution)/shard_map/all_to_all | solution.py:30
  75.4 5.0 %grad_partial.1 = f32[16,32,256]{2,1,0:T(8,128)} custom-call(bf16[4,32,768]{2,1,0:T(8,128)(2,1)S(1)} %all-to-all-done.1.low_ref, bf16[768,4096]{1,0:T(8,128)(2,1)} %cot_ref.2), custom_call_target="tpu_custom_call" | custom-call | flops 8589934592 | bytes 33554432 | tf_op jit(solution)/shard_map/grad_partial/pallas_call | solution.py:210
  80.5 5.1 %all-to-all-start.2 = ((f32[16,32,256]{2,1,0:T(8,128)}), f32[16,32,256]{2,1,0:T(8,128)S(1)}, u32[]{:S(2)}, u32[]{:S(2)}) async-start(f32[16,32,256]{2,1,0:T(8,128)} %grad_partial.1), calls=%async_computation.2 | async-start | bytes 1048576 | tf_op jit(solution)/shard_map/all_to_all | solution.py:30
  85.6 1.7 %collective-permute-start.22 = (bf16[384,256]{1,0:T(8,128)(2,1)}, bf16[384,256]{1,0:T(8,128)(2,1)}, u32[]{:S(2)}, u32[]{:S(2)}) collective-permute-start(bf16[384,256]{1,0:T(8,128)(2,1)} %get-tuple-element.71), channel_id=1, source_target_pairs={{0,48},{16,0},{32,16},{48,32},{1,49},{17,1},{33,17},{49,33},{2,50}... | collective-permute-start | bytes 589832 | tf_op jit(solution)/shard_map/ppermute | solution.py:26
  87.6 4.6 %partials.7 = (bf16[384,256]{1,0:T(8,128)(2,1)}, bf16[384,256]{1,0:T(8,128)(2,1)}, bf16[384,256]{1,0:T(8,128)(2,1)}, bf16[384,256]{1,0:T(8,128)(2,1)}) custom-call(s32[4]{0:T(128)S(1)} %pad_add_fusion.1.slot_of, bf16[768,896]{1,0:T(8,128)(2,1)} %h_ref.3, bf16[896,256]{1,0:T(8,128)(2,1)} %collective-permute-done.11.refs_0_.refs_12_, ...), custom_call_target="tpu_custom_call" | custom-call | flops 8589934592 | bytes 33554432 | tf_op jit(solution)/shard_map/partials/pallas_call | solution.py:82
  92.2 2.5 %collective-permute-start.24 = (bf16[384,256]{1,0:T(8,128)(2,1)}, bf16[384,256]{1,0:T(8,128)(2,1)S(1)}, u32[]{:S(2)}, u32[]{:S(2)}) collective-permute-start(bf16[384,256]{1,0:T(8,128)(2,1)} %get-tuple-element.78), channel_id=1, source_target_pairs={{0,16},{16,32},{32,48},{48,0},{1,17},{17,33},{33,49},{49,1},{2,18}... | collective-permute-start | bytes 589832 | tf_op jit(solution)/shard_map/ppermute | solution.py:26
  94.8 0.8 collective-permute-start.25
  95.6 1.7 %collective-permute-start.26 = (bf16[384,256]{1,0:T(8,128)(2,1)}, bf16[384,256]{1,0:T(8,128)(2,1)S(1)}, u32[]{:S(2)}, u32[]{:S(2)}) collective-permute-start(bf16[384,256]{1,0:T(8,128)(2,1)} %get-tuple-element.80), channel_id=1, source_target_pairs={{0,32},{16,48},{32,0},{48,16},{1,33},{17,49},{33,1},{49,17},{2,34}... | collective-permute-start | bytes 589832 | tf_op jit(solution)/shard_map/ppermute | solution.py:26
  97.4 0.8 moments.1
  98.2 9.5 %all-to-all-start.3 = ((bf16[16,32,256]{2,1,0:T(8,128)(2,1)}), bf16[16,32,256]{2,1,0:T(8,128)(2,1)S(1)}, u32[]{:S(2)}, u32[]{:S(2)}) async-start(bf16[16,32,256]{2,1,0:T(8,128)(2,1)} %get-tuple-element.74), calls=%async_computation.3 | async-start | bytes 524288 | tf_op jit(solution)/shard_map/all_to_all | solution.py:30
  107.8 0.6 copy-done.16
  108.6 5.9 %regroup.1 = (bf16[768,256]{1,0:T(8,128)(2,1)}, bf16[768,256]{1,0:T(8,128)(2,1)}, bf16[768,256]{1,0:T(8,128)(2,1)}, bf16[768,256]{1,0:T(8,128)(2,1)}) custom-call(s32[4]{0:T(128)S(1)} %pad_add_fusion.place, bf16[768,256]{1,0:T(8,128)(2,1)} %get-tuple-element.55.refs_0_, bf16[768,256]{1,0:T(8,128)(2,1)} %copy-done.12, bf16[768,256]{1,0:T(8,128)(2,1)} %copy-done.14, ...), custom_call_target="tpu_custom_call" | custom-call | flops 8589934592 | bytes 33554432 | tf_op jit(solution)/shard_map/regroup/pallas_call | solution.py:136
  114.4 2.9 %collective-permute-start.27 = (bf16[768,256]{1,0:T(8,128)(2,1)}, bf16[768,256]{1,0:T(8,128)(2,1)S(1)}, u32[]{:S(2)}, u32[]{:S(2)}) collective-permute-start(bf16[768,256]{1,0:T(8,128)(2,1)} %get-tuple-element.82), channel_id=1, source_target_pairs={{0,64},{64,128},{128,192},{192,0},{1,65},{65,129},{129,193},{193,1... | collective-permute-start | bytes 1179656 | tf_op jit(solution)/shard_map/ppermute | solution.py:26
  117.3 1.3 collective-permute-start.28
  118.7 5.8 %collective-permute-start.29 = (bf16[768,256]{1,0:T(8,128)(2,1)}, bf16[768,256]{1,0:T(8,128)(2,1)S(1)}, u32[]{:S(2)}, u32[]{:S(2)}) collective-permute-start(bf16[768,256]{1,0:T(8,128)(2,1)} %get-tuple-element.84), channel_id=1, source_target_pairs={{0,128},{64,192},{128,0},{192,64},{1,129},{65,193},{129,1},{193,65... | collective-permute-start | bytes 1179656 | tf_op jit(solution)/shard_map/ppermute | solution.py:26
  124.5 12.2 %act_grad.1 = bf16[768,896]{1,0:T(8,128)(2,1)} custom-call(s32[8]{0:T(128)S(1)} %stack.75.order, bf16[768,4096]{1,0:T(8,128)(2,1)} %cot_ref.2, bf16[896,256]{1,0:T(8,128)(2,1)} %refs_0_.3, bf16[896,256]{1,0:T(8,128)(2,1)} %collective-permute-done.4.refs_1_, bf16[896,256]{1,0:T(8,128)(2,1)} %copy-done.7, bf16[896,256]{1,0:T(8,128)(2,1)} %collective-permute-done.6.refs_3_, ...), custom_call_target="tpu_custom_call" | custom-call | flops 8589934592 | bytes 33554432 | tf_op jit(solution)/shard_map/act_grad/pallas_call | solution.py:294
  136.7 8.8 %collective-permute-done.27.b = bf16[768,256]{1,0:T(8,128)(2,1)S(1)} collective-permute-done((bf16[768,256]{1,0:T(8,128)(2,1)}, bf16[768,256]{1,0:T(8,128)(2,1)S(1)}, u32[]{:S(2)}, u32[]{:S(2)}) %collective-permute-start.27) | collective-permute-done | bytes 393248 | tf_op jit(solution)/shard_map/ppermute | solution.py:26
  145.5 10.5 %collective-permute-done.29.d = bf16[768,256]{1,0:T(8,128)(2,1)S(1)} collective-permute-done((bf16[768,256]{1,0:T(8,128)(2,1)}, bf16[768,256]{1,0:T(8,128)(2,1)S(1)}, u32[]{:S(2)}, u32[]{:S(2)}) %collective-permute-start.29) | collective-permute-done | bytes 393248 | tf_op jit(solution)/shard_map/ppermute | solution.py:26
  156.0 0.9 finish.1
  157.4 1.0 copy.13
  (75 shorter events, 1.8 us)
Async XLA Ops:
  0.6 5.2 %copy-start = (bf16[896,512]{1,0:T(8,128)(2,1)S(1)}, bf16[896,512]{1,0:T(8,128)(2,1)}, u32[]{:S(2)}) copy-start(bf16[896,512]{1,0:T(8,128)(2,1)} %param.9) | copy-start | bytes 2752516
  0.6 13.8 %collective-permute-start.2 = (bf16[896,256]{1,0:T(8,128)(2,1)}, bf16[896,256]{1,0:T(8,128)(2,1)S(1)}, u32[]{:S(2)}, u32[]{:S(2)}) collective-permute-start(bf16[896,256]{1,0:T(8,128)(2,1)} %refs_0_.3), channel_id=1, source_target_pairs={{0,4},{4,8},{8,12},{12,0},{1,5},{5,9},{9,13},{13,1},{2,6},{6,10},{... | collective-permute-start | bytes 1376264 | tf_op jit(solution)/shard_map/ppermute | solution.py:26
  2.3 12.2 %collective-permute-start = (bf16[896,256]{1,0:T(8,128)(2,1)}, bf16[896,256]{1,0:T(8,128)(2,1)S(1)}, u32[]{:S(2)}, u32[]{:S(2)}) collective-permute-start(bf16[896,256]{1,0:T(8,128)(2,1)} %refs_0_.3), channel_id=1, source_target_pairs={{0,12},{4,0},{8,4},{12,8},{1,13},{5,1},{9,5},{13,9},{2,14},{6,2},{... | collective-permute-start | bytes 1376264 | tf_op jit(solution)/shard_map/ppermute | solution.py:26
  4.0 12.1 %collective-permute-start.5 = (bf16[896,256]{1,0:T(8,128)(2,1)}, bf16[896,256]{1,0:T(8,128)(2,1)S(1)}, u32[]{:S(2)}, u32[]{:S(2)}) collective-permute-start(bf16[896,256]{1,0:T(8,128)(2,1)} %refs_0_.3), channel_id=1, source_target_pairs={{0,2},{2,0},{1,3},{3,1},{4,6},{6,4},{5,7},{7,5},{8,10},{10,8},{9,1... | collective-permute-start | bytes 1376264 | tf_op jit(solution)/shard_map/ppermute | solution.py:26
  8.2 4.5 %copy-start.4 = (bf16[896,256]{1,0:T(8,128)(2,1)S(1)}, bf16[896,256]{1,0:T(8,128)(2,1)}, u32[]{:S(2)}) copy-start(bf16[896,256]{1,0:T(8,128)(2,1)} %refs_0_.3) | copy-start | bytes 1376260
  9.1 14.3 %all-to-all-start = ((bf16[4,4,32,768]{3,2,1,0:T(8,128)(2,1)}), bf16[4,4,32,768]{3,2,1,0:T(8,128)(2,1)S(1)}, u32[]{:S(2)}, u32[]{:S(2)}) async-start(bf16[4,4,32,768]{3,2,1,0:T(8,128)(2,1)} %bitcast.27), calls=%async_computation | async-start | bytes 1572864 | tf_op jit(solution)/shard_map/all_to_all | solution.py:30
  12.6 10.8 %collective-permute-start.4 = (bf16[896,256]{1,0:T(8,128)(2,1)S(1)}, bf16[896,256]{1,0:T(8,128)(2,1)}, u32[]{:S(2)}, u32[]{:S(2)}) collective-permute-start(bf16[896,256]{1,0:T(8,128)(2,1)S(1)} %copy-done.4), channel_id=1, source_target_pairs={{0,1},{1,0},{2,3},{3,2},{4,5},{5,4},{6,7},{7,6},{8,9},{9,8},{10,11... | collective-permute-start | bytes 1376264 | tf_op jit(solution)/shard_map/ppermute | solution.py:26
  14.5 25.1 %copy-start.5 = (bf16[896,256]{1,0:T(8,128)(2,1)}, bf16[896,256]{1,0:T(8,128)(2,1)S(1)}, u32[]{:S(2)}) copy-start(bf16[896,256]{1,0:T(8,128)(2,1)S(1)} %collective-permute-done.2.refs_4_.refs_8_) | copy-start | bytes 1376260
  14.5 25.1 %copy-start.6 = (bf16[896,256]{1,0:T(8,128)(2,1)}, bf16[896,256]{1,0:T(8,128)(2,1)S(1)}, u32[]{:S(2)}) copy-start(bf16[896,256]{1,0:T(8,128)(2,1)S(1)} %collective-permute-done.refs_0_.refs_4_) | copy-start | bytes 1376260
  14.5 2.4 %collective-permute-start.1 = (bf16[896,256]{1,0:T(8,128)(2,1)S(1)}, bf16[896,256]{1,0:T(8,128)(2,1)}, u32[]{:S(2)}, u32[]{:S(2)}) collective-permute-start(bf16[896,256]{1,0:T(8,128)(2,1)S(1)} %collective-permute-done.refs_0_.refs_4_), channel_id=1, source_target_pairs={{0,1},{1,0},{2,3},{3,2},{4,5},{5,4},{6,7},{7,6},{8,9},{9,8},{10,11... | collective-permute-start | bytes 1376264 | tf_op jit(solution)/shard_map/ppermute | solution.py:26
  14.6 8.9 %collective-permute-start.3 = (bf16[896,256]{1,0:T(8,128)(2,1)S(1)}, bf16[896,256]{1,0:T(8,128)(2,1)}, u32[]{:S(2)}, u32[]{:S(2)}) collective-permute-start(bf16[896,256]{1,0:T(8,128)(2,1)S(1)} %collective-permute-done.2.refs_4_.refs_8_), channel_id=1, source_target_pairs={{0,1},{1,0},{2,3},{3,2},{4,5},{5,4},{6,7},{7,6},{8,9},{9,8},{10,11... | collective-permute-start | bytes 1376264 | tf_op jit(solution)/shard_map/ppermute | solution.py:26
  16.0 14.1 %copy-start.7 = (bf16[896,256]{1,0:T(8,128)(2,1)}, bf16[896,256]{1,0:T(8,128)(2,1)S(1)}, u32[]{:S(2)}) copy-start(bf16[896,256]{1,0:T(8,128)(2,1)S(1)} %collective-permute-done.5.refs_2_) | copy-start | bytes 1376260
  16.0 7.4 %collective-permute-start.6 = (bf16[896,256]{1,0:T(8,128)(2,1)S(1)}, bf16[896,256]{1,0:T(8,128)(2,1)}, u32[]{:S(2)}, u32[]{:S(2)}) collective-permute-start(bf16[896,256]{1,0:T(8,128)(2,1)S(1)} %collective-permute-done.5.refs_2_), channel_id=1, source_target_pairs={{0,1},{1,0},{2,3},{3,2},{4,5},{5,4},{6,7},{7,6},{8,9},{9,8},{10,11... | collective-permute-start | bytes 1376264 | tf_op jit(solution)/shard_map/ppermute | solution.py:26
  16.1 14.3 %collective-permute-start.9 = (bf16[896,256]{1,0:T(8,128)(2,1)S(1)}, bf16[896,256]{1,0:T(8,128)(2,1)}, u32[]{:S(2)}, u32[]{:S(2)}) collective-permute-start(bf16[896,256]{1,0:T(8,128)(2,1)S(1)} %collective-permute-done.5.refs_2_), channel_id=1, source_target_pairs={{0,4},{4,8},{8,12},{12,0},{1,5},{5,9},{9,13},{13,1},{2,6},{6,10},{... | collective-permute-start | bytes 1376264 | tf_op jit(solution)/shard_map/ppermute | solution.py:26
  16.9 13.5 %collective-permute-start.7 = (bf16[896,256]{1,0:T(8,128)(2,1)S(1)}, bf16[896,256]{1,0:T(8,128)(2,1)}, u32[]{:S(2)}, u32[]{:S(2)}) collective-permute-start(bf16[896,256]{1,0:T(8,128)(2,1)S(1)} %collective-permute-done.5.refs_2_), channel_id=1, source_target_pairs={{0,12},{4,0},{8,4},{12,8},{1,13},{5,1},{9,5},{13,9},{2,14},{6,2},{... | collective-permute-start | bytes 1376264 | tf_op jit(solution)/shard_map/ppermute | solution.py:26
  30.4 6.2 %collective-permute-start.8 = (bf16[896,256]{1,0:T(8,128)(2,1)}, bf16[896,256]{1,0:T(8,128)(2,1)S(1)}, u32[]{:S(2)}, u32[]{:S(2)}) collective-permute-start(bf16[896,256]{1,0:T(8,128)(2,1)} %collective-permute-done.7.refs_2_.refs_6_), channel_id=1, source_target_pairs={{0,1},{1,0},{2,3},{3,2},{4,5},{5,4},{6,7},{7,6},{8,9},{9,8},{10,11... | collective-permute-start | bytes 1376264 | tf_op jit(solution)/shard_map/ppermute | solution.py:26
  30.4 6.2 %collective-permute-start.10 = (bf16[896,256]{1,0:T(8,128)(2,1)}, bf16[896,256]{1,0:T(8,128)(2,1)S(1)}, u32[]{:S(2)}, u32[]{:S(2)}) collective-permute-start(bf16[896,256]{1,0:T(8,128)(2,1)} %collective-permute-done.9.refs_6_.refs_10_), channel_id=1, source_target_pairs={{0,1},{1,0},{2,3},{3,2},{4,5},{5,4},{6,7},{7,6},{8,9},{9,8},{10,11... | collective-permute-start | bytes 1376264 | tf_op jit(solution)/shard_map/ppermute | solution.py:26
  30.9 15.6 %collective-permute-start.12 = (bf16[768,256]{1,0:T(8,128)(2,1)}, bf16[768,256]{1,0:T(8,128)(2,1)S(1)}, u32[]{:S(2)}, u32[]{:S(2)}) collective-permute-start(bf16[768,256]{1,0:T(8,128)(2,1)} %get-tuple-element.52), channel_id=1, source_target_pairs={{0,16},{16,32},{32,48},{48,0},{1,17},{17,33},{33,49},{49,1},{2,18}... | collective-permute-start | bytes 1179656 | tf_op jit(solution)/shard_map/ppermute | solution.py:26
  32.4 21.4 %collective-permute-start.14 = (bf16[768,256]{1,0:T(8,128)(2,1)}, bf16[768,256]{1,0:T(8,128)(2,1)S(1)}, u32[]{:S(2)}, u32[]{:S(2)}) collective-permute-start(bf16[768,256]{1,0:T(8,128)(2,1)} %get-tuple-element.53), channel_id=1, source_target_pairs={{0,32},{16,48},{32,0},{48,16},{1,33},{17,49},{33,1},{49,17},{2,34}... | collective-permute-start | bytes 1179656 | tf_op jit(solution)/shard_map/ppermute | solution.py:26
  35.1 19.4 %collective-permute-start.13 = (bf16[768,256]{1,0:T(8,128)(2,1)}, bf16[768,256]{1,0:T(8,128)(2,1)S(1)}, u32[]{:S(2)}, u32[]{:S(2)}) collective-permute-start(bf16[768,256]{1,0:T(8,128)(2,1)} %get-tuple-element.54), channel_id=1, source_target_pairs={{0,48},{16,0},{32,16},{48,32},{1,49},{17,1},{33,17},{49,33},{2,50}... | collective-permute-start | bytes 1179656 | tf_op jit(solution)/shard_map/ppermute | solution.py:26
  36.5 9.9 %copy-start.8 = (bf16[896,256]{1,0:T(8,128)(2,1)}, bf16[896,256]{1,0:T(8,128)(2,1)S(1)}, u32[]{:S(2)}) copy-start(bf16[896,256]{1,0:T(8,128)(2,1)S(1)} %collective-permute-done.8.refs_3_.refs_7_) | copy-start | bytes 1376260
  36.5 9.9 %copy-start.9 = (bf16[896,256]{1,0:T(8,128)(2,1)}, bf16[896,256]{1,0:T(8,128)(2,1)S(1)}, u32[]{:S(2)}) copy-start(bf16[896,256]{1,0:T(8,128)(2,1)S(1)} %collective-permute-done.10.refs_7_.refs_11_) | copy-start | bytes 1376260
  36.6 19.7 %collective-permute-start.11 = (bf16[896,256]{1,0:T(8,128)(2,1)S(1)}, bf16[896,256]{1,0:T(8,128)(2,1)}, u32[]{:S(2)}, u32[]{:S(2)}) collective-permute-start(bf16[896,256]{1,0:T(8,128)(2,1)S(1)} %collective-permute-done.refs_0_.refs_4_), channel_id=1, source_target_pairs={{0,12},{4,0},{8,4},{12,8},{1,13},{5,1},{9,5},{13,9},{2,14},{6,2},{... | collective-permute-start | bytes 1376264 | tf_op jit(solution)/shard_map/ppermute | solution.py:26
  39.6 16.6 %collective-permute-start.16 = (bf16[896,256]{1,0:T(8,128)(2,1)}, bf16[896,256]{1,0:T(8,128)(2,1)}, u32[]{:S(2)}, u32[]{:S(2)}) collective-permute-start(bf16[896,256]{1,0:T(8,128)(2,1)} %collective-permute-done.9.refs_6_.refs_10_), channel_id=1, source_target_pairs={{0,4},{4,8},{8,12},{12,0},{1,5},{5,9},{9,13},{13,1},{2,6},{6,10},{... | collective-permute-start | bytes 1376264 | tf_op jit(solution)/shard_map/ppermute | solution.py:26
  46.5 9.7 %copy-start.12 = (bf16[768,256]{1,0:T(8,128)(2,1)}, bf16[768,256]{1,0:T(8,128)(2,1)S(1)}, u32[]{:S(2)}) copy-start(bf16[768,256]{1,0:T(8,128)(2,1)S(1)} %collective-permute-done.12.refs_1_) | copy-start | bytes 1179652
  46.5 39.1 %collective-permute-start.18 = (bf16[768,512]{1,0:T(8,128)(2,1)}, bf16[768,512]{1,0:T(8,128)(2,1)}, u32[]{:S(2)}, u32[]{:S(2)}) collective-permute-start(bf16[768,512]{1,0:T(8,128)(2,1)} %get-tuple-element.59), channel_id=1, source_target_pairs={{0,16},{16,32},{32,48},{48,0},{1,17},{17,33},{33,49},{49,1},{2,18}... | collective-permute-start | bytes 2359304 | tf_op jit(solution)/shard_map/ppermute | solution.py:26
  53.7 33.9 %collective-permute-start.20 = (bf16[768,512]{1,0:T(8,128)(2,1)}, bf16[768,512]{1,0:T(8,128)(2,1)}, u32[]{:S(2)}, u32[]{:S(2)}) collective-permute-start(bf16[768,512]{1,0:T(8,128)(2,1)} %get-tuple-element.60), channel_id=1, source_target_pairs={{0,32},{16,48},{32,0},{48,16},{1,33},{17,49},{33,1},{49,17},{2,34}... | collective-permute-start | bytes 2359304 | tf_op jit(solution)/shard_map/ppermute | solution.py:26
  54.5 33.0 %collective-permute-start.19 = (bf16[768,512]{1,0:T(8,128)(2,1)}, bf16[768,512]{1,0:T(8,128)(2,1)}, u32[]{:S(2)}, u32[]{:S(2)}) collective-permute-start(bf16[768,512]{1,0:T(8,128)(2,1)} %get-tuple-element.61), channel_id=1, source_target_pairs={{0,48},{16,0},{32,16},{48,32},{1,49},{17,1},{33,17},{49,33},{2,50}... | collective-permute-start | bytes 2359304 | tf_op jit(solution)/shard_map/ppermute | solution.py:26
  56.2 9.6 %collective-permute-start.15 = (bf16[896,256]{1,0:T(8,128)(2,1)}, bf16[896,256]{1,0:T(8,128)(2,1)S(1)}, u32[]{:S(2)}, u32[]{:S(2)}) collective-permute-start(bf16[896,256]{1,0:T(8,128)(2,1)} %collective-permute-done.11.refs_0_.refs_12_), channel_id=1, source_target_pairs={{0,1},{1,0},{2,3},{3,2},{4,5},{5,4},{6,7},{7,6},{8,9},{9,8},{10,11... | collective-permute-start | bytes 1376264 | tf_op jit(solution)/shard_map/ppermute | solution.py:26
  56.3 9.5 %collective-permute-start.17 = (bf16[896,256]{1,0:T(8,128)(2,1)}, bf16[896,256]{1,0:T(8,128)(2,1)S(1)}, u32[]{:S(2)}, u32[]{:S(2)}) collective-permute-start(bf16[896,256]{1,0:T(8,128)(2,1)} %collective-permute-done.16.refs_2_.refs_14_), channel_id=1, source_target_pairs={{0,1},{1,0},{2,3},{3,2},{4,5},{5,4},{6,7},{7,6},{8,9},{9,8},{10,11... | collective-permute-start | bytes 1376264 | tf_op jit(solution)/shard_map/ppermute | solution.py:26
  57.6 17.8 %all-to-all-start.1 = ((bf16[4,32,768]{2,1,0:T(8,128)(2,1)}), bf16[4,32,768]{2,1,0:T(8,128)(2,1)S(1)}, u32[]{:S(2)}, u32[]{:S(2)}) async-start(bf16[4,32,768]{2,1,0:T(8,128)(2,1)} %low_sum.1), calls=%async_computation.1 | async-start | bytes 393216 | tf_op jit(solution)/shard_map/all_to_all | solution.py:30
  65.8 21.8 %copy-start.10 = (bf16[896,256]{1,0:T(8,128)(2,1)}, bf16[896,256]{1,0:T(8,128)(2,1)S(1)}, u32[]{:S(2)}) copy-start(bf16[896,256]{1,0:T(8,128)(2,1)S(1)} %collective-permute-done.15.refs_1_.refs_13_) | copy-start | bytes 1376260
  65.8 21.8 %copy-start.11 = (bf16[896,256]{1,0:T(8,128)(2,1)}, bf16[896,256]{1,0:T(8,128)(2,1)S(1)}, u32[]{:S(2)}) copy-start(bf16[896,256]{1,0:T(8,128)(2,1)S(1)} %collective-permute-done.17.refs_3_.refs_15_) | copy-start | bytes 1376260
  70.4 25.1 %collective-permute-start.21 = (bf16[384,256]{1,0:T(8,128)(2,1)}, bf16[384,256]{1,0:T(8,128)(2,1)S(1)}, u32[]{:S(2)}, u32[]{:S(2)}) collective-permute-start(bf16[384,256]{1,0:T(8,128)(2,1)} %get-tuple-element.69), channel_id=1, source_target_pairs={{0,16},{16,32},{32,48},{48,0},{1,17},{17,33},{33,49},{49,1},{2,18}... | collective-permute-start | bytes 589832 | tf_op jit(solution)/shard_map/ppermute | solution.py:26
  70.5 37.1 %collective-permute-start.23 = (bf16[384,256]{1,0:T(8,128)(2,1)}, bf16[384,256]{1,0:T(8,128)(2,1)}, u32[]{:S(2)}, u32[]{:S(2)}) collective-permute-start(bf16[384,256]{1,0:T(8,128)(2,1)} %get-tuple-element.70), channel_id=1, source_target_pairs={{0,32},{16,48},{32,0},{48,16},{1,33},{17,49},{33,1},{49,17},{2,34}... | collective-permute-start | bytes 589832 | tf_op jit(solution)/shard_map/ppermute | solution.py:26
  80.5 16.9 %all-to-all-start.2 = ((f32[16,32,256]{2,1,0:T(8,128)}), f32[16,32,256]{2,1,0:T(8,128)S(1)}, u32[]{:S(2)}, u32[]{:S(2)}) async-start(f32[16,32,256]{2,1,0:T(8,128)} %grad_partial.1), calls=%async_computation.2 | async-start | bytes 1048576 | tf_op jit(solution)/shard_map/all_to_all | solution.py:30
  85.6 11.8 %copy-start.2 = (f32[32,256]{1,0:T(8,128)S(1)}, f32[32,256]{1,0:T(8,128)}, u32[]{:S(2)}) copy-start(f32[32,256]{1,0:T(8,128)} %first.1) | copy-start | bytes 98308
  85.6 11.8 %copy-start.3 = (f32[32,256]{1,0:T(8,128)S(1)}, f32[32,256]{1,0:T(8,128)}, u32[]{:S(2)}) copy-start(f32[32,256]{1,0:T(8,128)} %second.1) | copy-start | bytes 98308
  85.6 22.1 %collective-permute-start.22 = (bf16[384,256]{1,0:T(8,128)(2,1)}, bf16[384,256]{1,0:T(8,128)(2,1)}, u32[]{:S(2)}, u32[]{:S(2)}) collective-permute-start(bf16[384,256]{1,0:T(8,128)(2,1)} %get-tuple-element.71), channel_id=1, source_target_pairs={{0,48},{16,0},{32,16},{48,32},{1,49},{17,1},{33,17},{49,33},{2,50}... | collective-permute-start | bytes 589832 | tf_op jit(solution)/shard_map/ppermute | solution.py:26
  92.2 15.5 %collective-permute-start.24 = (bf16[384,256]{1,0:T(8,128)(2,1)}, bf16[384,256]{1,0:T(8,128)(2,1)S(1)}, u32[]{:S(2)}, u32[]{:S(2)}) collective-permute-start(bf16[384,256]{1,0:T(8,128)(2,1)} %get-tuple-element.78), channel_id=1, source_target_pairs={{0,16},{16,32},{32,48},{48,0},{1,17},{17,33},{33,49},{49,1},{2,18}... | collective-permute-start | bytes 589832 | tf_op jit(solution)/shard_map/ppermute | solution.py:26
  94.8 12.9 %collective-permute-start.25 = (bf16[384,256]{1,0:T(8,128)(2,1)}, bf16[384,256]{1,0:T(8,128)(2,1)S(1)}, u32[]{:S(2)}, u32[]{:S(2)}) collective-permute-start(bf16[384,256]{1,0:T(8,128)(2,1)} %get-tuple-element.79), channel_id=1, source_target_pairs={{0,48},{16,0},{32,16},{48,32},{1,49},{17,1},{33,17},{49,33},{2,50}... | collective-permute-start | bytes 589832 | tf_op jit(solution)/shard_map/ppermute | solution.py:26
  95.6 12.2 %copy-start.15 = (bf16[384,256]{1,0:T(8,128)(2,1)}, bf16[384,256]{1,0:T(8,128)(2,1)S(1)}, u32[]{:S(2)}) copy-start(bf16[384,256]{1,0:T(8,128)(2,1)S(1)} %collective-permute-done.21.refs_9_) | copy-start | bytes 589828
  95.6 12.2 %collective-permute-start.26 = (bf16[384,256]{1,0:T(8,128)(2,1)}, bf16[384,256]{1,0:T(8,128)(2,1)S(1)}, u32[]{:S(2)}, u32[]{:S(2)}) collective-permute-start(bf16[384,256]{1,0:T(8,128)(2,1)} %get-tuple-element.80), channel_id=1, source_target_pairs={{0,32},{16,48},{32,0},{48,16},{1,33},{17,49},{33,1},{49,17},{2,34}... | collective-permute-start | bytes 589832 | tf_op jit(solution)/shard_map/ppermute | solution.py:26
  98.2 58.7 %all-to-all-start.3 = ((bf16[16,32,256]{2,1,0:T(8,128)(2,1)}), bf16[16,32,256]{2,1,0:T(8,128)(2,1)S(1)}, u32[]{:S(2)}, u32[]{:S(2)}) async-start(bf16[16,32,256]{2,1,0:T(8,128)(2,1)} %get-tuple-element.74), calls=%async_computation.3 | async-start | bytes 524288 | tf_op jit(solution)/shard_map/all_to_all | solution.py:30
  114.4 31.0 %collective-permute-start.27 = (bf16[768,256]{1,0:T(8,128)(2,1)}, bf16[768,256]{1,0:T(8,128)(2,1)S(1)}, u32[]{:S(2)}, u32[]{:S(2)}) collective-permute-start(bf16[768,256]{1,0:T(8,128)(2,1)} %get-tuple-element.82), channel_id=1, source_target_pairs={{0,64},{64,128},{128,192},{192,0},{1,65},{65,129},{129,193},{193,1... | collective-permute-start | bytes 1179656 | tf_op jit(solution)/shard_map/ppermute | solution.py:26
  117.3 28.1 %collective-permute-start.28 = (bf16[768,256]{1,0:T(8,128)(2,1)}, bf16[768,256]{1,0:T(8,128)(2,1)S(1)}, u32[]{:S(2)}, u32[]{:S(2)}) collective-permute-start(bf16[768,256]{1,0:T(8,128)(2,1)} %get-tuple-element.83), channel_id=1, source_target_pairs={{0,192},{64,0},{128,64},{192,128},{1,193},{65,1},{129,65},{193,129... | collective-permute-start | bytes 1179656 | tf_op jit(solution)/shard_map/ppermute | solution.py:26
  118.7 37.4 %collective-permute-start.29 = (bf16[768,256]{1,0:T(8,128)(2,1)}, bf16[768,256]{1,0:T(8,128)(2,1)S(1)}, u32[]{:S(2)}, u32[]{:S(2)}) collective-permute-start(bf16[768,256]{1,0:T(8,128)(2,1)} %get-tuple-element.84), channel_id=1, source_target_pairs={{0,128},{64,192},{128,0},{192,64},{1,129},{65,193},{129,1},{193,65... | collective-permute-start | bytes 1179656 | tf_op jit(solution)/shard_map/ppermute | solution.py:26
  124.5 31.5 %copy-start.1 = (bf16[768,256]{1,0:T(8,128)(2,1)S(1)}, bf16[768,256]{1,0:T(8,128)(2,1)}, u32[]{:S(2)}) copy-start(bf16[768,256]{1,0:T(8,128)(2,1)} %get-tuple-element.81.a) | copy-start | bytes 1179652
  (5 other events, 7.1 us)

commit v2 on v1

--- a/solution.py
+++ b/solution.py
@@ -355,7 +355,7 @@
     sum2 = spread(part2, "x")
     grad_part = grad_partial(after(low_z, *part2), cotangent)
     grad_all = swap(grad_part, FSDP)
-    part3 = partials(after(hidden, grad_part, *sum1[1:], *part2), [slots[2]], slot_of, half, half)
+    part3 = partials(after(hidden, grad_part, sum1[1], *part2), [slots[2]], slot_of, half, half)
     sum3 = spread(part3, "x")
 
     new_first, new_second, normed = moments(grad_all, first_moment, second_moment)

time: 159 us -> 157 us (0.987)
  starting transfers between devices: 67.7 us -> 63.5 us
    ppermute x30, starting transfers between devices: 41.5 us -> 39.3 us  [shift(): return lax.ppermute(array, axis, [(i, (i + by) % n) for i in range(n)])]
    all_to_all x4, starting transfers between devices: 26.2 us -> 24.3 us  [swap(): return lax.all_to_all(array, axes, 0, 0, tiled=True)]
where the time goes in v2:
time: 157 us; the launch traced here: 156 us
  starting transfers between devices  63.5 us (40%)
  Pallas kernels  48.3 us (31%)
  waiting for transfers between devices  36.8 us (23%)
  local copies, waits for them, and re-layouts  2.91 us (2%)
  matrix products  2.84 us (2%)
    ppermute x30, starting transfers between devices, shift(): return lax.ppermute(array, axis, [(i, (i + by) % n) for i in range(n)])  39.3 us
    ppermute x30, waiting for transfers between devices, shift(): return lax.ppermute(array, axis, [(i, (i + by) % n) for i in range(n)])  30.5 us
    all_to_all x4, starting transfers between devices, swap(): return lax.all_to_all(array, axes, 0, 0, tiled=True)  24.3 us
    pallas_call x4, Pallas kernels, partials(): pl.pallas_call(functools.partial(partial_kernel, m, start), out_shape=[pl...  22.7 us
    pallas_call x1, Pallas kernels, act(): pl.pallas_call(act_kernel, out_shape=jax.ShapeDtypeStruct((tokens, full),...  12.2 us
    all_to_all x4, waiting for transfers between devices, swap(): return lax.all_to_all(array, axes, 0, 0, tiled=True)  6.3 us
    pallas_call x1, Pallas kernels, regroup(): pl.pallas_call(functools.partial(regroup_kernel, [offs for _, offs in gro...  5.89 us
    pallas_call x1, Pallas kernels, grad_partial(): pl.pallas_call(grad_kernel, out_shape=pltpu.HBM((features // W, ranks, W)...  5.04 us
  transfers between devices with their start and end apart: 34, of which 9 were waited for; matrix products, arithmetic and copies ran while one was open for 2% of the time, Pallas kernels for 31%

profile of v2, /device:TPU:32, one launch (start us, length us, event | category | flops | bytes accessed | tf_op | source)
XLA Modules:
  0.0 155.6 jit_solution(8298289014897513445)
XLA Ops:
  0.6 1.7 %collective-permute-start.2 = (bf16[896,256]{1,0:T(8,128)(2,1)}, bf16[896,256]{1,0:T(8,128)(2,1)S(1)}, u32[]{:S(2)}, u32[]{:S(2)}) collective-permute-start(bf16[896,256]{1,0:T(8,128)(2,1)} %refs_0_.3), channel_id=1, source_target_pairs={{0,4},{4,8},{8,12},{12,0},{1,5},{5,9},{9,13},{13,1},{2,6},{6,10},{... | collective-permute-start | bytes 1376264 | tf_op jit(solution)/shard_map/ppermute | solution.py:26
  2.3 1.7 %collective-permute-start = (bf16[896,256]{1,0:T(8,128)(2,1)}, bf16[896,256]{1,0:T(8,128)(2,1)S(1)}, u32[]{:S(2)}, u32[]{:S(2)}) collective-permute-start(bf16[896,256]{1,0:T(8,128)(2,1)} %refs_0_.3), channel_id=1, source_target_pairs={{0,12},{4,0},{8,4},{12,8},{1,13},{5,1},{9,5},{13,9},{2,14},{6,2},{... | collective-permute-start | bytes 1376264 | tf_op jit(solution)/shard_map/ppermute | solution.py:26
  4.0 1.8 %collective-permute-start.5 = (bf16[896,256]{1,0:T(8,128)(2,1)}, bf16[896,256]{1,0:T(8,128)(2,1)S(1)}, u32[]{:S(2)}, u32[]{:S(2)}) collective-permute-start(bf16[896,256]{1,0:T(8,128)(2,1)} %refs_0_.3), channel_id=1, source_target_pairs={{0,2},{2,0},{1,3},{3,1},{4,6},{6,4},{5,7},{7,5},{8,10},{10,8},{9,1... | collective-permute-start | bytes 1376264 | tf_op jit(solution)/shard_map/ppermute | solution.py:26
  5.8 2.4 %convolution_convert_fusion = bf16[512,768]{1,0:T(8,128)(2,1)S(1)} fusion(bf16[896,512]{1,0:T(8,128)(2,1)S(1)} %copy-done, bf16[768,896]{1,0:T(8,128)(2,1)} %h_ref.3), kind=kOutput, calls=%fused_computation | convolution fusion | flops 705036288 | bytes 3080192 | tf_op jit(solution)/shard_map/dot_general | solution.py:321
  8.2 0.9 copy.15
  9.1 3.5 %all-to-all-start = ((bf16[4,4,32,768]{3,2,1,0:T(8,128)(2,1)}), bf16[4,4,32,768]{3,2,1,0:T(8,128)(2,1)S(1)}, u32[]{:S(2)}, u32[]{:S(2)}) async-start(bf16[4,4,32,768]{3,2,1,0:T(8,128)(2,1)} %bitcast.27), calls=%async_computation | async-start | bytes 1572864 | tf_op jit(solution)/shard_map/all_to_all | solution.py:30
  12.7 1.7 %collective-permute-done.2.refs_4_.refs_8_ = bf16[896,256]{1,0:T(8,128)(2,1)S(1)} collective-permute-done((bf16[896,256]{1,0:T(8,128)(2,1)}, bf16[896,256]{1,0:T(8,128)(2,1)S(1)}, u32[]{:S(2)}, u32[]{:S(2)}) %collective-permute-start.2) | collective-permute-done | bytes 458784 | tf_op jit(solution)/shard_map/ppermute | solution.py:26
  14.6 0.5 collective-permute-start.3
  15.1 0.9 collective-permute-done.5.refs_2_
  16.1 0.7 collective-permute-start.9
  16.9 2.6 %collective-permute-start.7 = (bf16[896,256]{1,0:T(8,128)(2,1)S(1)}, bf16[896,256]{1,0:T(8,128)(2,1)}, u32[]{:S(2)}, u32[]{:S(2)}) collective-permute-start(bf16[896,256]{1,0:T(8,128)(2,1)S(1)} %collective-permute-done.5.refs_2_), channel_id=1, source_target_pairs={{0,12},{4,0},{8,4},{12,8},{1,13},{5,1},{9,5},{13,9},{2,14},{6,2},{... | collective-permute-start | bytes 1376264 | tf_op jit(solution)/shard_map/ppermute | solution.py:26
  19.5 4.0 %all-to-all-done.parts = bf16[4,4,32,768]{3,2,1,0:T(8,128)(2,1)S(1)} async-done(((bf16[4,4,32,768]{3,2,1,0:T(8,128)(2,1)}), bf16[4,4,32,768]{3,2,1,0:T(8,128)(2,1)S(1)}, u32[]{:S(2)}, u32[]{:S(2)}) %all-to-all-start) | async-done | bytes 786464 | tf_op jit(solution)/shard_map/all_to_all | solution.py:30
  23.5 6.7 %partials.4 = (bf16[768,256]{1,0:T(8,128)(2,1)}, bf16[768,256]{1,0:T(8,128)(2,1)}, bf16[768,256]{1,0:T(8,128)(2,1)}, bf16[768,256]{1,0:T(8,128)(2,1)}) custom-call(s32[4]{0:T(128)S(1)} %pad_add_fusion.1.slot_of, bf16[768,896]{1,0:T(8,128)(2,1)} %h_ref.3, bf16[896,256]{1,0:T(8,128)(2,1)S(1)} %copy-done.4, bf16[896,256]{1,0:T(8,128)(2,1)} %collective-permute-done.4.refs_1_, ...), custom_call_target="tpu_custom_call" | custom-call | flops 8589934592 | bytes 33554432 | tf_op jit(solution)/shard_map/partials/pallas_call | solution.py:82
  30.4 0.5 collective-permute-start.10
  30.9 1.5 collective-permute-start.12
  32.4 2.7 %collective-permute-start.14 = (bf16[768,256]{1,0:T(8,128)(2,1)}, bf16[768,256]{1,0:T(8,128)(2,1)S(1)}, u32[]{:S(2)}, u32[]{:S(2)}) collective-permute-start(bf16[768,256]{1,0:T(8,128)(2,1)} %get-tuple-element.53), channel_id=1, source_target_pairs={{0,32},{16,48},{32,0},{48,16},{1,33},{17,49},{33,1},{49,17},{2,34}... | collective-permute-start | bytes 1179656 | tf_op jit(solution)/shard_map/ppermute | solution.py:26
  35.1 1.4 collective-permute-start.13
  36.6 3.0 %collective-permute-start.11 = (bf16[896,256]{1,0:T(8,128)(2,1)S(1)}, bf16[896,256]{1,0:T(8,128)(2,1)}, u32[]{:S(2)}, u32[]{:S(2)}) collective-permute-start(bf16[896,256]{1,0:T(8,128)(2,1)S(1)} %collective-permute-done.refs_0_.refs_4_), channel_id=1, source_target_pairs={{0,12},{4,0},{8,4},{12,8},{1,13},{5,1},{9,5},{13,9},{2,14},{6,2},{... | collective-permute-start | bytes 1376264 | tf_op jit(solution)/shard_map/ppermute | solution.py:26
  39.6 6.8 %partials.5 = (bf16[768,512]{1,0:T(8,128)(2,1)}, bf16[768,512]{1,0:T(8,128)(2,1)}, bf16[768,512]{1,0:T(8,128)(2,1)}, bf16[768,512]{1,0:T(8,128)(2,1)}) custom-call(s32[4]{0:T(128)S(1)} %pad_add_fusion.1.slot_of, bf16[768,896]{1,0:T(8,128)(2,1)} %h_ref.3, bf16[896,256]{1,0:T(8,128)(2,1)S(1)} %collective-permute-done.refs_0_.refs_4_, ...), custom_call_target="tpu_custom_call" | custom-call | flops 8589934592 | bytes 33554432 | tf_op jit(solution)/shard_map/partials/pallas_call | solution.py:82
  46.5 0.7 collective-permute-start.18
  47.2 6.6 %collective-permute-done.14.refs_3_ = bf16[768,256]{1,0:T(8,128)(2,1)S(1)} collective-permute-done((bf16[768,256]{1,0:T(8,128)(2,1)}, bf16[768,256]{1,0:T(8,128)(2,1)S(1)}, u32[]{:S(2)}, u32[]{:S(2)}) %collective-permute-start.14) | collective-permute-done | bytes 393248 | tf_op jit(solution)/shard_map/ppermute | solution.py:26
  53.7 0.8 collective-permute-start.20
  54.5 1.7 %collective-permute-start.19 = (bf16[768,512]{1,0:T(8,128)(2,1)}, bf16[768,512]{1,0:T(8,128)(2,1)}, u32[]{:S(2)}, u32[]{:S(2)}) collective-permute-start(bf16[768,512]{1,0:T(8,128)(2,1)} %get-tuple-element.61), channel_id=1, source_target_pairs={{0,48},{16,0},{32,16},{48,32},{1,49},{17,1},{33,17},{49,33},{2,50}... | collective-permute-start | bytes 2359304 | tf_op jit(solution)/shard_map/ppermute | solution.py:26
  56.3 0.6 collective-permute-start.17
  56.8 0.8 low_sum.1
  57.6 8.2 %all-to-all-start.1 = ((bf16[4,32,768]{2,1,0:T(8,128)(2,1)}), bf16[4,32,768]{2,1,0:T(8,128)(2,1)S(1)}, u32[]{:S(2)}, u32[]{:S(2)}) async-start(bf16[4,32,768]{2,1,0:T(8,128)(2,1)} %low_sum.1), calls=%async_computation.1 | async-start | bytes 393216 | tf_op jit(solution)/shard_map/all_to_all | solution.py:30
  65.8 4.6 %partials.6 = (bf16[384,256]{1,0:T(8,128)(2,1)}, bf16[384,256]{1,0:T(8,128)(2,1)}, bf16[384,256]{1,0:T(8,128)(2,1)}, bf16[384,256]{1,0:T(8,128)(2,1)}) custom-call(s32[4]{0:T(128)S(1)} %pad_add_fusion.1.slot_of, bf16[768,896]{1,0:T(8,128)(2,1)} %h_ref.3, bf16[896,256]{1,0:T(8,128)(2,1)} %collective-permute-done.11.refs_0_.refs_12_, ...), custom_call_target="tpu_custom_call" | custom-call | flops 8589934592 | bytes 33554432 | tf_op jit(solution)/shard_map/partials/pallas_call | solution.py:82
  70.5 2.6 %collective-permute-start.23 = (bf16[384,256]{1,0:T(8,128)(2,1)}, bf16[384,256]{1,0:T(8,128)(2,1)}, u32[]{:S(2)}, u32[]{:S(2)}) collective-permute-start(bf16[384,256]{1,0:T(8,128)(2,1)} %get-tuple-element.70), channel_id=1, source_target_pairs={{0,32},{16,48},{32,0},{48,16},{1,33},{17,49},{33,1},{49,17},{2,34}... | collective-permute-start | bytes 589832 | tf_op jit(solution)/shard_map/ppermute | solution.py:26
  73.1 2.3 %all-to-all-done.1.low_ref = bf16[4,32,768]{2,1,0:T(8,128)(2,1)S(1)} async-done(((bf16[4,32,768]{2,1,0:T(8,128)(2,1)}), bf16[4,32,768]{2,1,0:T(8,128)(2,1)S(1)}, u32[]{:S(2)}, u32[]{:S(2)}) %all-to-all-start.1) | async-done | bytes 196640 | tf_op jit(solution)/shard_map/all_to_all | solution.py:30
  75.4 5.0 %grad_partial.1 = f32[16,32,256]{2,1,0:T(8,128)} custom-call(bf16[4,32,768]{2,1,0:T(8,128)(2,1)S(1)} %all-to-all-done.1.low_ref, bf16[768,4096]{1,0:T(8,128)(2,1)} %cot_ref.2), custom_call_target="tpu_custom_call" | custom-call | flops 8589934592 | bytes 33554432 | tf_op jit(solution)/shard_map/grad_partial/pallas_call | solution.py:210
  80.5 5.1 %all-to-all-start.2 = ((f32[16,32,256]{2,1,0:T(8,128)}), f32[16,32,256]{2,1,0:T(8,128)S(1)}, u32[]{:S(2)}, u32[]{:S(2)}) async-start(f32[16,32,256]{2,1,0:T(8,128)} %grad_partial.1), calls=%async_computation.2 | async-start | bytes 1048576 | tf_op jit(solution)/shard_map/all_to_all | solution.py:30
  85.6 1.7 %collective-permute-start.22 = (bf16[384,256]{1,0:T(8,128)(2,1)}, bf16[384,256]{1,0:T(8,128)(2,1)}, u32[]{:S(2)}, u32[]{:S(2)}) collective-permute-start(bf16[384,256]{1,0:T(8,128)(2,1)} %get-tuple-element.71), channel_id=1, source_target_pairs={{0,48},{16,0},{32,16},{48,32},{1,49},{17,1},{33,17},{49,33},{2,50}... | collective-permute-start | bytes 589832 | tf_op jit(solution)/shard_map/ppermute | solution.py:26
  87.3 4.6 %partials.7 = (bf16[384,256]{1,0:T(8,128)(2,1)}, bf16[384,256]{1,0:T(8,128)(2,1)}, bf16[384,256]{1,0:T(8,128)(2,1)}, bf16[384,256]{1,0:T(8,128)(2,1)}) custom-call(s32[4]{0:T(128)S(1)} %pad_add_fusion.1.slot_of, bf16[768,896]{1,0:T(8,128)(2,1)} %h_ref.3, bf16[896,256]{1,0:T(8,128)(2,1)} %collective-permute-done.11.refs_0_.refs_12_, ...), custom_call_target="tpu_custom_call" | custom-call | flops 8589934592 | bytes 33554432 | tf_op jit(solution)/shard_map/partials/pallas_call | solution.py:82
  91.9 0.6 collective-permute-start.24
  92.6 2.7 %collective-permute-start.25 = (bf16[384,256]{1,0:T(8,128)(2,1)}, bf16[384,256]{1,0:T(8,128)(2,1)S(1)}, u32[]{:S(2)}, u32[]{:S(2)}) collective-permute-start(bf16[384,256]{1,0:T(8,128)(2,1)} %get-tuple-element.79), channel_id=1, source_target_pairs={{0,48},{16,0},{32,16},{48,32},{1,49},{17,1},{33,17},{49,33},{2,50}... | collective-permute-start | bytes 589832 | tf_op jit(solution)/shard_map/ppermute | solution.py:26
  95.5 0.8 moments.1
  96.3 7.5 %all-to-all-start.3 = ((bf16[16,32,256]{2,1,0:T(8,128)(2,1)}), bf16[16,32,256]{2,1,0:T(8,128)(2,1)S(1)}, u32[]{:S(2)}, u32[]{:S(2)}) async-start(bf16[16,32,256]{2,1,0:T(8,128)(2,1)} %get-tuple-element.74), calls=%async_computation.3 | async-start | bytes 524288 | tf_op jit(solution)/shard_map/all_to_all | solution.py:30
  103.8 0.6 collective-permute-done.24.refs_13_
  104.5 0.7 copy-done.16
  105.3 5.9 %regroup.1 = (bf16[768,256]{1,0:T(8,128)(2,1)}, bf16[768,256]{1,0:T(8,128)(2,1)}, bf16[768,256]{1,0:T(8,128)(2,1)}, bf16[768,256]{1,0:T(8,128)(2,1)}) custom-call(s32[4]{0:T(128)S(1)} %pad_add_fusion.place, bf16[768,256]{1,0:T(8,128)(2,1)} %get-tuple-element.55.refs_0_, bf16[768,256]{1,0:T(8,128)(2,1)} %copy-done.12, bf16[768,256]{1,0:T(8,128)(2,1)} %copy-done.14, ...), custom_call_target="tpu_custom_call" | custom-call | flops 8589934592 | bytes 33554432 | tf_op jit(solution)/shard_map/regroup/pallas_call | solution.py:136
  111.2 2.3 %collective-permute-start.27 = (bf16[768,256]{1,0:T(8,128)(2,1)}, bf16[768,256]{1,0:T(8,128)(2,1)S(1)}, u32[]{:S(2)}, u32[]{:S(2)}) collective-permute-start(bf16[768,256]{1,0:T(8,128)(2,1)} %get-tuple-element.82), channel_id=1, source_target_pairs={{0,64},{64,128},{128,192},{192,0},{1,65},{65,129},{129,193},{193,1... | collective-permute-start | bytes 1179656 | tf_op jit(solution)/shard_map/ppermute | solution.py:26
  113.5 2.1 %collective-permute-start.28 = (bf16[768,256]{1,0:T(8,128)(2,1)}, bf16[768,256]{1,0:T(8,128)(2,1)S(1)}, u32[]{:S(2)}, u32[]{:S(2)}) collective-permute-start(bf16[768,256]{1,0:T(8,128)(2,1)} %get-tuple-element.83), channel_id=1, source_target_pairs={{0,192},{64,0},{128,64},{192,128},{1,193},{65,1},{129,65},{193,129... | collective-permute-start | bytes 1179656 | tf_op jit(solution)/shard_map/ppermute | solution.py:26
  115.6 5.1 %collective-permute-start.29 = (bf16[768,256]{1,0:T(8,128)(2,1)}, bf16[768,256]{1,0:T(8,128)(2,1)S(1)}, u32[]{:S(2)}, u32[]{:S(2)}) collective-permute-start(bf16[768,256]{1,0:T(8,128)(2,1)} %get-tuple-element.84), channel_id=1, source_target_pairs={{0,128},{64,192},{128,0},{192,64},{1,129},{65,193},{129,1},{193,65... | collective-permute-start | bytes 1179656 | tf_op jit(solution)/shard_map/ppermute | solution.py:26
  120.7 12.2 %act_grad.1 = bf16[768,896]{1,0:T(8,128)(2,1)} custom-call(s32[8]{0:T(128)S(1)} %stack.75.order, bf16[768,4096]{1,0:T(8,128)(2,1)} %cot_ref.2, bf16[896,256]{1,0:T(8,128)(2,1)} %refs_0_.3, bf16[896,256]{1,0:T(8,128)(2,1)} %collective-permute-done.4.refs_1_, bf16[896,256]{1,0:T(8,128)(2,1)} %copy-done.7, bf16[896,256]{1,0:T(8,128)(2,1)} %collective-permute-done.6.refs_3_, ...), custom_call_target="tpu_custom_call" | custom-call | flops 8589934592 | bytes 33554432 | tf_op jit(solution)/shard_map/act_grad/pallas_call | solution.py:294
  132.9 9.7 %collective-permute-done.27.b = bf16[768,256]{1,0:T(8,128)(2,1)S(1)} collective-permute-done((bf16[768,256]{1,0:T(8,128)(2,1)}, bf16[768,256]{1,0:T(8,128)(2,1)S(1)}, u32[]{:S(2)}, u32[]{:S(2)}) %collective-permute-start.27) | collective-permute-done | bytes 393248 | tf_op jit(solution)/shard_map/ppermute | solution.py:26
  142.6 10.7 %collective-permute-done.29.d = bf16[768,256]{1,0:T(8,128)(2,1)S(1)} collective-permute-done((bf16[768,256]{1,0:T(8,128)(2,1)}, bf16[768,256]{1,0:T(8,128)(2,1)S(1)}, u32[]{:S(2)}, u32[]{:S(2)}) %collective-permute-start.29) | collective-permute-done | bytes 393248 | tf_op jit(solution)/shard_map/ppermute | solution.py:26
  153.3 0.9 finish.1
  154.7 1.0 copy.13
  (75 shorter events, 1.5 us)
Async XLA Ops:
  0.6 5.2 %copy-start = (bf16[896,512]{1,0:T(8,128)(2,1)S(1)}, bf16[896,512]{1,0:T(8,128)(2,1)}, u32[]{:S(2)}) copy-start(bf16[896,512]{1,0:T(8,128)(2,1)} %param.9) | copy-start | bytes 2752516
  0.6 13.8 %collective-permute-start.2 = (bf16[896,256]{1,0:T(8,128)(2,1)}, bf16[896,256]{1,0:T(8,128)(2,1)S(1)}, u32[]{:S(2)}, u32[]{:S(2)}) collective-permute-start(bf16[896,256]{1,0:T(8,128)(2,1)} %refs_0_.3), channel_id=1, source_target_pairs={{0,4},{4,8},{8,12},{12,0},{1,5},{5,9},{9,13},{13,1},{2,6},{6,10},{... | collective-permute-start | bytes 1376264 | tf_op jit(solution)/shard_map/ppermute | solution.py:26
  2.3 12.2 %collective-permute-start = (bf16[896,256]{1,0:T(8,128)(2,1)}, bf16[896,256]{1,0:T(8,128)(2,1)S(1)}, u32[]{:S(2)}, u32[]{:S(2)}) collective-permute-start(bf16[896,256]{1,0:T(8,128)(2,1)} %refs_0_.3), channel_id=1, source_target_pairs={{0,12},{4,0},{8,4},{12,8},{1,13},{5,1},{9,5},{13,9},{2,14},{6,2},{... | collective-permute-start | bytes 1376264 | tf_op jit(solution)/shard_map/ppermute | solution.py:26
  4.0 12.1 %collective-permute-start.5 = (bf16[896,256]{1,0:T(8,128)(2,1)}, bf16[896,256]{1,0:T(8,128)(2,1)S(1)}, u32[]{:S(2)}, u32[]{:S(2)}) collective-permute-start(bf16[896,256]{1,0:T(8,128)(2,1)} %refs_0_.3), channel_id=1, source_target_pairs={{0,2},{2,0},{1,3},{3,1},{4,6},{6,4},{5,7},{7,5},{8,10},{10,8},{9,1... | collective-permute-start | bytes 1376264 | tf_op jit(solution)/shard_map/ppermute | solution.py:26
  8.2 4.5 %copy-start.4 = (bf16[896,256]{1,0:T(8,128)(2,1)S(1)}, bf16[896,256]{1,0:T(8,128)(2,1)}, u32[]{:S(2)}) copy-start(bf16[896,256]{1,0:T(8,128)(2,1)} %refs_0_.3) | copy-start | bytes 1376260
  9.1 14.3 %all-to-all-start = ((bf16[4,4,32,768]{3,2,1,0:T(8,128)(2,1)}), bf16[4,4,32,768]{3,2,1,0:T(8,128)(2,1)S(1)}, u32[]{:S(2)}, u32[]{:S(2)}) async-start(bf16[4,4,32,768]{3,2,1,0:T(8,128)(2,1)} %bitcast.27), calls=%async_computation | async-start | bytes 1572864 | tf_op jit(solution)/shard_map/all_to_all | solution.py:30
  12.6 10.8 %collective-permute-start.4 = (bf16[896,256]{1,0:T(8,128)(2,1)S(1)}, bf16[896,256]{1,0:T(8,128)(2,1)}, u32[]{:S(2)}, u32[]{:S(2)}) collective-permute-start(bf16[896,256]{1,0:T(8,128)(2,1)S(1)} %copy-done.4), channel_id=1, source_target_pairs={{0,1},{1,0},{2,3},{3,2},{4,5},{5,4},{6,7},{7,6},{8,9},{9,8},{10,11... | collective-permute-start | bytes 1376264 | tf_op jit(solution)/shard_map/ppermute | solution.py:26
  14.5 25.1 %copy-start.5 = (bf16[896,256]{1,0:T(8,128)(2,1)}, bf16[896,256]{1,0:T(8,128)(2,1)S(1)}, u32[]{:S(2)}) copy-start(bf16[896,256]{1,0:T(8,128)(2,1)S(1)} %collective-permute-done.2.refs_4_.refs_8_) | copy-start | bytes 1376260
  14.5 25.1 %copy-start.6 = (bf16[896,256]{1,0:T(8,128)(2,1)}, bf16[896,256]{1,0:T(8,128)(2,1)S(1)}, u32[]{:S(2)}) copy-start(bf16[896,256]{1,0:T(8,128)(2,1)S(1)} %collective-permute-done.refs_0_.refs_4_) | copy-start | bytes 1376260
  14.5 2.4 %collective-permute-start.1 = (bf16[896,256]{1,0:T(8,128)(2,1)S(1)}, bf16[896,256]{1,0:T(8,128)(2,1)}, u32[]{:S(2)}, u32[]{:S(2)}) collective-permute-start(bf16[896,256]{1,0:T(8,128)(2,1)S(1)} %collective-permute-done.refs_0_.refs_4_), channel_id=1, source_target_pairs={{0,1},{1,0},{2,3},{3,2},{4,5},{5,4},{6,7},{7,6},{8,9},{9,8},{10,11... | collective-permute-start | bytes 1376264 | tf_op jit(solution)/shard_map/ppermute | solution.py:26
  14.6 8.9 %collective-permute-start.3 = (bf16[896,256]{1,0:T(8,128)(2,1)S(1)}, bf16[896,256]{1,0:T(8,128)(2,1)}, u32[]{:S(2)}, u32[]{:S(2)}) collective-permute-start(bf16[896,256]{1,0:T(8,128)(2,1)S(1)} %collective-permute-done.2.refs_4_.refs_8_), channel_id=1, source_target_pairs={{0,1},{1,0},{2,3},{3,2},{4,5},{5,4},{6,7},{7,6},{8,9},{9,8},{10,11... | collective-permute-start | bytes 1376264 | tf_op jit(solution)/shard_map/ppermute | solution.py:26
  16.0 14.1 %copy-start.7 = (bf16[896,256]{1,0:T(8,128)(2,1)}, bf16[896,256]{1,0:T(8,128)(2,1)S(1)}, u32[]{:S(2)}) copy-start(bf16[896,256]{1,0:T(8,128)(2,1)S(1)} %collective-permute-done.5.refs_2_) | copy-start | bytes 1376260
  16.0 7.4 %collective-permute-start.6 = (bf16[896,256]{1,0:T(8,128)(2,1)S(1)}, bf16[896,256]{1,0:T(8,128)(2,1)}, u32[]{:S(2)}, u32[]{:S(2)}) collective-permute-start(bf16[896,256]{1,0:T(8,128)(2,1)S(1)} %collective-permute-done.5.refs_2_), channel_id=1, source_target_pairs={{0,1},{1,0},{2,3},{3,2},{4,5},{5,4},{6,7},{7,6},{8,9},{9,8},{10,11... | collective-permute-start | bytes 1376264 | tf_op jit(solution)/shard_map/ppermute | solution.py:26
  16.1 14.3 %collective-permute-start.9 = (bf16[896,256]{1,0:T(8,128)(2,1)S(1)}, bf16[896,256]{1,0:T(8,128)(2,1)}, u32[]{:S(2)}, u32[]{:S(2)}) collective-permute-start(bf16[896,256]{1,0:T(8,128)(2,1)S(1)} %collective-permute-done.5.refs_2_), channel_id=1, source_target_pairs={{0,4},{4,8},{8,12},{12,0},{1,5},{5,9},{9,13},{13,1},{2,6},{6,10},{... | collective-permute-start | bytes 1376264 | tf_op jit(solution)/shard_map/ppermute | solution.py:26
  16.9 13.5 %collective-permute-start.7 = (bf16[896,256]{1,0:T(8,128)(2,1)S(1)}, bf16[896,256]{1,0:T(8,128)(2,1)}, u32[]{:S(2)}, u32[]{:S(2)}) collective-permute-start(bf16[896,256]{1,0:T(8,128)(2,1)S(1)} %collective-permute-done.5.refs_2_), channel_id=1, source_target_pairs={{0,12},{4,0},{8,4},{12,8},{1,13},{5,1},{9,5},{13,9},{2,14},{6,2},{... | collective-permute-start | bytes 1376264 | tf_op jit(solution)/shard_map/ppermute | solution.py:26
  30.4 6.2 %collective-permute-start.8 = (bf16[896,256]{1,0:T(8,128)(2,1)}, bf16[896,256]{1,0:T(8,128)(2,1)S(1)}, u32[]{:S(2)}, u32[]{:S(2)}) collective-permute-start(bf16[896,256]{1,0:T(8,128)(2,1)} %collective-permute-done.7.refs_2_.refs_6_), channel_id=1, source_target_pairs={{0,1},{1,0},{2,3},{3,2},{4,5},{5,4},{6,7},{7,6},{8,9},{9,8},{10,11... | collective-permute-start | bytes 1376264 | tf_op jit(solution)/shard_map/ppermute | solution.py:26
  30.4 6.2 %collective-permute-start.10 = (bf16[896,256]{1,0:T(8,128)(2,1)}, bf16[896,256]{1,0:T(8,128)(2,1)S(1)}, u32[]{:S(2)}, u32[]{:S(2)}) collective-permute-start(bf16[896,256]{1,0:T(8,128)(2,1)} %collective-permute-done.9.refs_6_.refs_10_), channel_id=1, source_target_pairs={{0,1},{1,0},{2,3},{3,2},{4,5},{5,4},{6,7},{7,6},{8,9},{9,8},{10,11... | collective-permute-start | bytes 1376264 | tf_op jit(solution)/shard_map/ppermute | solution.py:26
  30.9 15.6 %collective-permute-start.12 = (bf16[768,256]{1,0:T(8,128)(2,1)}, bf16[768,256]{1,0:T(8,128)(2,1)S(1)}, u32[]{:S(2)}, u32[]{:S(2)}) collective-permute-start(bf16[768,256]{1,0:T(8,128)(2,1)} %get-tuple-element.52), channel_id=1, source_target_pairs={{0,16},{16,32},{32,48},{48,0},{1,17},{17,33},{33,49},{49,1},{2,18}... | collective-permute-start | bytes 1179656 | tf_op jit(solution)/shard_map/ppermute | solution.py:26
  32.4 21.4 %collective-permute-start.14 = (bf16[768,256]{1,0:T(8,128)(2,1)}, bf16[768,256]{1,0:T(8,128)(2,1)S(1)}, u32[]{:S(2)}, u32[]{:S(2)}) collective-permute-start(bf16[768,256]{1,0:T(8,128)(2,1)} %get-tuple-element.53), channel_id=1, source_target_pairs={{0,32},{16,48},{32,0},{48,16},{1,33},{17,49},{33,1},{49,17},{2,34}... | collective-permute-start | bytes 1179656 | tf_op jit(solution)/shard_map/ppermute | solution.py:26
  35.1 19.4 %collective-permute-start.13 = (bf16[768,256]{1,0:T(8,128)(2,1)}, bf16[768,256]{1,0:T(8,128)(2,1)S(1)}, u32[]{:S(2)}, u32[]{:S(2)}) collective-permute-start(bf16[768,256]{1,0:T(8,128)(2,1)} %get-tuple-element.54), channel_id=1, source_target_pairs={{0,48},{16,0},{32,16},{48,32},{1,49},{17,1},{33,17},{49,33},{2,50}... | collective-permute-start | bytes 1179656 | tf_op jit(solution)/shard_map/ppermute | solution.py:26
  36.5 9.9 %copy-start.8 = (bf16[896,256]{1,0:T(8,128)(2,1)}, bf16[896,256]{1,0:T(8,128)(2,1)S(1)}, u32[]{:S(2)}) copy-start(bf16[896,256]{1,0:T(8,128)(2,1)S(1)} %collective-permute-done.8.refs_3_.refs_7_) | copy-start | bytes 1376260
  36.5 9.9 %copy-start.9 = (bf16[896,256]{1,0:T(8,128)(2,1)}, bf16[896,256]{1,0:T(8,128)(2,1)S(1)}, u32[]{:S(2)}) copy-start(bf16[896,256]{1,0:T(8,128)(2,1)S(1)} %collective-permute-done.10.refs_7_.refs_11_) | copy-start | bytes 1376260
  36.6 19.7 %collective-permute-start.11 = (bf16[896,256]{1,0:T(8,128)(2,1)S(1)}, bf16[896,256]{1,0:T(8,128)(2,1)}, u32[]{:S(2)}, u32[]{:S(2)}) collective-permute-start(bf16[896,256]{1,0:T(8,128)(2,1)S(1)} %collective-permute-done.refs_0_.refs_4_), channel_id=1, source_target_pairs={{0,12},{4,0},{8,4},{12,8},{1,13},{5,1},{9,5},{13,9},{2,14},{6,2},{... | collective-permute-start | bytes 1376264 | tf_op jit(solution)/shard_map/ppermute | solution.py:26
  39.6 16.6 %collective-permute-start.16 = (bf16[896,256]{1,0:T(8,128)(2,1)}, bf16[896,256]{1,0:T(8,128)(2,1)}, u32[]{:S(2)}, u32[]{:S(2)}) collective-permute-start(bf16[896,256]{1,0:T(8,128)(2,1)} %collective-permute-done.9.refs_6_.refs_10_), channel_id=1, source_target_pairs={{0,4},{4,8},{8,12},{12,0},{1,5},{5,9},{9,13},{13,1},{2,6},{6,10},{... | collective-permute-start | bytes 1376264 | tf_op jit(solution)/shard_map/ppermute | solution.py:26
  46.5 9.7 %copy-start.12 = (bf16[768,256]{1,0:T(8,128)(2,1)}, bf16[768,256]{1,0:T(8,128)(2,1)S(1)}, u32[]{:S(2)}) copy-start(bf16[768,256]{1,0:T(8,128)(2,1)S(1)} %collective-permute-done.12.refs_1_) | copy-start | bytes 1179652
  46.5 39.1 %collective-permute-start.18 = (bf16[768,512]{1,0:T(8,128)(2,1)}, bf16[768,512]{1,0:T(8,128)(2,1)}, u32[]{:S(2)}, u32[]{:S(2)}) collective-permute-start(bf16[768,512]{1,0:T(8,128)(2,1)} %get-tuple-element.59), channel_id=1, source_target_pairs={{0,16},{16,32},{32,48},{48,0},{1,17},{17,33},{33,49},{49,1},{2,18}... | collective-permute-start | bytes 2359304 | tf_op jit(solution)/shard_map/ppermute | solution.py:26
  53.7 38.2 %collective-permute-start.20 = (bf16[768,512]{1,0:T(8,128)(2,1)}, bf16[768,512]{1,0:T(8,128)(2,1)}, u32[]{:S(2)}, u32[]{:S(2)}) collective-permute-start(bf16[768,512]{1,0:T(8,128)(2,1)} %get-tuple-element.60), channel_id=1, source_target_pairs={{0,32},{16,48},{32,0},{48,16},{1,33},{17,49},{33,1},{49,17},{2,34}... | collective-permute-start | bytes 2359304 | tf_op jit(solution)/shard_map/ppermute | solution.py:26
  54.5 38.0 %collective-permute-start.19 = (bf16[768,512]{1,0:T(8,128)(2,1)}, bf16[768,512]{1,0:T(8,128)(2,1)}, u32[]{:S(2)}, u32[]{:S(2)}) collective-permute-start(bf16[768,512]{1,0:T(8,128)(2,1)} %get-tuple-element.61), channel_id=1, source_target_pairs={{0,48},{16,0},{32,16},{48,32},{1,49},{17,1},{33,17},{49,33},{2,50}... | collective-permute-start | bytes 2359304 | tf_op jit(solution)/shard_map/ppermute | solution.py:26
  56.2 9.6 %collective-permute-start.15 = (bf16[896,256]{1,0:T(8,128)(2,1)}, bf16[896,256]{1,0:T(8,128)(2,1)S(1)}, u32[]{:S(2)}, u32[]{:S(2)}) collective-permute-start(bf16[896,256]{1,0:T(8,128)(2,1)} %collective-permute-done.11.refs_0_.refs_12_), channel_id=1, source_target_pairs={{0,1},{1,0},{2,3},{3,2},{4,5},{5,4},{6,7},{7,6},{8,9},{9,8},{10,11... | collective-permute-start | bytes 1376264 | tf_op jit(solution)/shard_map/ppermute | solution.py:26
  56.3 9.5 %collective-permute-start.17 = (bf16[896,256]{1,0:T(8,128)(2,1)}, bf16[896,256]{1,0:T(8,128)(2,1)S(1)}, u32[]{:S(2)}, u32[]{:S(2)}) collective-permute-start(bf16[896,256]{1,0:T(8,128)(2,1)} %collective-permute-done.16.refs_2_.refs_14_), channel_id=1, source_target_pairs={{0,1},{1,0},{2,3},{3,2},{4,5},{5,4},{6,7},{7,6},{8,9},{9,8},{10,11... | collective-permute-start | bytes 1376264 | tf_op jit(solution)/shard_map/ppermute | solution.py:26
  57.6 17.8 %all-to-all-start.1 = ((bf16[4,32,768]{2,1,0:T(8,128)(2,1)}), bf16[4,32,768]{2,1,0:T(8,128)(2,1)S(1)}, u32[]{:S(2)}, u32[]{:S(2)}) async-start(bf16[4,32,768]{2,1,0:T(8,128)(2,1)} %low_sum.1), calls=%async_computation.1 | async-start | bytes 393216 | tf_op jit(solution)/shard_map/all_to_all | solution.py:30
  65.8 21.5 %copy-start.10 = (bf16[896,256]{1,0:T(8,128)(2,1)}, bf16[896,256]{1,0:T(8,128)(2,1)S(1)}, u32[]{:S(2)}) copy-start(bf16[896,256]{1,0:T(8,128)(2,1)S(1)} %collective-permute-done.15.refs_1_.refs_13_) | copy-start | bytes 1376260
  65.8 21.5 %copy-start.11 = (bf16[896,256]{1,0:T(8,128)(2,1)}, bf16[896,256]{1,0:T(8,128)(2,1)S(1)}, u32[]{:S(2)}) copy-start(bf16[896,256]{1,0:T(8,128)(2,1)S(1)} %collective-permute-done.17.refs_3_.refs_15_) | copy-start | bytes 1376260
  70.4 24.8 %collective-permute-start.21 = (bf16[384,256]{1,0:T(8,128)(2,1)}, bf16[384,256]{1,0:T(8,128)(2,1)S(1)}, u32[]{:S(2)}, u32[]{:S(2)}) collective-permute-start(bf16[384,256]{1,0:T(8,128)(2,1)} %get-tuple-element.69), channel_id=1, source_target_pairs={{0,16},{16,32},{32,48},{48,0},{1,17},{17,33},{33,49},{49,1},{2,18}... | collective-permute-start | bytes 589832 | tf_op jit(solution)/shard_map/ppermute | solution.py:26
  70.5 33.3 %collective-permute-start.23 = (bf16[384,256]{1,0:T(8,128)(2,1)}, bf16[384,256]{1,0:T(8,128)(2,1)}, u32[]{:S(2)}, u32[]{:S(2)}) collective-permute-start(bf16[384,256]{1,0:T(8,128)(2,1)} %get-tuple-element.70), channel_id=1, source_target_pairs={{0,32},{16,48},{32,0},{48,16},{1,33},{17,49},{33,1},{49,17},{2,34}... | collective-permute-start | bytes 589832 | tf_op jit(solution)/shard_map/ppermute | solution.py:26
  80.5 15.1 %all-to-all-start.2 = ((f32[16,32,256]{2,1,0:T(8,128)}), f32[16,32,256]{2,1,0:T(8,128)S(1)}, u32[]{:S(2)}, u32[]{:S(2)}) async-start(f32[16,32,256]{2,1,0:T(8,128)} %grad_partial.1), calls=%async_computation.2 | async-start | bytes 1048576 | tf_op jit(solution)/shard_map/all_to_all | solution.py:30
  85.6 9.9 %copy-start.2 = (f32[32,256]{1,0:T(8,128)S(1)}, f32[32,256]{1,0:T(8,128)}, u32[]{:S(2)}) copy-start(f32[32,256]{1,0:T(8,128)} %first.1) | copy-start | bytes 98308
  85.6 9.9 %copy-start.3 = (f32[32,256]{1,0:T(8,128)S(1)}, f32[32,256]{1,0:T(8,128)}, u32[]{:S(2)}) copy-start(f32[32,256]{1,0:T(8,128)} %second.1) | copy-start | bytes 98308
  85.6 18.2 %collective-permute-start.22 = (bf16[384,256]{1,0:T(8,128)(2,1)}, bf16[384,256]{1,0:T(8,128)(2,1)}, u32[]{:S(2)}, u32[]{:S(2)}) collective-permute-start(bf16[384,256]{1,0:T(8,128)(2,1)} %get-tuple-element.71), channel_id=1, source_target_pairs={{0,48},{16,0},{32,16},{48,32},{1,49},{17,1},{33,17},{49,33},{2,50}... | collective-permute-start | bytes 589832 | tf_op jit(solution)/shard_map/ppermute | solution.py:26
  91.9 12.5 %collective-permute-start.24 = (bf16[384,256]{1,0:T(8,128)(2,1)}, bf16[384,256]{1,0:T(8,128)(2,1)S(1)}, u32[]{:S(2)}, u32[]{:S(2)}) collective-permute-start(bf16[384,256]{1,0:T(8,128)(2,1)} %get-tuple-element.78), channel_id=1, source_target_pairs={{0,16},{16,32},{32,48},{48,0},{1,17},{17,33},{33,49},{49,1},{2,18}... | collective-permute-start | bytes 589832 | tf_op jit(solution)/shard_map/ppermute | solution.py:26
  92.6 11.9 %collective-permute-start.25 = (bf16[384,256]{1,0:T(8,128)(2,1)}, bf16[384,256]{1,0:T(8,128)(2,1)S(1)}, u32[]{:S(2)}, u32[]{:S(2)}) collective-permute-start(bf16[384,256]{1,0:T(8,128)(2,1)} %get-tuple-element.79), channel_id=1, source_target_pairs={{0,48},{16,0},{32,16},{48,32},{1,49},{17,1},{33,17},{49,33},{2,50}... | collective-permute-start | bytes 589832 | tf_op jit(solution)/shard_map/ppermute | solution.py:26
  95.2 9.2 %copy-start.15 = (bf16[384,256]{1,0:T(8,128)(2,1)}, bf16[384,256]{1,0:T(8,128)(2,1)S(1)}, u32[]{:S(2)}) copy-start(bf16[384,256]{1,0:T(8,128)(2,1)S(1)} %collective-permute-done.21.refs_9_) | copy-start | bytes 589828
  95.2 9.2 %collective-permute-start.26 = (bf16[384,256]{1,0:T(8,128)(2,1)}, bf16[384,256]{1,0:T(8,128)(2,1)S(1)}, u32[]{:S(2)}, u32[]{:S(2)}) collective-permute-start(bf16[384,256]{1,0:T(8,128)(2,1)} %get-tuple-element.80), channel_id=1, source_target_pairs={{0,32},{16,48},{32,0},{48,16},{1,33},{17,49},{33,1},{49,17},{2,34}... | collective-permute-start | bytes 589832 | tf_op jit(solution)/shard_map/ppermute | solution.py:26
  96.3 57.9 %all-to-all-start.3 = ((bf16[16,32,256]{2,1,0:T(8,128)(2,1)}), bf16[16,32,256]{2,1,0:T(8,128)(2,1)S(1)}, u32[]{:S(2)}, u32[]{:S(2)}) async-start(bf16[16,32,256]{2,1,0:T(8,128)(2,1)} %get-tuple-element.74), calls=%async_computation.3 | async-start | bytes 524288 | tf_op jit(solution)/shard_map/all_to_all | solution.py:30
  111.2 31.4 %collective-permute-start.27 = (bf16[768,256]{1,0:T(8,128)(2,1)}, bf16[768,256]{1,0:T(8,128)(2,1)S(1)}, u32[]{:S(2)}, u32[]{:S(2)}) collective-permute-start(bf16[768,256]{1,0:T(8,128)(2,1)} %get-tuple-element.82), channel_id=1, source_target_pairs={{0,64},{64,128},{128,192},{192,0},{1,65},{65,129},{129,193},{193,1... | collective-permute-start | bytes 1179656 | tf_op jit(solution)/shard_map/ppermute | solution.py:26
  113.5 29.1 %collective-permute-start.28 = (bf16[768,256]{1,0:T(8,128)(2,1)}, bf16[768,256]{1,0:T(8,128)(2,1)S(1)}, u32[]{:S(2)}, u32[]{:S(2)}) collective-permute-start(bf16[768,256]{1,0:T(8,128)(2,1)} %get-tuple-element.83), channel_id=1, source_target_pairs={{0,192},{64,0},{128,64},{192,128},{1,193},{65,1},{129,65},{193,129... | collective-permute-start | bytes 1179656 | tf_op jit(solution)/shard_map/ppermute | solution.py:26
  115.6 37.7 %collective-permute-start.29 = (bf16[768,256]{1,0:T(8,128)(2,1)}, bf16[768,256]{1,0:T(8,128)(2,1)S(1)}, u32[]{:S(2)}, u32[]{:S(2)}) collective-permute-start(bf16[768,256]{1,0:T(8,128)(2,1)} %get-tuple-element.84), channel_id=1, source_target_pairs={{0,128},{64,192},{128,0},{192,64},{1,129},{65,193},{129,1},{193,65... | collective-permute-start | bytes 1179656 | tf_op jit(solution)/shard_map/ppermute | solution.py:26
  120.7 32.6 %copy-start.1 = (bf16[768,256]{1,0:T(8,128)(2,1)S(1)}, bf16[768,256]{1,0:T(8,128)(2,1)}, u32[]{:S(2)}) copy-start(bf16[768,256]{1,0:T(8,128)(2,1)} %get-tuple-element.81.a) | copy-start | bytes 1179652
  (5 other events, 7.1 us)

commit v3 on v2

--- a/solution.py
+++ b/solution.py
@@ -355,7 +355,7 @@
     sum2 = spread(part2, "x")
     grad_part = grad_partial(after(low_z, *part2), cotangent)
     grad_all = swap(grad_part, FSDP)
-    part3 = partials(after(hidden, grad_part, sum1[1], *part2), [slots[2]], slot_of, half, half)
+    part3 = partials(after(hidden, grad_part, *part2), [slots[2]], slot_of, half, half)
     sum3 = spread(part3, "x")
 
     new_first, new_second, normed = moments(grad_all, first_moment, second_moment)

time: 157 us -> 157 us (level)
  no operation moved by 1% of the time
where the time goes in v3:
time: 157 us; the launch traced here: 156 us
  starting transfers between devices  64.1 us (41%)
  Pallas kernels  48.2 us (31%)
  waiting for transfers between devices  36.3 us (23%)
  local copies, waits for them, and re-layouts  2.9 us (2%)
  matrix products  2.84 us (2%)
    ppermute x30, starting transfers between devices, shift(): return lax.ppermute(array, axis, [(i, (i + by) % n) for i in range(n)])  39.8 us
    ppermute x30, waiting for transfers between devices, shift(): return lax.ppermute(array, axis, [(i, (i + by) % n) for i in range(n)])  30 us
    all_to_all x4, starting transfers between devices, swap(): return lax.all_to_all(array, axes, 0, 0, tiled=True)  24.3 us
    pallas_call x4, Pallas kernels, partials(): pl.pallas_call(functools.partial(partial_kernel, m, start), out_shape=[pl...  22.7 us
    pallas_call x1, Pallas kernels, act(): pl.pallas_call(act_kernel, out_shape=jax.ShapeDtypeStruct((tokens, full),...  12.2 us
    all_to_all x4, waiting for transfers between devices, swap(): return lax.all_to_all(array, axes, 0, 0, tiled=True)  6.31 us
    pallas_call x1, Pallas kernels, regroup(): pl.pallas_call(functools.partial(regroup_kernel, [offs for _, offs in gro...  5.86 us
    pallas_call x1, Pallas kernels, grad_partial(): pl.pallas_call(grad_kernel, out_shape=pltpu.HBM((features // W, ranks, W)...  5.02 us
  transfers between devices with their start and end apart: 34, of which 9 were waited for; matrix products, arithmetic and copies ran while one was open for 2% of the time, Pallas kernels for 31%

profile of v3, /device:TPU:32, one launch (start us, length us, event | category | flops | bytes accessed | tf_op | source)
XLA Modules:
  0.0 155.6 jit_solution(2055209869438813193)
XLA Ops:
  0.6 1.7 %collective-permute-start.2 = (bf16[896,256]{1,0:T(8,128)(2,1)}, bf16[896,256]{1,0:T(8,128)(2,1)S(1)}, u32[]{:S(2)}, u32[]{:S(2)}) collective-permute-start(bf16[896,256]{1,0:T(8,128)(2,1)} %refs_0_.3), channel_id=1, source_target_pairs={{0,4},{4,8},{8,12},{12,0},{1,5},{5,9},{9,13},{13,1},{2,6},{6,10},{... | collective-permute-start | bytes 1376264 | tf_op jit(solution)/shard_map/ppermute | solution.py:26
  2.3 1.7 %collective-permute-start = (bf16[896,256]{1,0:T(8,128)(2,1)}, bf16[896,256]{1,0:T(8,128)(2,1)S(1)}, u32[]{:S(2)}, u32[]{:S(2)}) collective-permute-start(bf16[896,256]{1,0:T(8,128)(2,1)} %refs_0_.3), channel_id=1, source_target_pairs={{0,12},{4,0},{8,4},{12,8},{1,13},{5,1},{9,5},{13,9},{2,14},{6,2},{... | collective-permute-start | bytes 1376264 | tf_op jit(solution)/shard_map/ppermute | solution.py:26
  4.0 1.8 %collective-permute-start.5 = (bf16[896,256]{1,0:T(8,128)(2,1)}, bf16[896,256]{1,0:T(8,128)(2,1)S(1)}, u32[]{:S(2)}, u32[]{:S(2)}) collective-permute-start(bf16[896,256]{1,0:T(8,128)(2,1)} %refs_0_.3), channel_id=1, source_target_pairs={{0,2},{2,0},{1,3},{3,1},{4,6},{6,4},{5,7},{7,5},{8,10},{10,8},{9,1... | collective-permute-start | bytes 1376264 | tf_op jit(solution)/shard_map/ppermute | solution.py:26
  5.8 2.4 %convolution_convert_fusion = bf16[512,768]{1,0:T(8,128)(2,1)S(1)} fusion(bf16[896,512]{1,0:T(8,128)(2,1)S(1)} %copy-done, bf16[768,896]{1,0:T(8,128)(2,1)} %h_ref.3), kind=kOutput, calls=%fused_computation | convolution fusion | flops 705036288 | bytes 3080192 | tf_op jit(solution)/shard_map/dot_general | solution.py:321
  8.2 0.9 copy.15
  9.1 3.5 %all-to-all-start = ((bf16[4,4,32,768]{3,2,1,0:T(8,128)(2,1)}), bf16[4,4,32,768]{3,2,1,0:T(8,128)(2,1)S(1)}, u32[]{:S(2)}, u32[]{:S(2)}) async-start(bf16[4,4,32,768]{3,2,1,0:T(8,128)(2,1)} %bitcast.27), calls=%async_computation | async-start | bytes 1572864 | tf_op jit(solution)/shard_map/all_to_all | solution.py:30
  12.7 1.7 %collective-permute-done.2.refs_4_.refs_8_ = bf16[896,256]{1,0:T(8,128)(2,1)S(1)} collective-permute-done((bf16[896,256]{1,0:T(8,128)(2,1)}, bf16[896,256]{1,0:T(8,128)(2,1)S(1)}, u32[]{:S(2)}, u32[]{:S(2)}) %collective-permute-start.2) | collective-permute-done | bytes 458784 | tf_op jit(solution)/shard_map/ppermute | solution.py:26
  14.6 0.5 collective-permute-start.3
  15.1 0.9 collective-permute-done.5.refs_2_
  16.1 0.7 collective-permute-start.9
  16.9 2.6 %collective-permute-start.7 = (bf16[896,256]{1,0:T(8,128)(2,1)S(1)}, bf16[896,256]{1,0:T(8,128)(2,1)}, u32[]{:S(2)}, u32[]{:S(2)}) collective-permute-start(bf16[896,256]{1,0:T(8,128)(2,1)S(1)} %collective-permute-done.5.refs_2_), channel_id=1, source_target_pairs={{0,12},{4,0},{8,4},{12,8},{1,13},{5,1},{9,5},{13,9},{2,14},{6,2},{... | collective-permute-start | bytes 1376264 | tf_op jit(solution)/shard_map/ppermute | solution.py:26
  19.5 4.0 %all-to-all-done.parts = bf16[4,4,32,768]{3,2,1,0:T(8,128)(2,1)S(1)} async-done(((bf16[4,4,32,768]{3,2,1,0:T(8,128)(2,1)}), bf16[4,4,32,768]{3,2,1,0:T(8,128)(2,1)S(1)}, u32[]{:S(2)}, u32[]{:S(2)}) %all-to-all-start) | async-done | bytes 786464 | tf_op jit(solution)/shard_map/all_to_all | solution.py:30
  23.5 6.7 %partials.4 = (bf16[768,256]{1,0:T(8,128)(2,1)}, bf16[768,256]{1,0:T(8,128)(2,1)}, bf16[768,256]{1,0:T(8,128)(2,1)}, bf16[768,256]{1,0:T(8,128)(2,1)}) custom-call(s32[4]{0:T(128)S(1)} %pad_add_fusion.1.slot_of, bf16[768,896]{1,0:T(8,128)(2,1)} %h_ref.3, bf16[896,256]{1,0:T(8,128)(2,1)S(1)} %copy-done.4, bf16[896,256]{1,0:T(8,128)(2,1)} %collective-permute-done.4.refs_1_, ...), custom_call_target="tpu_custom_call" | custom-call | flops 8589934592 | bytes 33554432 | tf_op jit(solution)/shard_map/partials/pallas_call | solution.py:82
  30.4 0.5 collective-permute-start.10
  30.9 1.5 collective-permute-start.12
  32.4 2.7 %collective-permute-start.14 = (bf16[768,256]{1,0:T(8,128)(2,1)}, bf16[768,256]{1,0:T(8,128)(2,1)S(1)}, u32[]{:S(2)}, u32[]{:S(2)}) collective-permute-start(bf16[768,256]{1,0:T(8,128)(2,1)} %get-tuple-element.53), channel_id=1, source_target_pairs={{0,32},{16,48},{32,0},{48,16},{1,33},{17,49},{33,1},{49,17},{2,34}... | collective-permute-start | bytes 1179656 | tf_op jit(solution)/shard_map/ppermute | solution.py:26
  35.1 1.4 collective-permute-start.13
  36.6 3.0 %collective-permute-start.11 = (bf16[896,256]{1,0:T(8,128)(2,1)S(1)}, bf16[896,256]{1,0:T(8,128)(2,1)}, u32[]{:S(2)}, u32[]{:S(2)}) collective-permute-start(bf16[896,256]{1,0:T(8,128)(2,1)S(1)} %collective-permute-done.refs_0_.refs_4_), channel_id=1, source_target_pairs={{0,12},{4,0},{8,4},{12,8},{1,13},{5,1},{9,5},{13,9},{2,14},{6,2},{... | collective-permute-start | bytes 1376264 | tf_op jit(solution)/shard_map/ppermute | solution.py:26
  39.6 6.8 %partials.5 = (bf16[768,512]{1,0:T(8,128)(2,1)}, bf16[768,512]{1,0:T(8,128)(2,1)}, bf16[768,512]{1,0:T(8,128)(2,1)}, bf16[768,512]{1,0:T(8,128)(2,1)}) custom-call(s32[4]{0:T(128)S(1)} %pad_add_fusion.1.slot_of, bf16[768,896]{1,0:T(8,128)(2,1)} %h_ref.3, bf16[896,256]{1,0:T(8,128)(2,1)S(1)} %collective-permute-done.refs_0_.refs_4_, ...), custom_call_target="tpu_custom_call" | custom-call | flops 8589934592 | bytes 33554432 | tf_op jit(solution)/shard_map/partials/pallas_call | solution.py:82
  46.5 0.7 collective-permute-start.18
  47.2 6.6 %collective-permute-done.14.refs_3_ = bf16[768,256]{1,0:T(8,128)(2,1)S(1)} collective-permute-done((bf16[768,256]{1,0:T(8,128)(2,1)}, bf16[768,256]{1,0:T(8,128)(2,1)S(1)}, u32[]{:S(2)}, u32[]{:S(2)}) %collective-permute-start.14) | collective-permute-done | bytes 393248 | tf_op jit(solution)/shard_map/ppermute | solution.py:26
  53.7 0.8 collective-permute-start.20
  54.5 1.7 %collective-permute-start.19 = (bf16[768,512]{1,0:T(8,128)(2,1)}, bf16[768,512]{1,0:T(8,128)(2,1)}, u32[]{:S(2)}, u32[]{:S(2)}) collective-permute-start(bf16[768,512]{1,0:T(8,128)(2,1)} %get-tuple-element.61), channel_id=1, source_target_pairs={{0,48},{16,0},{32,16},{48,32},{1,49},{17,1},{33,17},{49,33},{2,50}... | collective-permute-start | bytes 2359304 | tf_op jit(solution)/shard_map/ppermute | solution.py:26
  56.3 0.6 collective-permute-start.17
  56.8 0.8 low_sum.1
  57.6 8.2 %all-to-all-start.1 = ((bf16[4,32,768]{2,1,0:T(8,128)(2,1)}), bf16[4,32,768]{2,1,0:T(8,128)(2,1)S(1)}, u32[]{:S(2)}, u32[]{:S(2)}) async-start(bf16[4,32,768]{2,1,0:T(8,128)(2,1)} %low_sum.1), calls=%async_computation.1 | async-start | bytes 393216 | tf_op jit(solution)/shard_map/all_to_all | solution.py:30
  65.8 4.6 %partials.6 = (bf16[384,256]{1,0:T(8,128)(2,1)}, bf16[384,256]{1,0:T(8,128)(2,1)}, bf16[384,256]{1,0:T(8,128)(2,1)}, bf16[384,256]{1,0:T(8,128)(2,1)}) custom-call(s32[4]{0:T(128)S(1)} %pad_add_fusion.1.slot_of, bf16[768,896]{1,0:T(8,128)(2,1)} %h_ref.3, bf16[896,256]{1,0:T(8,128)(2,1)} %collective-permute-done.11.refs_0_.refs_12_, ...), custom_call_target="tpu_custom_call" | custom-call | flops 8589934592 | bytes 33554432 | tf_op jit(solution)/shard_map/partials/pallas_call | solution.py:82
  70.5 2.6 %collective-permute-start.23 = (bf16[384,256]{1,0:T(8,128)(2,1)}, bf16[384,256]{1,0:T(8,128)(2,1)}, u32[]{:S(2)}, u32[]{:S(2)}) collective-permute-start(bf16[384,256]{1,0:T(8,128)(2,1)} %get-tuple-element.70), channel_id=1, source_target_pairs={{0,32},{16,48},{32,0},{48,16},{1,33},{17,49},{33,1},{49,17},{2,34}... | collective-permute-start | bytes 589832 | tf_op jit(solution)/shard_map/ppermute | solution.py:26
  73.1 2.3 %all-to-all-done.1.low_ref = bf16[4,32,768]{2,1,0:T(8,128)(2,1)S(1)} async-done(((bf16[4,32,768]{2,1,0:T(8,128)(2,1)}), bf16[4,32,768]{2,1,0:T(8,128)(2,1)S(1)}, u32[]{:S(2)}, u32[]{:S(2)}) %all-to-all-start.1) | async-done | bytes 196640 | tf_op jit(solution)/shard_map/all_to_all | solution.py:30
  75.4 5.0 %grad_partial.1 = f32[16,32,256]{2,1,0:T(8,128)} custom-call(bf16[4,32,768]{2,1,0:T(8,128)(2,1)S(1)} %all-to-all-done.1.low_ref, bf16[768,4096]{1,0:T(8,128)(2,1)} %cot_ref.2), custom_call_target="tpu_custom_call" | custom-call | flops 8589934592 | bytes 33554432 | tf_op jit(solution)/shard_map/grad_partial/pallas_call | solution.py:210
  80.4 5.1 %all-to-all-start.2 = ((f32[16,32,256]{2,1,0:T(8,128)}), f32[16,32,256]{2,1,0:T(8,128)S(1)}, u32[]{:S(2)}, u32[]{:S(2)}) async-start(f32[16,32,256]{2,1,0:T(8,128)} %grad_partial.1), calls=%async_computation.2 | async-start | bytes 1048576 | tf_op jit(solution)/shard_map/all_to_all | solution.py:30
  85.6 4.6 %partials.7 = (bf16[384,256]{1,0:T(8,128)(2,1)}, bf16[384,256]{1,0:T(8,128)(2,1)}, bf16[384,256]{1,0:T(8,128)(2,1)}, bf16[384,256]{1,0:T(8,128)(2,1)}) custom-call(s32[4]{0:T(128)S(1)} %pad_add_fusion.1.slot_of, bf16[768,896]{1,0:T(8,128)(2,1)} %h_ref.3, bf16[896,256]{1,0:T(8,128)(2,1)} %collective-permute-done.11.refs_0_.refs_12_, ...), custom_call_target="tpu_custom_call" | custom-call | flops 8589934592 | bytes 33554432 | tf_op jit(solution)/shard_map/partials/pallas_call | solution.py:82
  90.2 2.0 %collective-permute-start.22 = (bf16[384,256]{1,0:T(8,128)(2,1)}, bf16[384,256]{1,0:T(8,128)(2,1)S(1)}, u32[]{:S(2)}, u32[]{:S(2)}) collective-permute-start(bf16[384,256]{1,0:T(8,128)(2,1)} %get-tuple-element.71), channel_id=1, source_target_pairs={{0,48},{16,0},{32,16},{48,32},{1,49},{17,1},{33,17},{49,33},{2,50}... | collective-permute-start | bytes 589832 | tf_op jit(solution)/shard_map/ppermute | solution.py:26
  92.5 2.9 %collective-permute-start.25 = (bf16[384,256]{1,0:T(8,128)(2,1)}, bf16[384,256]{1,0:T(8,128)(2,1)S(1)}, u32[]{:S(2)}, u32[]{:S(2)}) collective-permute-start(bf16[384,256]{1,0:T(8,128)(2,1)} %get-tuple-element.79), channel_id=1, source_target_pairs={{0,48},{16,0},{32,16},{48,32},{1,49},{17,1},{33,17},{49,33},{2,50}... | collective-permute-start | bytes 589832 | tf_op jit(solution)/shard_map/ppermute | solution.py:26
  95.8 0.8 moments.1
  96.5 7.5 %all-to-all-start.3 = ((bf16[16,32,256]{2,1,0:T(8,128)(2,1)}), bf16[16,32,256]{2,1,0:T(8,128)(2,1)S(1)}, u32[]{:S(2)}, u32[]{:S(2)}) async-start(bf16[16,32,256]{2,1,0:T(8,128)(2,1)} %get-tuple-element.74), calls=%async_computation.3 | async-start | bytes 524288 | tf_op jit(solution)/shard_map/all_to_all | solution.py:30
  104.1 0.4 collective-permute-done.24.refs_13_
  104.8 0.4 copy-done.17
  105.3 5.9 %regroup.1 = (bf16[768,256]{1,0:T(8,128)(2,1)}, bf16[768,256]{1,0:T(8,128)(2,1)}, bf16[768,256]{1,0:T(8,128)(2,1)}, bf16[768,256]{1,0:T(8,128)(2,1)}) custom-call(s32[4]{0:T(128)S(1)} %pad_add_fusion.place, bf16[768,256]{1,0:T(8,128)(2,1)} %get-tuple-element.55.refs_0_, bf16[768,256]{1,0:T(8,128)(2,1)} %copy-done.12, bf16[768,256]{1,0:T(8,128)(2,1)} %copy-done.14, ...), custom_call_target="tpu_custom_call" | custom-call | flops 8589934592 | bytes 33554432 | tf_op jit(solution)/shard_map/regroup/pallas_call | solution.py:136
  111.1 2.6 %collective-permute-start.27 = (bf16[768,256]{1,0:T(8,128)(2,1)}, bf16[768,256]{1,0:T(8,128)(2,1)S(1)}, u32[]{:S(2)}, u32[]{:S(2)}) collective-permute-start(bf16[768,256]{1,0:T(8,128)(2,1)} %get-tuple-element.82), channel_id=1, source_target_pairs={{0,64},{64,128},{128,192},{192,0},{1,65},{65,129},{129,193},{193,1... | collective-permute-start | bytes 1179656 | tf_op jit(solution)/shard_map/ppermute | solution.py:26
  113.8 1.8 %collective-permute-start.28 = (bf16[768,256]{1,0:T(8,128)(2,1)}, bf16[768,256]{1,0:T(8,128)(2,1)S(1)}, u32[]{:S(2)}, u32[]{:S(2)}) collective-permute-start(bf16[768,256]{1,0:T(8,128)(2,1)} %get-tuple-element.83), channel_id=1, source_target_pairs={{0,192},{64,0},{128,64},{192,128},{1,193},{65,1},{129,65},{193,129... | collective-permute-start | bytes 1179656 | tf_op jit(solution)/shard_map/ppermute | solution.py:26
  115.5 5.4 %collective-permute-start.29 = (bf16[768,256]{1,0:T(8,128)(2,1)}, bf16[768,256]{1,0:T(8,128)(2,1)S(1)}, u32[]{:S(2)}, u32[]{:S(2)}) collective-permute-start(bf16[768,256]{1,0:T(8,128)(2,1)} %get-tuple-element.84), channel_id=1, source_target_pairs={{0,128},{64,192},{128,0},{192,64},{1,129},{65,193},{129,1},{193,65... | collective-permute-start | bytes 1179656 | tf_op jit(solution)/shard_map/ppermute | solution.py:26
  120.9 12.2 %act_grad.1 = bf16[768,896]{1,0:T(8,128)(2,1)} custom-call(s32[8]{0:T(128)S(1)} %stack.75.order, bf16[768,4096]{1,0:T(8,128)(2,1)} %cot_ref.2, bf16[896,256]{1,0:T(8,128)(2,1)} %refs_0_.3, bf16[896,256]{1,0:T(8,128)(2,1)} %collective-permute-done.4.refs_1_, bf16[896,256]{1,0:T(8,128)(2,1)} %copy-done.7, bf16[896,256]{1,0:T(8,128)(2,1)} %collective-permute-done.6.refs_3_, ...), custom_call_target="tpu_custom_call" | custom-call | flops 8589934592 | bytes 33554432 | tf_op jit(solution)/shard_map/act_grad/pallas_call | solution.py:294
  133.1 9.5 %collective-permute-done.27.b = bf16[768,256]{1,0:T(8,128)(2,1)S(1)} collective-permute-done((bf16[768,256]{1,0:T(8,128)(2,1)}, bf16[768,256]{1,0:T(8,128)(2,1)S(1)}, u32[]{:S(2)}, u32[]{:S(2)}) %collective-permute-start.27) | collective-permute-done | bytes 393248 | tf_op jit(solution)/shard_map/ppermute | solution.py:26
  142.6 10.7 %collective-permute-done.29.d = bf16[768,256]{1,0:T(8,128)(2,1)S(1)} collective-permute-done((bf16[768,256]{1,0:T(8,128)(2,1)}, bf16[768,256]{1,0:T(8,128)(2,1)S(1)}, u32[]{:S(2)}, u32[]{:S(2)}) %collective-permute-start.29) | collective-permute-done | bytes 393248 | tf_op jit(solution)/shard_map/ppermute | solution.py:26
  153.2 0.9 finish.1
  154.1 0.5 fusion
  154.6 1.0 copy.13
  (77 shorter events, 1.6 us)
Async XLA Ops:
  0.6 5.2 %copy-start = (bf16[896,512]{1,0:T(8,128)(2,1)S(1)}, bf16[896,512]{1,0:T(8,128)(2,1)}, u32[]{:S(2)}) copy-start(bf16[896,512]{1,0:T(8,128)(2,1)} %param.9) | copy-start | bytes 2752516
  0.6 13.8 %collective-permute-start.2 = (bf16[896,256]{1,0:T(8,128)(2,1)}, bf16[896,256]{1,0:T(8,128)(2,1)S(1)}, u32[]{:S(2)}, u32[]{:S(2)}) collective-permute-start(bf16[896,256]{1,0:T(8,128)(2,1)} %refs_0_.3), channel_id=1, source_target_pairs={{0,4},{4,8},{8,12},{12,0},{1,5},{5,9},{9,13},{13,1},{2,6},{6,10},{... | collective-permute-start | bytes 1376264 | tf_op jit(solution)/shard_map/ppermute | solution.py:26
  2.3 12.2 %collective-permute-start = (bf16[896,256]{1,0:T(8,128)(2,1)}, bf16[896,256]{1,0:T(8,128)(2,1)S(1)}, u32[]{:S(2)}, u32[]{:S(2)}) collective-permute-start(bf16[896,256]{1,0:T(8,128)(2,1)} %refs_0_.3), channel_id=1, source_target_pairs={{0,12},{4,0},{8,4},{12,8},{1,13},{5,1},{9,5},{13,9},{2,14},{6,2},{... | collective-permute-start | bytes 1376264 | tf_op jit(solution)/shard_map/ppermute | solution.py:26
  4.0 12.1 %collective-permute-start.5 = (bf16[896,256]{1,0:T(8,128)(2,1)}, bf16[896,256]{1,0:T(8,128)(2,1)S(1)}, u32[]{:S(2)}, u32[]{:S(2)}) collective-permute-start(bf16[896,256]{1,0:T(8,128)(2,1)} %refs_0_.3), channel_id=1, source_target_pairs={{0,2},{2,0},{1,3},{3,1},{4,6},{6,4},{5,7},{7,5},{8,10},{10,8},{9,1... | collective-permute-start | bytes 1376264 | tf_op jit(solution)/shard_map/ppermute | solution.py:26
  8.2 4.5 %copy-start.4 = (bf16[896,256]{1,0:T(8,128)(2,1)S(1)}, bf16[896,256]{1,0:T(8,128)(2,1)}, u32[]{:S(2)}) copy-start(bf16[896,256]{1,0:T(8,128)(2,1)} %refs_0_.3) | copy-start | bytes 1376260
  9.1 14.3 %all-to-all-start = ((bf16[4,4,32,768]{3,2,1,0:T(8,128)(2,1)}), bf16[4,4,32,768]{3,2,1,0:T(8,128)(2,1)S(1)}, u32[]{:S(2)}, u32[]{:S(2)}) async-start(bf16[4,4,32,768]{3,2,1,0:T(8,128)(2,1)} %bitcast.27), calls=%async_computation | async-start | bytes 1572864 | tf_op jit(solution)/shard_map/all_to_all | solution.py:30
  12.6 10.8 %collective-permute-start.4 = (bf16[896,256]{1,0:T(8,128)(2,1)S(1)}, bf16[896,256]{1,0:T(8,128)(2,1)}, u32[]{:S(2)}, u32[]{:S(2)}) collective-permute-start(bf16[896,256]{1,0:T(8,128)(2,1)S(1)} %copy-done.4), channel_id=1, source_target_pairs={{0,1},{1,0},{2,3},{3,2},{4,5},{5,4},{6,7},{7,6},{8,9},{9,8},{10,11... | collective-permute-start | bytes 1376264 | tf_op jit(solution)/shard_map/ppermute | solution.py:26
  14.5 25.1 %copy-start.5 = (bf16[896,256]{1,0:T(8,128)(2,1)}, bf16[896,256]{1,0:T(8,128)(2,1)S(1)}, u32[]{:S(2)}) copy-start(bf16[896,256]{1,0:T(8,128)(2,1)S(1)} %collective-permute-done.2.refs_4_.refs_8_) | copy-start | bytes 1376260
  14.5 25.1 %copy-start.6 = (bf16[896,256]{1,0:T(8,128)(2,1)}, bf16[896,256]{1,0:T(8,128)(2,1)S(1)}, u32[]{:S(2)}) copy-start(bf16[896,256]{1,0:T(8,128)(2,1)S(1)} %collective-permute-done.refs_0_.refs_4_) | copy-start | bytes 1376260
  14.5 2.4 %collective-permute-start.1 = (bf16[896,256]{1,0:T(8,128)(2,1)S(1)}, bf16[896,256]{1,0:T(8,128)(2,1)}, u32[]{:S(2)}, u32[]{:S(2)}) collective-permute-start(bf16[896,256]{1,0:T(8,128)(2,1)S(1)} %collective-permute-done.refs_0_.refs_4_), channel_id=1, source_target_pairs={{0,1},{1,0},{2,3},{3,2},{4,5},{5,4},{6,7},{7,6},{8,9},{9,8},{10,11... | collective-permute-start | bytes 1376264 | tf_op jit(solution)/shard_map/ppermute | solution.py:26
  14.6 8.9 %collective-permute-start.3 = (bf16[896,256]{1,0:T(8,128)(2,1)S(1)}, bf16[896,256]{1,0:T(8,128)(2,1)}, u32[]{:S(2)}, u32[]{:S(2)}) collective-permute-start(bf16[896,256]{1,0:T(8,128)(2,1)S(1)} %collective-permute-done.2.refs_4_.refs_8_), channel_id=1, source_target_pairs={{0,1},{1,0},{2,3},{3,2},{4,5},{5,4},{6,7},{7,6},{8,9},{9,8},{10,11... | collective-permute-start | bytes 1376264 | tf_op jit(solution)/shard_map/ppermute | solution.py:26
  16.0 14.1 %copy-start.7 = (bf16[896,256]{1,0:T(8,128)(2,1)}, bf16[896,256]{1,0:T(8,128)(2,1)S(1)}, u32[]{:S(2)}) copy-start(bf16[896,256]{1,0:T(8,128)(2,1)S(1)} %collective-permute-done.5.refs_2_) | copy-start | bytes 1376260
  16.0 7.4 %collective-permute-start.6 = (bf16[896,256]{1,0:T(8,128)(2,1)S(1)}, bf16[896,256]{1,0:T(8,128)(2,1)}, u32[]{:S(2)}, u32[]{:S(2)}) collective-permute-start(bf16[896,256]{1,0:T(8,128)(2,1)S(1)} %collective-permute-done.5.refs_2_), channel_id=1, source_target_pairs={{0,1},{1,0},{2,3},{3,2},{4,5},{5,4},{6,7},{7,6},{8,9},{9,8},{10,11... | collective-permute-start | bytes 1376264 | tf_op jit(solution)/shard_map/ppermute | solution.py:26
  16.1 14.3 %collective-permute-start.9 = (bf16[896,256]{1,0:T(8,128)(2,1)S(1)}, bf16[896,256]{1,0:T(8,128)(2,1)}, u32[]{:S(2)}, u32[]{:S(2)}) collective-permute-start(bf16[896,256]{1,0:T(8,128)(2,1)S(1)} %collective-permute-done.5.refs_2_), channel_id=1, source_target_pairs={{0,4},{4,8},{8,12},{12,0},{1,5},{5,9},{9,13},{13,1},{2,6},{6,10},{... | collective-permute-start | bytes 1376264 | tf_op jit(solution)/shard_map/ppermute | solution.py:26
  16.9 13.5 %collective-permute-start.7 = (bf16[896,256]{1,0:T(8,128)(2,1)S(1)}, bf16[896,256]{1,0:T(8,128)(2,1)}, u32[]{:S(2)}, u32[]{:S(2)}) collective-permute-start(bf16[896,256]{1,0:T(8,128)(2,1)S(1)} %collective-permute-done.5.refs_2_), channel_id=1, source_target_pairs={{0,12},{4,0},{8,4},{12,8},{1,13},{5,1},{9,5},{13,9},{2,14},{6,2},{... | collective-permute-start | bytes 1376264 | tf_op jit(solution)/shard_map/ppermute | solution.py:26
  30.4 6.2 %collective-permute-start.8 = (bf16[896,256]{1,0:T(8,128)(2,1)}, bf16[896,256]{1,0:T(8,128)(2,1)S(1)}, u32[]{:S(2)}, u32[]{:S(2)}) collective-permute-start(bf16[896,256]{1,0:T(8,128)(2,1)} %collective-permute-done.7.refs_2_.refs_6_), channel_id=1, source_target_pairs={{0,1},{1,0},{2,3},{3,2},{4,5},{5,4},{6,7},{7,6},{8,9},{9,8},{10,11... | collective-permute-start | bytes 1376264 | tf_op jit(solution)/shard_map/ppermute | solution.py:26
  30.4 6.2 %collective-permute-start.10 = (bf16[896,256]{1,0:T(8,128)(2,1)}, bf16[896,256]{1,0:T(8,128)(2,1)S(1)}, u32[]{:S(2)}, u32[]{:S(2)}) collective-permute-start(bf16[896,256]{1,0:T(8,128)(2,1)} %collective-permute-done.9.refs_6_.refs_10_), channel_id=1, source_target_pairs={{0,1},{1,0},{2,3},{3,2},{4,5},{5,4},{6,7},{7,6},{8,9},{9,8},{10,11... | collective-permute-start | bytes 1376264 | tf_op jit(solution)/shard_map/ppermute | solution.py:26
  30.9 15.6 %collective-permute-start.12 = (bf16[768,256]{1,0:T(8,128)(2,1)}, bf16[768,256]{1,0:T(8,128)(2,1)S(1)}, u32[]{:S(2)}, u32[]{:S(2)}) collective-permute-start(bf16[768,256]{1,0:T(8,128)(2,1)} %get-tuple-element.52), channel_id=1, source_target_pairs={{0,16},{16,32},{32,48},{48,0},{1,17},{17,33},{33,49},{49,1},{2,18}... | collective-permute-start | bytes 1179656 | tf_op jit(solution)/shard_map/ppermute | solution.py:26
  32.4 21.4 %collective-permute-start.14 = (bf16[768,256]{1,0:T(8,128)(2,1)}, bf16[768,256]{1,0:T(8,128)(2,1)S(1)}, u32[]{:S(2)}, u32[]{:S(2)}) collective-permute-start(bf16[768,256]{1,0:T(8,128)(2,1)} %get-tuple-element.53), channel_id=1, source_target_pairs={{0,32},{16,48},{32,0},{48,16},{1,33},{17,49},{33,1},{49,17},{2,34}... | collective-permute-start | bytes 1179656 | tf_op jit(solution)/shard_map/ppermute | solution.py:26
  35.1 19.4 %collective-permute-start.13 = (bf16[768,256]{1,0:T(8,128)(2,1)}, bf16[768,256]{1,0:T(8,128)(2,1)S(1)}, u32[]{:S(2)}, u32[]{:S(2)}) collective-permute-start(bf16[768,256]{1,0:T(8,128)(2,1)} %get-tuple-element.54), channel_id=1, source_target_pairs={{0,48},{16,0},{32,16},{48,32},{1,49},{17,1},{33,17},{49,33},{2,50}... | collective-permute-start | bytes 1179656 | tf_op jit(solution)/shard_map/ppermute | solution.py:26
  36.5 9.9 %copy-start.8 = (bf16[896,256]{1,0:T(8,128)(2,1)}, bf16[896,256]{1,0:T(8,128)(2,1)S(1)}, u32[]{:S(2)}) copy-start(bf16[896,256]{1,0:T(8,128)(2,1)S(1)} %collective-permute-done.8.refs_3_.refs_7_) | copy-start | bytes 1376260
  36.5 9.9 %copy-start.9 = (bf16[896,256]{1,0:T(8,128)(2,1)}, bf16[896,256]{1,0:T(8,128)(2,1)S(1)}, u32[]{:S(2)}) copy-start(bf16[896,256]{1,0:T(8,128)(2,1)S(1)} %collective-permute-done.10.refs_7_.refs_11_) | copy-start | bytes 1376260
  36.6 19.7 %collective-permute-start.11 = (bf16[896,256]{1,0:T(8,128)(2,1)S(1)}, bf16[896,256]{1,0:T(8,128)(2,1)}, u32[]{:S(2)}, u32[]{:S(2)}) collective-permute-start(bf16[896,256]{1,0:T(8,128)(2,1)S(1)} %collective-permute-done.refs_0_.refs_4_), channel_id=1, source_target_pairs={{0,12},{4,0},{8,4},{12,8},{1,13},{5,1},{9,5},{13,9},{2,14},{6,2},{... | collective-permute-start | bytes 1376264 | tf_op jit(solution)/shard_map/ppermute | solution.py:26
  39.6 16.6 %collective-permute-start.16 = (bf16[896,256]{1,0:T(8,128)(2,1)}, bf16[896,256]{1,0:T(8,128)(2,1)}, u32[]{:S(2)}, u32[]{:S(2)}) collective-permute-start(bf16[896,256]{1,0:T(8,128)(2,1)} %collective-permute-done.9.refs_6_.refs_10_), channel_id=1, source_target_pairs={{0,4},{4,8},{8,12},{12,0},{1,5},{5,9},{9,13},{13,1},{2,6},{6,10},{... | collective-permute-start | bytes 1376264 | tf_op jit(solution)/shard_map/ppermute | solution.py:26
  46.5 9.8 %copy-start.12 = (bf16[768,256]{1,0:T(8,128)(2,1)}, bf16[768,256]{1,0:T(8,128)(2,1)S(1)}, u32[]{:S(2)}) copy-start(bf16[768,256]{1,0:T(8,128)(2,1)S(1)} %collective-permute-done.12.refs_1_) | copy-start | bytes 1179652
  46.5 43.7 %collective-permute-start.18 = (bf16[768,512]{1,0:T(8,128)(2,1)}, bf16[768,512]{1,0:T(8,128)(2,1)}, u32[]{:S(2)}, u32[]{:S(2)}) collective-permute-start(bf16[768,512]{1,0:T(8,128)(2,1)} %get-tuple-element.59), channel_id=1, source_target_pairs={{0,16},{16,32},{32,48},{48,0},{1,17},{17,33},{33,49},{49,1},{2,18}... | collective-permute-start | bytes 2359304 | tf_op jit(solution)/shard_map/ppermute | solution.py:26
  53.7 38.5 %collective-permute-start.20 = (bf16[768,512]{1,0:T(8,128)(2,1)}, bf16[768,512]{1,0:T(8,128)(2,1)}, u32[]{:S(2)}, u32[]{:S(2)}) collective-permute-start(bf16[768,512]{1,0:T(8,128)(2,1)} %get-tuple-element.60), channel_id=1, source_target_pairs={{0,32},{16,48},{32,0},{48,16},{1,33},{17,49},{33,1},{49,17},{2,34}... | collective-permute-start | bytes 2359304 | tf_op jit(solution)/shard_map/ppermute | solution.py:26
  54.5 38.0 %collective-permute-start.19 = (bf16[768,512]{1,0:T(8,128)(2,1)}, bf16[768,512]{1,0:T(8,128)(2,1)}, u32[]{:S(2)}, u32[]{:S(2)}) collective-permute-start(bf16[768,512]{1,0:T(8,128)(2,1)} %get-tuple-element.61), channel_id=1, source_target_pairs={{0,48},{16,0},{32,16},{48,32},{1,49},{17,1},{33,17},{49,33},{2,50}... | collective-permute-start | bytes 2359304 | tf_op jit(solution)/shard_map/ppermute | solution.py:26
  56.2 9.6 %collective-permute-start.15 = (bf16[896,256]{1,0:T(8,128)(2,1)}, bf16[896,256]{1,0:T(8,128)(2,1)S(1)}, u32[]{:S(2)}, u32[]{:S(2)}) collective-permute-start(bf16[896,256]{1,0:T(8,128)(2,1)} %collective-permute-done.11.refs_0_.refs_12_), channel_id=1, source_target_pairs={{0,1},{1,0},{2,3},{3,2},{4,5},{5,4},{6,7},{7,6},{8,9},{9,8},{10,11... | collective-permute-start | bytes 1376264 | tf_op jit(solution)/shard_map/ppermute | solution.py:26
  56.3 9.5 %collective-permute-start.17 = (bf16[896,256]{1,0:T(8,128)(2,1)}, bf16[896,256]{1,0:T(8,128)(2,1)S(1)}, u32[]{:S(2)}, u32[]{:S(2)}) collective-permute-start(bf16[896,256]{1,0:T(8,128)(2,1)} %collective-permute-done.16.refs_2_.refs_14_), channel_id=1, source_target_pairs={{0,1},{1,0},{2,3},{3,2},{4,5},{5,4},{6,7},{7,6},{8,9},{9,8},{10,11... | collective-permute-start | bytes 1376264 | tf_op jit(solution)/shard_map/ppermute | solution.py:26
  57.6 17.8 %all-to-all-start.1 = ((bf16[4,32,768]{2,1,0:T(8,128)(2,1)}), bf16[4,32,768]{2,1,0:T(8,128)(2,1)S(1)}, u32[]{:S(2)}, u32[]{:S(2)}) async-start(bf16[4,32,768]{2,1,0:T(8,128)(2,1)} %low_sum.1), calls=%async_computation.1 | async-start | bytes 393216 | tf_op jit(solution)/shard_map/all_to_all | solution.py:30
  65.8 19.8 %copy-start.10 = (bf16[896,256]{1,0:T(8,128)(2,1)}, bf16[896,256]{1,0:T(8,128)(2,1)S(1)}, u32[]{:S(2)}) copy-start(bf16[896,256]{1,0:T(8,128)(2,1)S(1)} %collective-permute-done.15.refs_1_.refs_13_) | copy-start | bytes 1376260
  65.8 19.8 %copy-start.11 = (bf16[896,256]{1,0:T(8,128)(2,1)}, bf16[896,256]{1,0:T(8,128)(2,1)S(1)}, u32[]{:S(2)}) copy-start(bf16[896,256]{1,0:T(8,128)(2,1)S(1)} %collective-permute-done.17.refs_3_.refs_15_) | copy-start | bytes 1376260
  70.4 25.1 %collective-permute-start.21 = (bf16[384,256]{1,0:T(8,128)(2,1)}, bf16[384,256]{1,0:T(8,128)(2,1)S(1)}, u32[]{:S(2)}, u32[]{:S(2)}) collective-permute-start(bf16[384,256]{1,0:T(8,128)(2,1)} %get-tuple-element.69), channel_id=1, source_target_pairs={{0,16},{16,32},{32,48},{48,0},{1,17},{17,33},{33,49},{49,1},{2,18}... | collective-permute-start | bytes 589832 | tf_op jit(solution)/shard_map/ppermute | solution.py:26
  70.5 33.5 %collective-permute-start.23 = (bf16[384,256]{1,0:T(8,128)(2,1)}, bf16[384,256]{1,0:T(8,128)(2,1)}, u32[]{:S(2)}, u32[]{:S(2)}) collective-permute-start(bf16[384,256]{1,0:T(8,128)(2,1)} %get-tuple-element.70), channel_id=1, source_target_pairs={{0,32},{16,48},{32,0},{48,16},{1,33},{17,49},{33,1},{49,17},{2,34}... | collective-permute-start | bytes 589832 | tf_op jit(solution)/shard_map/ppermute | solution.py:26
  80.4 15.3 %all-to-all-start.2 = ((f32[16,32,256]{2,1,0:T(8,128)}), f32[16,32,256]{2,1,0:T(8,128)S(1)}, u32[]{:S(2)}, u32[]{:S(2)}) async-start(f32[16,32,256]{2,1,0:T(8,128)} %grad_partial.1), calls=%async_computation.2 | async-start | bytes 1048576 | tf_op jit(solution)/shard_map/all_to_all | solution.py:30
  85.6 10.2 %copy-start.2 = (f32[32,256]{1,0:T(8,128)S(1)}, f32[32,256]{1,0:T(8,128)}, u32[]{:S(2)}) copy-start(f32[32,256]{1,0:T(8,128)} %first.1) | copy-start | bytes 98308
  85.6 10.2 %copy-start.3 = (f32[32,256]{1,0:T(8,128)S(1)}, f32[32,256]{1,0:T(8,128)}, u32[]{:S(2)}) copy-start(f32[32,256]{1,0:T(8,128)} %second.1) | copy-start | bytes 98308
  90.2 13.8 %collective-permute-start.22 = (bf16[384,256]{1,0:T(8,128)(2,1)}, bf16[384,256]{1,0:T(8,128)(2,1)S(1)}, u32[]{:S(2)}, u32[]{:S(2)}) collective-permute-start(bf16[384,256]{1,0:T(8,128)(2,1)} %get-tuple-element.71), channel_id=1, source_target_pairs={{0,48},{16,0},{32,16},{48,32},{1,49},{17,1},{33,17},{49,33},{2,50}... | collective-permute-start | bytes 589832 | tf_op jit(solution)/shard_map/ppermute | solution.py:26
  92.2 12.2 %collective-permute-start.24 = (bf16[384,256]{1,0:T(8,128)(2,1)}, bf16[384,256]{1,0:T(8,128)(2,1)S(1)}, u32[]{:S(2)}, u32[]{:S(2)}) collective-permute-start(bf16[384,256]{1,0:T(8,128)(2,1)} %get-tuple-element.78), channel_id=1, source_target_pairs={{0,16},{16,32},{32,48},{48,0},{1,17},{17,33},{33,49},{49,1},{2,18}... | collective-permute-start | bytes 589832 | tf_op jit(solution)/shard_map/ppermute | solution.py:26
  92.5 11.9 %collective-permute-start.25 = (bf16[384,256]{1,0:T(8,128)(2,1)}, bf16[384,256]{1,0:T(8,128)(2,1)S(1)}, u32[]{:S(2)}, u32[]{:S(2)}) collective-permute-start(bf16[384,256]{1,0:T(8,128)(2,1)} %get-tuple-element.79), channel_id=1, source_target_pairs={{0,48},{16,0},{32,16},{48,32},{1,49},{17,1},{33,17},{49,33},{2,50}... | collective-permute-start | bytes 589832 | tf_op jit(solution)/shard_map/ppermute | solution.py:26
  95.5 9.0 %copy-start.15 = (bf16[384,256]{1,0:T(8,128)(2,1)}, bf16[384,256]{1,0:T(8,128)(2,1)S(1)}, u32[]{:S(2)}) copy-start(bf16[384,256]{1,0:T(8,128)(2,1)S(1)} %collective-permute-done.21.refs_9_) | copy-start | bytes 589828
  95.5 9.0 %collective-permute-start.26 = (bf16[384,256]{1,0:T(8,128)(2,1)}, bf16[384,256]{1,0:T(8,128)(2,1)S(1)}, u32[]{:S(2)}, u32[]{:S(2)}) collective-permute-start(bf16[384,256]{1,0:T(8,128)(2,1)} %get-tuple-element.80), channel_id=1, source_target_pairs={{0,32},{16,48},{32,0},{48,16},{1,33},{17,49},{33,1},{49,17},{2,34}... | collective-permute-start | bytes 589832 | tf_op jit(solution)/shard_map/ppermute | solution.py:26
  96.5 57.6 %all-to-all-start.3 = ((bf16[16,32,256]{2,1,0:T(8,128)(2,1)}), bf16[16,32,256]{2,1,0:T(8,128)(2,1)S(1)}, u32[]{:S(2)}, u32[]{:S(2)}) async-start(bf16[16,32,256]{2,1,0:T(8,128)(2,1)} %get-tuple-element.74), calls=%async_computation.3 | async-start | bytes 524288 | tf_op jit(solution)/shard_map/all_to_all | solution.py:30
  111.1 31.4 %collective-permute-start.27 = (bf16[768,256]{1,0:T(8,128)(2,1)}, bf16[768,256]{1,0:T(8,128)(2,1)S(1)}, u32[]{:S(2)}, u32[]{:S(2)}) collective-permute-start(bf16[768,256]{1,0:T(8,128)(2,1)} %get-tuple-element.82), channel_id=1, source_target_pairs={{0,64},{64,128},{128,192},{192,0},{1,65},{65,129},{129,193},{193,1... | collective-permute-start | bytes 1179656 | tf_op jit(solution)/shard_map/ppermute | solution.py:26
  113.8 28.8 %collective-permute-start.28 = (bf16[768,256]{1,0:T(8,128)(2,1)}, bf16[768,256]{1,0:T(8,128)(2,1)S(1)}, u32[]{:S(2)}, u32[]{:S(2)}) collective-permute-start(bf16[768,256]{1,0:T(8,128)(2,1)} %get-tuple-element.83), channel_id=1, source_target_pairs={{0,192},{64,0},{128,64},{192,128},{1,193},{65,1},{129,65},{193,129... | collective-permute-start | bytes 1179656 | tf_op jit(solution)/shard_map/ppermute | solution.py:26
  115.5 37.7 %collective-permute-start.29 = (bf16[768,256]{1,0:T(8,128)(2,1)}, bf16[768,256]{1,0:T(8,128)(2,1)S(1)}, u32[]{:S(2)}, u32[]{:S(2)}) collective-permute-start(bf16[768,256]{1,0:T(8,128)(2,1)} %get-tuple-element.84), channel_id=1, source_target_pairs={{0,128},{64,192},{128,0},{192,64},{1,129},{65,193},{129,1},{193,65... | collective-permute-start | bytes 1179656 | tf_op jit(solution)/shard_map/ppermute | solution.py:26
  120.9 32.4 %copy-start.1 = (bf16[768,256]{1,0:T(8,128)(2,1)S(1)}, bf16[768,256]{1,0:T(8,128)(2,1)}, u32[]{:S(2)}) copy-start(bf16[768,256]{1,0:T(8,128)(2,1)} %get-tuple-element.81.a) | copy-start | bytes 1179652
  (6 other events, 7.8 us)
